TPU v7x, 32 devices: a whole 2x2x4 slice. The times are simulated.
32 devices in a mesh: sec: 4 (over y, core), op: 8 (over z, x).
Axes of the slice: x: 2, y: 2, z: 4, core: 2. Of those that a mesh axis runs over, the one named last changes fastest.
Arguments:
- psi: bfloat16 [8, 256, 256], P('sec', 'op'), may hold values from -6 to 6
- left_ops: bfloat16 [256, 256, 256], P(('sec', 'op')), may hold values from -0.0234375 to 0.0234375
- right_ops: bfloat16 [256, 256, 256], P(('sec', 'op')), may hold values from -0.375 to 0.375
- send_list: int32 [4, 8, 4, 1], replicated, may hold values from 0 to 7, as said below
- term_slot: int32 [2048], P(('sec', 'op')), may hold values from 0 to 3
- term_out: int32 [2048], P(('sec', 'op')), may hold values from 0 to 1
- left_pick: int32 [2048], P(('sec', 'op')), may hold values from 0 to 7
- right_pick: int32 [2048], P(('sec', 'op')), may hold values from 0 to 7
Outputs:
- h_psi: float32 [8, 256, 256], P('sec', 'op')
Inputs may be any that keep to these rules, and one draw needn't show every extreme that they name: `send_list`: entry [s, o, d, c] is a sector held by index s of sec, between 2 * s and 2 * s + 1; the 1 entries of one s, o, d are distinct.
All inputs are finite; a program needn't handle non-finite values.
Results may differ from a plain program's by a relative error of at most 0.0041.
Values may be sent and summed in bfloat16 or wider, within the bound.
No kernel may reach another device: no remote copies, remote signals or barrier semaphores. Data moves between devices by JAX's collectives and lax.ppermute only.
A program may use at most 64 MiB of HBM per device.

v0:
```python
import jax
import jax.numpy as jnp
from jax import lax
from jax.sharding import PartitionSpec as P

GROUP = 8


def shards(psi, left_ops, right_ops, send_list, term_slot, term_out, left_pick, right_pick):
    full = lax.all_gather(psi, "op", axis=1, tiled=True)
    my_sec = lax.axis_index("sec")
    my_op = lax.axis_index("op")
    held = full.shape[0]
    width = full.shape[1]
    listed = jnp.take(send_list, my_op, axis=1)
    listed = jnp.take(listed, my_sec, axis=1)
    table = lax.all_gather(full, "sec", axis=0, tiled=True)
    wanted = jnp.take(listed.reshape(-1), term_slot, axis=0)
    groups = term_slot.shape[0] // GROUP
    items = (
        wanted.reshape(groups, GROUP),
        term_out.reshape(groups, GROUP),
        left_pick.reshape(groups, GROUP),
        right_pick.reshape(groups, GROUP),
    )
    targets = jnp.arange(held, dtype=jnp.int32)

    def one_group(total, group_items):
        block_ids, out_ids, left_ids, right_ids = group_items
        left = jnp.take(left_ops, left_ids, axis=0)
        block = jnp.take(table, block_ids, axis=0)
        right = jnp.take(right_ops, right_ids, axis=0)
        half = jnp.einsum("kab,kbc->kac", left, block, preferred_element_type=jnp.float32).astype(
            jnp.bfloat16
        )
        term = jnp.einsum("kac,kdc->kad", half, right, preferred_element_type=jnp.float32).astype(
            jnp.bfloat16
        )
        onehot = (targets[:, None] == out_ids[None, :]).astype(jnp.bfloat16)
        return (
            total + jnp.einsum("jk,kad->jad", onehot, term, preferred_element_type=jnp.float32),
            None,
        )

    start = jnp.zeros((held, width, width), jnp.float32)
    partial_value, unused = lax.scan(one_group, start, items)
    return lax.psum_scatter(partial_value, "op", scatter_dimension=1, tiled=True)


def solution(mesh):
    in_specs = (
        P("sec", "op", None),
        P(("sec", "op"), None, None),
        P(("sec", "op"), None, None),
        P(),
        P(("sec", "op")),
        P(("sec", "op")),
        P(("sec", "op")),
        P(("sec", "op")),
    )
    out_specs = P("sec", "op", None)
    return jax.shard_map(shards, mesh=mesh, in_specs=in_specs, out_specs=out_specs, check_vma=False)
```

profile of v0, /device:TPU:0, one launch (start us, length us, event | category | flops | bytes accessed | tf_op | source)
XLA Modules:
  0.0 223.4 jit_solution(16948694345847506093)
XLA Ops:
  6.5 34.7 %all_gather.6 = bf16[2,256,256]{2,1,0:T(8,128)(2,1)} all-gather(bf16[2,32,256]{2,1,0:T(8,128)(2,1)} %param.12), channel_id=1, replica_groups=mesh['sec'=4,'op'=8] {'op'}, dimensions={1}, use_global_device_ids=true | all-gather | bytes 294912 | tf_op jit(solution)/shard_map/all_gather | solution.py:10
  42.7 3.0 %and_select_fusion = s32[64]{0:T(128)S(1)} fusion(s32[64]{0:T(128)} %param.16, s32[]{:T(128)} %bitcast, s32[]{:T(128)} %bitcast.1, s32[]{:T(128)} %bitcast.2, s32[]{:T(128)} %bitcast.3), kind=kLoop, calls=%fused_computation.43 | loop fusion | flops 832 | bytes 528 | tf_op jit(solution)/shard_map/jit(_take)/select_n | solution.py:18
  48.0 11.1 %all-gather.2.cloned.1.call-done = bf16[8,256,256]{2,1,0:T(8,128)(2,1)} async-done(((bf16[2,256,256]{2,1,0:T(8,128)(2,1)}), bf16[8,256,256]{2,1,0:T(8,128)(2,1)}) %all-gather.2.cloned.1.call-update) | async-done | bytes 1048592 | tf_op jit(solution)/shard_map/all_gather | solution.py:17
  59.1 93.0 %while.13 = (s32[]{:T(128)}, f32[2,256,256]{2,0,1:T(2,128)}, s32[8,8]{1,0:T(8,128)S(1)}, s32[8,8]{1,0:T(8,128)S(1)}, bf16[8,256,256]{2,1,0:T(8,128)(2,1)}, /*ind...) while((s32[]{:T(128)}, f32[2,256,256]{2,0,1:T(2,128)}, ...), condition=%wide.region_1.3_spmd.clone, body=%wide.region_0.0_spmd.clone.sunk | while | flops 541330560 | bytes 29373212 | solution.py:46
  59.1 1.9 gather_fusion.1
  64.4 3.1 %fusion.36 = bf16[8,256,256]{2,1,0:T(8,128)(2,1)} fusion(bf16[8,256,256]{2,1,0:T(8,128)(2,1)S(1)} %copy-done.2, bf16[8,256,256]{2,1,0:T(8,128)(2,1)S(1)} %gather_fusion.1, bf16[8,256,256]{2,1,0:T(8,128)(2,1)} %gather_fusion.2, pred[8]{0:T(512)(128)(4,1)S(1)} %get-tuple-element.207, pred[8]{0:T(512)(128)(4,1)S(1)} %get-tuple-element.208, ...), kind=kOutput, calls=%fused_computation.6.clone.1 | convolution fusion | flops 538968064 | bytes 4194328 | tf_op jit(solution)/shard_map/while/body/eval_jaxpr/kac,kdc->kad/dot_general | solution.py:36
  67.5 2.4 %convolution_add_fusion.2 = f32[2,256,256]{2,0,1:T(2,128)S(1)} fusion(bf16[8,256,256]{2,1,0:T(8,128)(2,1)} %fusion.36, f32[2,256,256]{2,0,1:T(2,128)S(1)} %copy-done.3, pred[]{:T(512)S(6)} %compare.24, s32[8]{0:T(128)S(1)} %fusion.37), kind=kOutput, calls=%fused_computation.7.clone.1 | convolution fusion | flops 2359312 | bytes 2097185 | tf_op jit(solution)/shard_map/while/body/eval_jaxpr/jk,kad->jad/dot_general | solution.py:41
  70.8 1.9 gather_fusion.1
  76.0 3.1 %fusion.36 = bf16[8,256,256]{2,1,0:T(8,128)(2,1)} fusion(bf16[8,256,256]{2,1,0:T(8,128)(2,1)S(1)} %copy-done.2, bf16[8,256,256]{2,1,0:T(8,128)(2,1)S(1)} %gather_fusion.1, bf16[8,256,256]{2,1,0:T(8,128)(2,1)} %gather_fusion.2, pred[8]{0:T(512)(128)(4,1)S(1)} %get-tuple-element.207, pred[8]{0:T(512)(128)(4,1)S(1)} %get-tuple-element.208, ...), kind=kOutput, calls=%fused_computation.6.clone.1 | convolution fusion | flops 538968064 | bytes 4194328 | tf_op jit(solution)/shard_map/while/body/eval_jaxpr/kac,kdc->kad/dot_general | solution.py:36
  79.1 2.4 %convolution_add_fusion.2 = f32[2,256,256]{2,0,1:T(2,128)S(1)} fusion(bf16[8,256,256]{2,1,0:T(8,128)(2,1)} %fusion.36, f32[2,256,256]{2,0,1:T(2,128)S(1)} %copy-done.3, pred[]{:T(512)S(6)} %compare.24, s32[8]{0:T(128)S(1)} %fusion.37), kind=kOutput, calls=%fused_computation.7.clone.1 | convolution fusion | flops 2359312 | bytes 2097185 | tf_op jit(solution)/shard_map/while/body/eval_jaxpr/jk,kad->jad/dot_general | solution.py:41
  82.4 1.9 gather_fusion.1
  87.6 3.1 %fusion.36 = bf16[8,256,256]{2,1,0:T(8,128)(2,1)} fusion(bf16[8,256,256]{2,1,0:T(8,128)(2,1)S(1)} %copy-done.2, bf16[8,256,256]{2,1,0:T(8,128)(2,1)S(1)} %gather_fusion.1, bf16[8,256,256]{2,1,0:T(8,128)(2,1)} %gather_fusion.2, pred[8]{0:T(512)(128)(4,1)S(1)} %get-tuple-element.207, pred[8]{0:T(512)(128)(4,1)S(1)} %get-tuple-element.208, ...), kind=kOutput, calls=%fused_computation.6.clone.1 | convolution fusion | flops 538968064 | bytes 4194328 | tf_op jit(solution)/shard_map/while/body/eval_jaxpr/kac,kdc->kad/dot_general | solution.py:36
  90.7 2.4 %convolution_add_fusion.2 = f32[2,256,256]{2,0,1:T(2,128)S(1)} fusion(bf16[8,256,256]{2,1,0:T(8,128)(2,1)} %fusion.36, f32[2,256,256]{2,0,1:T(2,128)S(1)} %copy-done.3, pred[]{:T(512)S(6)} %compare.24, s32[8]{0:T(128)S(1)} %fusion.37), kind=kOutput, calls=%fused_computation.7.clone.1 | convolution fusion | flops 2359312 | bytes 2097185 | tf_op jit(solution)/shard_map/while/body/eval_jaxpr/jk,kad->jad/dot_general | solution.py:41
  99.2 3.1 %fusion.36 = bf16[8,256,256]{2,1,0:T(8,128)(2,1)} fusion(bf16[8,256,256]{2,1,0:T(8,128)(2,1)S(1)} %copy-done.2, bf16[8,256,256]{2,1,0:T(8,128)(2,1)S(1)} %gather_fusion.1, bf16[8,256,256]{2,1,0:T(8,128)(2,1)} %gather_fusion.2, pred[8]{0:T(512)(128)(4,1)S(1)} %get-tuple-element.207, pred[8]{0:T(512)(128)(4,1)S(1)} %get-tuple-element.208, ...), kind=kOutput, calls=%fused_computation.6.clone.1 | convolution fusion | flops 538968064 | bytes 4194328 | tf_op jit(solution)/shard_map/while/body/eval_jaxpr/kac,kdc->kad/dot_general | solution.py:36
  102.3 2.4 %convolution_add_fusion.2 = f32[2,256,256]{2,0,1:T(2,128)S(1)} fusion(bf16[8,256,256]{2,1,0:T(8,128)(2,1)} %fusion.36, f32[2,256,256]{2,0,1:T(2,128)S(1)} %copy-done.3, pred[]{:T(512)S(6)} %compare.24, s32[8]{0:T(128)S(1)} %fusion.37), kind=kOutput, calls=%fused_computation.7.clone.1 | convolution fusion | flops 2359312 | bytes 2097185 | tf_op jit(solution)/shard_map/while/body/eval_jaxpr/jk,kad->jad/dot_general | solution.py:41
  110.8 3.1 %fusion.36 = bf16[8,256,256]{2,1,0:T(8,128)(2,1)} fusion(bf16[8,256,256]{2,1,0:T(8,128)(2,1)S(1)} %copy-done.2, bf16[8,256,256]{2,1,0:T(8,128)(2,1)S(1)} %gather_fusion.1, bf16[8,256,256]{2,1,0:T(8,128)(2,1)} %gather_fusion.2, pred[8]{0:T(512)(128)(4,1)S(1)} %get-tuple-element.207, pred[8]{0:T(512)(128)(4,1)S(1)} %get-tuple-element.208, ...), kind=kOutput, calls=%fused_computation.6.clone.1 | convolution fusion | flops 538968064 | bytes 4194328 | tf_op jit(solution)/shard_map/while/body/eval_jaxpr/kac,kdc->kad/dot_general | solution.py:36
  113.9 2.4 %convolution_add_fusion.2 = f32[2,256,256]{2,0,1:T(2,128)S(1)} fusion(bf16[8,256,256]{2,1,0:T(8,128)(2,1)} %fusion.36, f32[2,256,256]{2,0,1:T(2,128)S(1)} %copy-done.3, pred[]{:T(512)S(6)} %compare.24, s32[8]{0:T(128)S(1)} %fusion.37), kind=kOutput, calls=%fused_computation.7.clone.1 | convolution fusion | flops 2359312 | bytes 2097185 | tf_op jit(solution)/shard_map/while/body/eval_jaxpr/jk,kad->jad/dot_general | solution.py:41
  122.5 3.1 %fusion.36 = bf16[8,256,256]{2,1,0:T(8,128)(2,1)} fusion(bf16[8,256,256]{2,1,0:T(8,128)(2,1)S(1)} %copy-done.2, bf16[8,256,256]{2,1,0:T(8,128)(2,1)S(1)} %gather_fusion.1, bf16[8,256,256]{2,1,0:T(8,128)(2,1)} %gather_fusion.2, pred[8]{0:T(512)(128)(4,1)S(1)} %get-tuple-element.207, pred[8]{0:T(512)(128)(4,1)S(1)} %get-tuple-element.208, ...), kind=kOutput, calls=%fused_computation.6.clone.1 | convolution fusion | flops 538968064 | bytes 4194328 | tf_op jit(solution)/shard_map/while/body/eval_jaxpr/kac,kdc->kad/dot_general | solution.py:36
  125.6 2.4 %convolution_add_fusion.2 = f32[2,256,256]{2,0,1:T(2,128)S(1)} fusion(bf16[8,256,256]{2,1,0:T(8,128)(2,1)} %fusion.36, f32[2,256,256]{2,0,1:T(2,128)S(1)} %copy-done.3, pred[]{:T(512)S(6)} %compare.24, s32[8]{0:T(128)S(1)} %fusion.37), kind=kOutput, calls=%fused_computation.7.clone.1 | convolution fusion | flops 2359312 | bytes 2097185 | tf_op jit(solution)/shard_map/while/body/eval_jaxpr/jk,kad->jad/dot_general | solution.py:41
  134.1 3.1 %fusion.36 = bf16[8,256,256]{2,1,0:T(8,128)(2,1)} fusion(bf16[8,256,256]{2,1,0:T(8,128)(2,1)S(1)} %copy-done.2, bf16[8,256,256]{2,1,0:T(8,128)(2,1)S(1)} %gather_fusion.1, bf16[8,256,256]{2,1,0:T(8,128)(2,1)} %gather_fusion.2, pred[8]{0:T(512)(128)(4,1)S(1)} %get-tuple-element.207, pred[8]{0:T(512)(128)(4,1)S(1)} %get-tuple-element.208, ...), kind=kOutput, calls=%fused_computation.6.clone.1 | convolution fusion | flops 538968064 | bytes 4194328 | tf_op jit(solution)/shard_map/while/body/eval_jaxpr/kac,kdc->kad/dot_general | solution.py:36
  137.2 2.4 %convolution_add_fusion.2 = f32[2,256,256]{2,0,1:T(2,128)S(1)} fusion(bf16[8,256,256]{2,1,0:T(8,128)(2,1)} %fusion.36, f32[2,256,256]{2,0,1:T(2,128)S(1)} %copy-done.3, pred[]{:T(512)S(6)} %compare.24, s32[8]{0:T(128)S(1)} %fusion.37), kind=kOutput, calls=%fused_computation.7.clone.1 | convolution fusion | flops 2359312 | bytes 2097185 | tf_op jit(solution)/shard_map/while/body/eval_jaxpr/jk,kad->jad/dot_general | solution.py:41
  145.7 3.1 %fusion.36 = bf16[8,256,256]{2,1,0:T(8,128)(2,1)} fusion(bf16[8,256,256]{2,1,0:T(8,128)(2,1)S(1)} %copy-done.2, bf16[8,256,256]{2,1,0:T(8,128)(2,1)S(1)} %gather_fusion.1, bf16[8,256,256]{2,1,0:T(8,128)(2,1)} %gather_fusion.2, pred[8]{0:T(512)(128)(4,1)S(1)} %get-tuple-element.207, pred[8]{0:T(512)(128)(4,1)S(1)} %get-tuple-element.208, ...), kind=kOutput, calls=%fused_computation.6.clone.1 | convolution fusion | flops 538968064 | bytes 4194328 | tf_op jit(solution)/shard_map/while/body/eval_jaxpr/kac,kdc->kad/dot_general | solution.py:36
  148.8 2.4 %convolution_add_fusion.2 = f32[2,256,256]{2,0,1:T(2,128)S(1)} fusion(bf16[8,256,256]{2,1,0:T(8,128)(2,1)} %fusion.36, f32[2,256,256]{2,0,1:T(2,128)S(1)} %copy-done.3, pred[]{:T(512)S(6)} %compare.24, s32[8]{0:T(128)S(1)} %fusion.37), kind=kOutput, calls=%fused_computation.7.clone.1 | convolution fusion | flops 2359312 | bytes 2097185 | tf_op jit(solution)/shard_map/while/body/eval_jaxpr/jk,kad->jad/dot_general | solution.py:41
  154.0 62.6 %reduce-scatter.2.cloned.1.call-done = f32[2,32,256]{2,1,0:T(8,128)} async-done(((f32[2,256,256]{2,1,0:T(8,128)}), f32[2,32,256]{2,1,0:T(8,128)}) %reduce-scatter.2.cloned.1.call-update) | async-done | bytes 65552 | tf_op jit(solution)/shard_map/reduce_scatter | solution.py:47
  (161 shorter events, 47.8 us)
Async XLA Ops:
  6.5 52.6 %all-gather.2.cloned.1.call-start = ((), (), s32[]{:S(2)}) async-start(), calls=%async_computation.1 | async-start | bytes 1310720 | tf_op jit(solution)/shard_map/all_gather | solution.py:17
  41.3 175.2 %reduce-scatter.2.cloned.1.call-start = ((), (), s32[]{:S(2)}) async-start(), calls=%async_computation.2 | async-start | bytes 589824 | tf_op jit(solution)/shard_map/reduce_scatter | solution.py:47
  59.1 2.0 copy-start.1
  62.7 1.6 copy-start.2
  64.4 3.1 %copy-start.3 = (f32[2,256,256]{2,0,1:T(2,128)S(1)}, f32[2,256,256]{2,0,1:T(2,128)}, u32[]{:S(2)}) copy-start(f32[2,256,256]{2,0,1:T(2,128)} %get-tuple-element.222) | copy-start | bytes 1572868 | tf_op jit(solution)/shard_map/while
  70.8 2.0 copy-start.1
  74.4 1.6 copy-start.2
  76.0 3.1 %copy-start.3 = (f32[2,256,256]{2,0,1:T(2,128)S(1)}, f32[2,256,256]{2,0,1:T(2,128)}, u32[]{:S(2)}) copy-start(f32[2,256,256]{2,0,1:T(2,128)} %get-tuple-element.222) | copy-start | bytes 1572868 | tf_op jit(solution)/shard_map/while
  82.4 2.0 copy-start.1
  86.0 1.6 copy-start.2
  87.6 3.1 %copy-start.3 = (f32[2,256,256]{2,0,1:T(2,128)S(1)}, f32[2,256,256]{2,0,1:T(2,128)}, u32[]{:S(2)}) copy-start(f32[2,256,256]{2,0,1:T(2,128)} %get-tuple-element.222) | copy-start | bytes 1572868 | tf_op jit(solution)/shard_map/while
  94.0 2.0 copy-start.1
  97.6 1.6 copy-start.2
  99.2 3.1 %copy-start.3 = (f32[2,256,256]{2,0,1:T(2,128)S(1)}, f32[2,256,256]{2,0,1:T(2,128)}, u32[]{:S(2)}) copy-start(f32[2,256,256]{2,0,1:T(2,128)} %get-tuple-element.222) | copy-start | bytes 1572868 | tf_op jit(solution)/shard_map/while
  105.6 2.0 copy-start.1
  109.2 1.6 copy-start.2
  110.8 3.1 %copy-start.3 = (f32[2,256,256]{2,0,1:T(2,128)S(1)}, f32[2,256,256]{2,0,1:T(2,128)}, u32[]{:S(2)}) copy-start(f32[2,256,256]{2,0,1:T(2,128)} %get-tuple-element.222) | copy-start | bytes 1572868 | tf_op jit(solution)/shard_map/while
  117.2 2.0 copy-start.1
  120.8 1.6 copy-start.2
  122.5 3.1 %copy-start.3 = (f32[2,256,256]{2,0,1:T(2,128)S(1)}, f32[2,256,256]{2,0,1:T(2,128)}, u32[]{:S(2)}) copy-start(f32[2,256,256]{2,0,1:T(2,128)} %get-tuple-element.222) | copy-start | bytes 1572868 | tf_op jit(solution)/shard_map/while
  128.8 2.0 copy-start.1
  134.1 3.1 %copy-start.3 = (f32[2,256,256]{2,0,1:T(2,128)S(1)}, f32[2,256,256]{2,0,1:T(2,128)}, u32[]{:S(2)}) copy-start(f32[2,256,256]{2,0,1:T(2,128)} %get-tuple-element.222) | copy-start | bytes 1572868 | tf_op jit(solution)/shard_map/while
  140.5 2.0 copy-start.1
  145.7 3.1 %copy-start.3 = (f32[2,256,256]{2,0,1:T(2,128)S(1)}, f32[2,256,256]{2,0,1:T(2,128)}, u32[]{:S(2)}) copy-start(f32[2,256,256]{2,0,1:T(2,128)} %get-tuple-element.222) | copy-start | bytes 1572868 | tf_op jit(solution)/shard_map/while
  (18 other events, 22.8 us)
Sparse Core Ops, SparseCore 0:
  41.4 17.6 all-gather.1
  154.1 62.3 reduce-scatter.1
where the time goes:
time: 224 us; the launch traced here: 223 us
  waiting for transfers between devices  73.7 us (33%)
  local copies, waits for them, and re-layouts  52.5 us (23%)
  matrix products  44.2 us (20%)
  blocking collectives  34.7 us (15%)
  between operations  13.4 us (6%)
  other arithmetic  4.09 us (2%)
    reduce_scatter x1, waiting for transfers between devices, shards(): lax.psum_scatter(partial_value, 'op', scatter_dimension=1, tiled=True)  62.6 us
    all_gather x1, blocking collectives, shards(): full = lax.all_gather(psi, 'op', axis=1, tiled=True)  34.7 us
    dot_general x8, matrix products, one_group(): jnp.einsum('kac,kdc->kad', half, right, preferred_element_type=jnp.float32)  24.6 us
    dot_general x8, matrix products, one_group(): jnp.einsum('jk,kad->jad', onehot, term, preferred_element_type=jnp.float32)  19.6 us
    gather x8, local copies, waits for them, and re-layouts, one_group(): block = jnp.take(table, block_ids, axis=0)  15.4 us
    gather x8, local copies, waits for them, and re-layouts, one_group(): left = jnp.take(left_ops, left_ids, axis=0)  12.9 us
    gather x8, local copies, waits for them, and re-layouts, one_group(): right = jnp.take(right_ops, right_ids, axis=0)  12.7 us
    all_gather x1, waiting for transfers between devices, shards(): table = lax.all_gather(full, 'sec', axis=0, tiled=True)  11.1 us
  transfers between devices with their start and end apart: 2, of which 2 were waited for; matrix products, arithmetic and copies ran while one was open for 3% of the time, Pallas kernels for 0%

commit v1 on v0

v1 whole, which is shorter than its diff:
```python
import functools

import jax
import jax.numpy as jnp
from jax import lax
from jax.experimental import pallas as pl
from jax.experimental.pallas import tpu as pltpu
from jax.sharding import PartitionSpec as P

CHUNK = 16
VMEM = pl.BlockSpec(memory_space=pltpu.VMEM)
SMEM = pl.BlockSpec(memory_space=pltpu.SMEM)
NT = (((1,), (1,)), ((), ()))


def pack_kernel(cap, held, place_ref, listed_ref, psi_ref, out_ref):
    my_sec = place_ref[0]
    n_sec, n_op = out_ref.shape[0], out_ref.shape[1]
    for d in range(n_sec):
        for o in range(n_op):
            for c in range(cap):
                sector = listed_ref[((my_sec * n_op + o) * n_sec + d) * cap + c] - my_sec * held
                out_ref[d, o, c] = psi_ref[sector]


def pack(psi, send_list):
    held, rows, width = psi.shape
    n_sec, n_op, _, cap = send_list.shape
    place = lax.axis_index("sec").astype(jnp.int32).reshape(1)
    return pl.pallas_call(
        functools.partial(pack_kernel, cap, held),
        out_shape=jax.ShapeDtypeStruct((n_sec, n_op, cap, rows, width), psi.dtype),
        in_specs=[SMEM, SMEM, VMEM],
        out_specs=VMEM,
    )(place, send_list.reshape(-1), psi)


def terms_kernel(split, slot_ref, out_id_ref, left_id_ref, right_id_ref, left_ref, right_ref, table_ref,
                 out_ref, half_ref, weight_ref, sum_ref):
    n_left, width = left_ref.shape[0], left_ref.shape[1]
    n_right = right_ref.shape[0]
    n_slot = table_ref.shape[0]
    n_pair = n_left * n_slot
    held = sum_ref.shape[0] // width
    n_cell = held * n_right
    chunks = width // CHUNK

    cell = out_id_ref[...] * n_right + right_id_ref[...]
    pair = slot_ref[...] * n_left + left_id_ref[...]
    n_term = cell.shape[1]
    row_cell = lax.broadcasted_iota(jnp.int32, (n_cell * CHUNK, n_term), 0) // CHUNK
    row_pair = lax.broadcasted_iota(jnp.int32, (n_pair * CHUNK, n_term), 0) // CHUNK
    in_cell = jnp.where(row_cell == cell, 1.0, 0.0).astype(jnp.bfloat16)
    in_pair = jnp.where(row_pair == pair, 1.0, 0.0).astype(jnp.bfloat16)
    count = lax.dot_general(in_cell, in_pair, NT, preferred_element_type=jnp.float32)
    a = lax.broadcasted_iota(jnp.int32, count.shape, 0) % CHUNK
    b = lax.broadcasted_iota(jnp.int32, count.shape, 1) % CHUNK
    weight_ref[...] = jnp.where(a == b, count, 0.0).astype(jnp.bfloat16)

    for s in range(n_slot):
        for l in range(n_left):
            half = jnp.dot(left_ref[l], table_ref[s], preferred_element_type=jnp.float32).astype(jnp.bfloat16)
            p = s * n_left + l
            for m in range(chunks):
                half_ref[m, p * CHUNK:(p + 1) * CHUNK, :] = half[m * CHUNK:(m + 1) * CHUNK, :]

    for m in range(chunks):
        total = jnp.dot(weight_ref[...], half_ref[m], preferred_element_type=jnp.float32).astype(jnp.bfloat16)
        for j in range(held):
            for r in range(n_right):
                p = j * n_right + r
                sum_ref[j * width + m * CHUNK:j * width + (m + 1) * CHUNK, r * width:(r + 1) * width] = (
                    total[p * CHUNK:(p + 1) * CHUNK, :])

    for j in range(held):
        acc = jnp.zeros((width, width), jnp.float32)
        for r in range(n_right):
            acc = acc + lax.dot_general(
                sum_ref[j * width:(j + 1) * width, r * width:(r + 1) * width], right_ref[r], NT,
                preferred_element_type=jnp.float32)
        acc = acc.astype(out_ref.dtype)
        if split:
            n_op, rows = out_ref.shape[0], out_ref.shape[2]
            for o in range(n_op):
                out_ref[o, j] = acc[o * rows:(o + 1) * rows, :]
        else:
            out_ref[j] = acc


def terms(table, left_ops, right_ops, term_slot, term_out, left_pick, right_pick, held, n_op):
    n_slot, width = table.shape[0], table.shape[1]
    n_left, n_right = left_ops.shape[0], right_ops.shape[0]
    n_term = term_slot.shape[0]
    rows = width // n_op
    split = rows % 16 == 0
    shape = (n_op, held, rows, width) if split else (held, width, width)
    ids = [x.reshape(1, n_term) for x in (term_slot, term_out, left_pick, right_pick)]
    out = pl.pallas_call(
        functools.partial(terms_kernel, split),
        out_shape=jax.ShapeDtypeStruct(shape, jnp.bfloat16),
        in_specs=[VMEM] * 7,
        out_specs=VMEM,
        scratch_shapes=[
            pltpu.VMEM((width // CHUNK, n_slot * n_left * CHUNK, width), jnp.bfloat16),
            pltpu.VMEM((held * n_right * CHUNK, n_slot * n_left * CHUNK), jnp.bfloat16),
            pltpu.VMEM((held * width, n_right * width), jnp.bfloat16),
        ],
        compiler_params=pltpu.CompilerParams(vmem_limit_bytes=48 * 1024 * 1024),
        cost_estimate=pl.CostEstimate(flops=6 * 10**9, bytes_accessed=4 * 10**6, transcendentals=0),
    )(*ids, left_ops, right_ops, table)
    if not split:
        out = out.reshape(held, n_op, rows, width).transpose(1, 0, 2, 3)
    return out


def shards(psi, left_ops, right_ops, send_list, term_slot, term_out, left_pick, right_pick):
    held, rows, width = psi.shape
    n_sec, n_op, _, cap = send_list.shape
    packed = pack(psi, send_list).reshape(n_sec * n_op, cap, rows, width)
    got = lax.all_to_all(packed, ("sec", "op"), 0, 0, tiled=True)
    table = got.reshape(n_sec, n_op, cap, rows, width).transpose(0, 2, 1, 3, 4).reshape(n_sec * cap, width, width)
    partial_sum = terms(table, left_ops, right_ops, term_slot, term_out, left_pick, right_pick, held, n_op)
    parts = lax.all_to_all(partial_sum, "op", 0, 0, tiled=True)
    return jnp.sum(parts.astype(jnp.float32), axis=0)


def solution(mesh):
    in_specs = (
        P("sec", "op", None),
        P(("sec", "op"), None, None),
        P(("sec", "op"), None, None),
        P(),
        P(("sec", "op")),
        P(("sec", "op")),
        P(("sec", "op")),
        P(("sec", "op")),
    )
    out_specs = P("sec", "op", None)
    return jax.shard_map(shards, mesh=mesh, in_specs=in_specs, out_specs=out_specs, check_vma=False)
```

time: 224 us -> 44.1 us (0.20)
  waiting for transfers between devices: 73.7 us -> 0 us
  local copies, waits for them, and re-layouts: 52.5 us -> 3.39 us
  matrix products: 44.2 us -> 0 us
  between operations: 13.4 us -> 0.03 us
  Pallas kernels: 0 us -> 4.64 us
  other arithmetic: 4.09 us -> 0.67 us
    reduce_scatter x1 -> x0, waiting for transfers between devices: 62.6 us -> none  [shards(): lax.psum_scatter(partial_value, 'op', scatter_dimension=1, tiled=True)]
    dot_general x16 -> x0, matrix products: 44.2 us -> none  [the longest x8 24.6 us: one_group(): jnp.einsum('kac,kdc->kad', half, right, preferred_element_type=jnp.float32)]
    gather x25 -> x0, local copies, waits for them, and re-layouts: 41.6 us -> none  [the longest x8 15.4 us: one_group(): block = jnp.take(table, block_ids, axis=0)]
    all_to_all x0 -> x2, blocking collectives: none -> 35 us  [the longest x1 23.7 us: shards(): got = lax.all_to_all(packed, ('sec', 'op'), 0, 0, tiled=True)]
    all_gather x1 -> x0, blocking collectives: 34.7 us -> none  [shards(): full = lax.all_gather(psi, 'op', axis=1, tiled=True)]
    all_gather x1 -> x0, waiting for transfers between devices: 11.1 us -> none  [shards(): table = lax.all_gather(full, 'sec', axis=0, tiled=True)]
    while x81 -> x0, local copies, waits for them, and re-layouts: 8.55 us -> none
    pallas_call x0 -> x2, Pallas kernels: none -> 4.64 us  [the longest x1 3.04 us: terms(): pl.pallas_call(functools.partial(terms_kernel, split), out_shape=jax.Shap...]
  transfers between devices with their start and end apart: 2 -> 0, of which waited for: 2 -> 0; matrix products, arithmetic and copies ran while one was open for 3% -> 0% of each run, Pallas kernels for 0% -> 0%
where the time goes in v1:
time: 44.1 us; the launch traced here: 43.7 us
  blocking collectives  35 us (79%)
  Pallas kernels  4.64 us (11%)
  local copies, waits for them, and re-layouts  3.39 us (8%)
  other arithmetic  0.67 us (2%)
    all_to_all x1, blocking collectives, shards(): got = lax.all_to_all(packed, ('sec', 'op'), 0, 0, tiled=True)  23.7 us
    all_to_all x1, blocking collectives, shards(): parts = lax.all_to_all(partial_sum, 'op', 0, 0, tiled=True)  11.3 us
    pallas_call x1, Pallas kernels, terms(): pl.pallas_call(functools.partial(terms_kernel, split), out_shape=jax.Shap...  3.04 us
    unnamed x13, local copies, waits for them, and re-layouts  2.78 us
    pallas_call x1, Pallas kernels, pack(): pl.pallas_call(functools.partial(pack_kernel, cap, held), out_shape=jax.S...  1.6 us

profile of v1, /device:TPU:0, one launch (start us, length us, event | category | flops | bytes accessed | tf_op | source)
XLA Modules:
  0.0 43.7 jit_solution(1866463121888977551)
XLA Ops:
  0.0 0.0 copy-start
  0.0 0.9 %copy.11 = s32[4,8,4,1]{2,1,0,3:T(8,128)S(1)} copy(s32[4,8,4,1]{1,3,2,0:T(1,128)} %param.11) | data formatting | bytes 1024 | tf_op args[3]
  0.9 0.6 %reshape.26.listed_ref = s32[128]{0:T(128)} reshape(s32[4,8,4,1]{2,1,0,3:T(8,128)S(1)} %copy.11) | data formatting | bytes 1024 | tf_op jit(solution)/shard_map/reshape | solution.py:35
  1.5 1.6 %shard_map.82 = bf16[4,8,1,32,256]{4,3,2,1,0:T(8,128)(2,1)} custom-call(s32[1]{0:T(128)} %bitcast.4.place_ref, s32[128]{0:T(128)} %reshape.26.listed_ref, bf16[2,32,256]{2,1,0:T(8,128)(2,1)} %psi_ref.1), custom_call_target="tpu_custom_call" | custom-call | tf_op jit(solution)/shard_map/pallas_call | solution.py:30
  3.1 0.0 copy-start.5
  3.1 23.7 %all_to_all.10 = bf16[32,1,32,256]{3,2,1,0:T(8,128)(2,1)S(1)} all-to-all(bf16[32,1,32,256]{3,2,1,0:T(8,128)(2,1)} %bitcast.18), channel_id=1, replica_groups=mesh['sec'=4,'op'=8] {'sec','op'}, dimensions={0} | all-to-all | bytes 1048576 | tf_op jit(solution)/shard_map/all_to_all | solution.py:120
  26.8 0.0 copy-start.2
  26.8 0.0 copy-start.3
  26.8 0.0 copy-start.4
  26.8 0.0 copy-done
  26.8 0.0 copy-done.5
  26.8 0.6 %copy-done.2 = s32[64]{0:T(128)S(1)} copy-done((s32[64]{0:T(128)S(1)}, s32[64]{0:T(128)}, u32[]{:S(2)}) %copy-start.2) | copy-done | bytes 280
  27.4 0.0 copy-done.3
  27.4 0.0 copy-done.4
  27.4 0.0 copy-start.1
  27.4 1.2 %copy-done.1 = bf16[8,256,256]{2,1,0:T(8,128)(2,1)S(1)} copy-done((bf16[8,256,256]{2,1,0:T(8,128)(2,1)S(1)}, bf16[8,256,256]{2,1,0:T(8,128)(2,1)}, u32[]{:S(2)}) %copy-start.1) | copy-done | bytes 1048600
  28.7 3.0 %shard_map.83 = bf16[8,2,32,256]{3,2,1,0:T(8,128)(2,1)S(1)} custom-call(s32[1,64]{1,0:T(1,128)S(1)} %bitcast.14, s32[1,64]{1,0:T(1,128)S(1)} %bitcast.15, s32[1,64]{1,0:T(1,128)S(1)} %bitcast.16, s32[1,64]{1,0:T(1,128)S(1)} %bitcast.17, bf16[8,256,256]{2,1,0:T(8,128)(2,1)S(1)} %copy-done, bf16[8,256,256]{2,1,0:T(8,128)(2,1)S(1)} %copy-done.1, ...), custom_call_target="tpu_custom_call" | custom-call | flops 6000000000 | bytes 4000000 | tf_op jit(solution)/shard_map/pallas_call | solution.py:98
  31.7 11.3 %all_to_all.11 = bf16[8,2,32,256]{3,2,1,0:T(8,128)(2,1)S(1)} all-to-all(bf16[8,2,32,256]{3,2,1,0:T(8,128)(2,1)S(1)} %shard_map.83), channel_id=1, replica_groups=mesh['sec'=4,'op'=8] {'op'}, dimensions={0} | all-to-all | bytes 524288 | tf_op jit(solution)/shard_map/all_to_all | solution.py:123
  43.1 0.7 %convert_reduce_fusion = f32[2,32,256]{2,1,0:T(8,128)} fusion(bf16[8,2,32,256]{3,2,1,0:T(8,128)(2,1)S(1)} %all_to_all.11), kind=kLoop, calls=%fused_computation | loop fusion | flops 245760 | bytes 327680 | tf_op jit(solution)/shard_map/reduce_sum | solution.py:124
Async XLA Ops:
  0.0 26.8 %copy-start = (bf16[8,256,256]{2,1,0:T(8,128)(2,1)S(1)}, bf16[8,256,256]{2,1,0:T(8,128)(2,1)}, u32[]{:S(2)}) copy-start(bf16[8,256,256]{2,1,0:T(8,128)(2,1)} %left_ref.1) | copy-start | bytes 3145732
  3.1 23.7 %copy-start.5 = (s32[64]{0:T(128)S(1)}, s32[64]{0:T(128)}, u32[]{:S(2)}) copy-start(s32[64]{0:T(128)} %param.15) | copy-start | bytes 772
  26.8 0.7 %copy-start.2 = (s32[64]{0:T(128)S(1)}, s32[64]{0:T(128)}, u32[]{:S(2)}) copy-start(s32[64]{0:T(128)} %param.12) | copy-start | bytes 772
  26.8 0.7 %copy-start.3 = (s32[64]{0:T(128)S(1)}, s32[64]{0:T(128)}, u32[]{:S(2)}) copy-start(s32[64]{0:T(128)} %param.13) | copy-start | bytes 772
  26.8 0.7 %copy-start.4 = (s32[64]{0:T(128)S(1)}, s32[64]{0:T(128)}, u32[]{:S(2)}) copy-start(s32[64]{0:T(128)} %param.14) | copy-start | bytes 772
  27.4 1.2 %copy-start.1 = (bf16[8,256,256]{2,1,0:T(8,128)(2,1)S(1)}, bf16[8,256,256]{2,1,0:T(8,128)(2,1)}, u32[]{:S(2)}) copy-start(bf16[8,256,256]{2,1,0:T(8,128)(2,1)} %right_ref.1) | copy-start | bytes 3145732

commit v2 on v1

v2 whole, which is shorter than its diff:
```python
import functools

import jax
import jax.numpy as jnp
from jax import lax
from jax.experimental import pallas as pl
from jax.experimental.pallas import tpu as pltpu
from jax.sharding import PartitionSpec as P

CHUNK = 8
VMEM = pl.BlockSpec(memory_space=pltpu.VMEM)
SMEM = pl.BlockSpec(memory_space=pltpu.SMEM)
ANY = pl.BlockSpec(memory_space=pl.ANY)
NT = (((1,), (1,)), ((), ()))
BF16 = jnp.bfloat16


def choose_kernel(held, place_ref, listed_ref, choice_ref, side_ref):
    my_sec, my_half = place_ref[0], place_ref[1]
    n_sec, half_op, cap = choice_ref.shape[:3]
    for d in range(n_sec):
        for q in range(half_op):
            for c in range(cap):
                choice = listed_ref[my_sec, d, c, my_half * half_op + q] - my_sec * held
                choice_ref[d, q, c] = jnp.full(choice_ref.shape[3:], choice.astype(jnp.float32)).astype(BF16)
    side_ref[...] = jnp.full(side_ref.shape, my_half.astype(jnp.float32)).astype(BF16)


def choose(send_list, held, rows, width):
    n_sec, n_op, _, cap = send_list.shape
    place = jnp.stack([lax.axis_index("sec"), lax.div(lax.axis_index("op"), n_op // 2)]).astype(jnp.int32)
    return pl.pallas_call(
        functools.partial(choose_kernel, held),
        out_shape=[
            jax.ShapeDtypeStruct((n_sec, n_op // 2, cap, rows, width), BF16),
            jax.ShapeDtypeStruct((rows, width), BF16),
        ],
        in_specs=[SMEM, SMEM],
        out_specs=[VMEM, VMEM],
        compiler_params=pltpu.CompilerParams(vmem_limit_bytes=4 * 1024 * 1024),
        cost_estimate=pl.CostEstimate(flops=10**6, bytes_accessed=2 * 10**6, transcendentals=0),
    )(place, send_list.transpose(0, 2, 3, 1))


def weight_kernel(n_left, n_right, slot_hbm, out_id_hbm, left_id_hbm, right_id_hbm, weight_ref, ids_ref, sems):
    n_pair, n_cell = weight_ref.shape[1] // CHUNK, weight_ref.shape[0] // CHUNK
    copies = [pltpu.make_async_copy(x, ids_ref.at[i], sems.at[i])
              for i, x in enumerate((slot_hbm, out_id_hbm, left_id_hbm, right_id_hbm))]
    for copy in copies:
        copy.start()
    for copy in copies:
        copy.wait()

    cell = ids_ref[1] * n_right + ids_ref[3]
    pair = ids_ref[0] * n_left + ids_ref[2]
    n_term = cell.shape[1]
    row_cell = lax.broadcasted_iota(jnp.int32, (n_cell * CHUNK, n_term), 0) // CHUNK
    row_pair = lax.broadcasted_iota(jnp.int32, (n_pair * CHUNK, n_term), 0) // CHUNK
    in_cell = jnp.where(row_cell == cell, 1.0, 0.0).astype(BF16)
    in_pair = jnp.where(row_pair == pair, 1.0, 0.0).astype(BF16)
    count = lax.dot_general(in_cell, in_pair, NT, preferred_element_type=jnp.float32)
    a = lax.broadcasted_iota(jnp.int32, count.shape, 0) % CHUNK
    b = lax.broadcasted_iota(jnp.int32, count.shape, 1) % CHUNK
    weight_ref[...] = jnp.where(a == b, count, 0.0).astype(BF16)


def weights(n_slot, n_left, n_right, held, term_slot, term_out, left_pick, right_pick):
    n_pair, n_cell = n_slot * n_left, held * n_right
    n_term = term_slot.shape[0]
    ids = [x.reshape(1, n_term) for x in (term_slot, term_out, left_pick, right_pick)]
    return pl.pallas_call(
        functools.partial(weight_kernel, n_left, n_right),
        out_shape=jax.ShapeDtypeStruct((n_cell * CHUNK, n_pair * CHUNK), BF16),
        in_specs=[ANY] * 4,
        out_specs=VMEM,
        scratch_shapes=[pltpu.VMEM((4, 1, n_term), jnp.int32), pltpu.SemaphoreType.DMA((4,))],
        compiler_params=pltpu.CompilerParams(vmem_limit_bytes=8 * 1024 * 1024),
        cost_estimate=pl.CostEstimate(flops=10**9, bytes_accessed=8 * 10**6, transcendentals=0),
    )(*ids)


def pack_kernel(choice_ref, side_ref, near_ref, far_ref, out_ref):
    n_sec, half_op, cap = choice_ref.shape[:3]
    low = side_ref[...] == 0
    pairs = [(jnp.where(low, near_ref[t], far_ref[t]), jnp.where(low, far_ref[t], near_ref[t]))
             for t in range(near_ref.shape[0])]
    for d in range(n_sec):
        for q in range(half_op):
            for c in range(cap):
                choice = choice_ref[d, q, c]
                first, second = pairs[0]
                for t in range(1, len(pairs)):
                    first = jnp.where(choice == t, pairs[t][0], first)
                    second = jnp.where(choice == t, pairs[t][1], second)
                out_ref[d, q, 0, c] = first
                out_ref[d, q, 1, c] = second


def pack(near, far, choice, side):
    n_sec, half_op, cap, rows, width = choice.shape
    return pl.pallas_call(
        pack_kernel,
        out_shape=jax.ShapeDtypeStruct((n_sec, half_op, 2, cap, rows, width), near.dtype),
        in_specs=[VMEM] * 4,
        out_specs=VMEM,
        compiler_params=pltpu.CompilerParams(vmem_limit_bytes=4 * 1024 * 1024),
        cost_estimate=pl.CostEstimate(flops=10**6, bytes_accessed=2 * 10**6, transcendentals=0),
    )(choice, side, near, far)


def terms_kernel(split, left_ref, right_ref, weight_ref, table_ref, out_ref, half_ref, sum_ref):
    n_left, width = left_ref.shape[0], left_ref.shape[1]
    n_right = right_ref.shape[0]
    n_slot = table_ref.shape[0]
    held = sum_ref.shape[0] // width
    chunks = width // CHUNK

    for s in range(n_slot):
        block = [table_ref[s, q, h] for h in range(table_ref.shape[2]) for q in range(table_ref.shape[1])]
        block = jnp.concatenate(block, axis=0) if len(block) > 1 else block[0]
        for l in range(0, n_left, 2):
            two = [jnp.dot(left_ref[l + i], block, preferred_element_type=jnp.float32) for i in range(2)]
            p = s * n_left + l
            for m in range(chunks):
                piece = jnp.concatenate([x[m * CHUNK:(m + 1) * CHUNK, :] for x in two], axis=0)
                half_ref[m, p * CHUNK:(p + 2) * CHUNK, :] = piece.astype(BF16)

    for m in range(0, chunks, 2):
        two = [jnp.dot(weight_ref[...], half_ref[m + i], preferred_element_type=jnp.float32) for i in range(2)]
        for j in range(held):
            for r in range(n_right):
                p = j * n_right + r
                piece = jnp.concatenate([x[p * CHUNK:(p + 1) * CHUNK, :] for x in two], axis=0)
                sum_ref[j * width + m * CHUNK:j * width + (m + 2) * CHUNK, r * width:(r + 1) * width] = piece.astype(BF16)

    for j in range(held):
        acc = None
        for r in range(n_right):
            part = lax.dot_general(
                sum_ref[j * width:(j + 1) * width, r * width:(r + 1) * width], right_ref[r], NT,
                preferred_element_type=jnp.float32)
            acc = part if acc is None else acc + part
        acc = acc.astype(out_ref.dtype)
        if split:
            n_op, rows = out_ref.shape[0], out_ref.shape[2]
            for o in range(n_op):
                out_ref[o, j] = acc[o * rows:(o + 1) * rows, :]
        else:
            out_ref[j] = acc


def terms(table, left, right, weight, held, n_op):
    n_slot, width = table.shape[0], table.shape[-1]
    n_left, n_right = left.shape[0], right.shape[0]
    rows = width // n_op
    split = rows % 16 == 0
    shape = (n_op, held, rows, width) if split else (held, width, width)
    n_pair, n_cell = n_slot * n_left, held * n_right
    blocks = n_pair + n_cell + n_left + n_right + n_slot + 4 * held
    out = pl.pallas_call(
        functools.partial(terms_kernel, split),
        out_shape=jax.ShapeDtypeStruct(shape, BF16),
        in_specs=[VMEM] * 4,
        out_specs=VMEM,
        scratch_shapes=[
            pltpu.VMEM((width // CHUNK, n_pair * CHUNK, width), BF16),
            pltpu.VMEM((held * width, n_right * width), BF16),
        ],
        compiler_params=pltpu.CompilerParams(vmem_limit_bytes=2 * width * width * blocks + 16 * 1024 * 1024),
        cost_estimate=pl.CostEstimate(flops=5 * 10**9, bytes_accessed=4 * 10**6, transcendentals=0),
    )(left, right, weight, table)
    if not split:
        out = out.reshape(held, n_op, rows, width).transpose(1, 0, 2, 3)
    return out


def shards(psi, left_ops, right_ops, send_list, term_slot, term_out, left_pick, right_pick):
    held, rows, width = psi.shape
    n_sec, n_op, _, cap = send_list.shape
    half_op = n_op // 2
    far = lax.ppermute(psi, "op", [(o, o ^ half_op) for o in range(n_op)])
    choice, side = choose(send_list, held, rows, psi.shape[2])
    weight = weights(
        n_sec * cap, left_ops.shape[0], right_ops.shape[0], held, term_slot, term_out, left_pick, right_pick)
    packed = pack(psi, far, choice, side).reshape(n_sec * half_op, 2, cap, rows, width)
    groups = [[s * n_op + h * half_op + q for s in range(n_sec) for q in range(half_op)] for h in range(2)]
    got = lax.all_to_all(packed, ("sec", "op"), 0, 0, tiled=True, axis_index_groups=groups)
    got = got.reshape(n_sec, half_op, 2, cap, rows, width).transpose(0, 3, 1, 2, 4, 5)
    table = got.reshape(n_sec * cap, half_op, 2, rows, width)
    if rows % 16:
        table = table.transpose(0, 2, 1, 3, 4).reshape(n_sec * cap, 1, 1, width, width)
    partial_sum = terms(table, left_ops, right_ops, weight, held, n_op)
    parts = lax.all_to_all(partial_sum, "op", 0, 0, tiled=True)
    return jnp.sum(parts.astype(jnp.float32), axis=0)


def solution(mesh):
    in_specs = (
        P("sec", "op", None),
        P(("sec", "op"), None, None),
        P(("sec", "op"), None, None),
        P(),
        P(("sec", "op")),
        P(("sec", "op")),
        P(("sec", "op")),
        P(("sec", "op")),
    )
    out_specs = P("sec", "op", None)
    return jax.shard_map(shards, mesh=mesh, in_specs=in_specs, out_specs=out_specs, check_vma=False)
```

time: 44.1 us -> 39.1 us (0.89)
  blocking collectives: 35 us -> 14.1 us
  waiting for transfers between devices: 0 us -> 9.4 us
  starting transfers between devices: 0 us -> 8.92 us
  local copies, waits for them, and re-layouts: 3.39 us -> 1.37 us
    all_to_all x1 -> x0, blocking collectives: 23.7 us -> none  [shards(): got = lax.all_to_all(packed, ('sec', 'op'), 0, 0, tiled=True)]
    all_to_all x0 -> x1, waiting for transfers between devices: none -> 8.37 us  [shards(): lax.all_to_all(packed, ('sec', 'op'), 0, 0, tiled=True, axis_index_groups...]
    all_to_all x0 -> x1, starting transfers between devices: none -> 4.88 us  [shards(): lax.all_to_all(packed, ('sec', 'op'), 0, 0, tiled=True, axis_index_groups...]
    ppermute x0 -> x1, starting transfers between devices: none -> 4.04 us  [shards(): far = lax.ppermute(psi, 'op', [(o, o ^ half_op) for o in range(n_op)])]
    all_to_all x1, blocking collectives: 11.3 us -> 14.1 us  [shards(): parts = lax.all_to_all(partial_sum, 'op', 0, 0, tiled=True)]
    unnamed x13 -> x16, local copies, waits for them, and re-layouts: 2.78 us -> 1.37 us
    ppermute x0 -> x1, waiting for transfers between devices: none -> 1.03 us  [shards(): far = lax.ppermute(psi, 'op', [(o, o ^ half_op) for o in range(n_op)])]
    reshape x1 -> x0, local copies, waits for them, and re-layouts: 0.61 us -> none  [pack(): send_list.reshape(-1)]
  transfers between devices with their start and end apart: 0 -> 2, of which waited for: 0 -> 2; matrix products, arithmetic and copies ran while one was open for 0% -> 0% of each run, Pallas kernels for 0% -> 2%
where the time goes in v2:
time: 39.1 us; the launch traced here: 38.8 us
  blocking collectives  14.1 us (36%)
  waiting for transfers between devices  9.4 us (24%)
  starting transfers between devices  8.92 us (23%)
  Pallas kernels  4.28 us (11%)
  local copies, waits for them, and re-layouts  1.37 us (4%)
  other arithmetic  0.74 us (2%)
    all_to_all x1, blocking collectives, shards(): parts = lax.all_to_all(partial_sum, 'op', 0, 0, tiled=True)  14.1 us
    all_to_all x1, waiting for transfers between devices, shards(): lax.all_to_all(packed, ('sec', 'op'), 0, 0, tiled=True, axis_index_groups...  8.37 us
    all_to_all x1, starting transfers between devices, shards(): lax.all_to_all(packed, ('sec', 'op'), 0, 0, tiled=True, axis_index_groups...  4.88 us
    ppermute x1, starting transfers between devices, shards(): far = lax.ppermute(psi, 'op', [(o, o ^ half_op) for o in range(n_op)])  4.04 us
    pallas_call x1, Pallas kernels, terms(): pl.pallas_call(functools.partial(terms_kernel, split), out_shape=jax.Shap...  2.51 us
    unnamed x16, local copies, waits for them, and re-layouts  1.37 us
    ppermute x1, waiting for transfers between devices, shards(): far = lax.ppermute(psi, 'op', [(o, o ^ half_op) for o in range(n_op)])  1.03 us
    pallas_call x1, Pallas kernels, pack(): pl.pallas_call(pack_kernel, out_shape=jax.ShapeDtypeStruct((n_sec, half_o...  0.84 us
  transfers between devices with their start and end apart: 2, of which 2 were waited for; matrix products, arithmetic and copies ran while one was open for 0% of the time, Pallas kernels for 2%

profile of v2, /device:TPU:0, one launch (start us, length us, event | category | flops | bytes accessed | tf_op | source)
XLA Modules:
  0.0 38.8 jit_solution(10575025957789860933)
XLA Ops:
  0.0 0.0 copy-start
  0.0 4.0 %collective-permute-start = (bf16[2,32,256]{2,1,0:T(8,128)(2,1)}, bf16[2,32,256]{2,1,0:T(8,128)(2,1)S(1)}, u32[]{:S(2)}, u32[]{:S(2)}) collective-permute-start(bf16[2,32,256]{2,1,0:T(8,128)(2,1)} %near_ref.1), channel_id=1, source_target_pairs={{0,4},{1,5},{2,6},{3,7},{4,0},{5,1},{6,2},{7,3},{8,12},{9,13},{10,... | collective-permute-start | bytes 98312 | tf_op jit(solution)/shard_map/ppermute | solution.py:181
  4.0 0.1 pad_add_fusion.place_ref
  4.1 0.0 copy-start.1
  4.1 0.7 %copy-done.1 = s32[4,8,4,1]{1,3,2,0:T(1,128)S(1)} copy-done((s32[4,8,4,1]{1,3,2,0:T(1,128)S(1)}, s32[4,8,4,1]{1,3,2,0:T(1,128)}, u32[]{:S(2)}) %copy-start.1) | copy-done | bytes 536
  4.8 0.7 %shard_map.83 = (bf16[4,4,1,32,256]{4,3,2,1,0:T(8,128)(2,1)S(1)}, bf16[32,256]{1,0:T(8,128)(2,1)S(1)}) custom-call(s32[2]{0:T(128)S(1)} %pad_add_fusion.place_ref, s32[4,4,1,8]{3,2,1,0:T(1,128)S(1)} %bitcast.12), custom_call_target="tpu_custom_call" | custom-call | flops 1000000 | bytes 2000000 | tf_op jit(solution)/shard_map/pallas_call | solution.py:32
  5.5 1.0 %collective-permute-done.far_ref = bf16[2,32,256]{2,1,0:T(8,128)(2,1)S(1)} collective-permute-done((bf16[2,32,256]{2,1,0:T(8,128)(2,1)}, bf16[2,32,256]{2,1,0:T(8,128)(2,1)S(1)}, u32[]{:S(2)}, u32[]{:S(2)}) %collective-permute-start) | collective-permute-done | bytes 32800 | tf_op jit(solution)/shard_map/ppermute | solution.py:181
  6.6 0.0 copy-done
  6.6 0.8 %shard_map.84 = bf16[4,4,2,1,32,256]{5,4,3,2,1,0:T(8,128)(2,1)} custom-call(bf16[4,4,1,32,256]{4,3,2,1,0:T(8,128)(2,1)S(1)} %get-tuple-element.7.choice_ref, bf16[32,256]{1,0:T(8,128)(2,1)S(1)} %get-tuple-element.8.side_ref, bf16[2,32,256]{2,1,0:T(8,128)(2,1)S(1)} %copy-done, bf16[2,32,256]{2,1,0:T(8,128)(2,1)S(1)} %collective-permute-done.far_ref), custom_call_target="tpu_custom_call" | custom-call | flops 1000000 | bytes 2000000 | tf_op jit(solution)/shard_map/pallas_call | solution.py:101
  7.4 4.9 %all-to-all-start = ((bf16[16,2,1,32,256]{4,3,1,2,0:T(8,128)(2,1)}), bf16[16,2,1,32,256]{4,3,1,2,0:T(8,128)(2,1)S(1)}, u32[]{:S(2)}, u32[]{:S(2)}) async-start(bf16[16,2,1,32,256]{4,3,1,2,0:T(8,128)(2,1)} %bitcast.8), calls=%async_computation | async-start | bytes 1048576 | tf_op jit(solution)/shard_map/all_to_all | solution.py:187
  12.3 0.0 copy-start.4
  12.3 0.0 copy-start.5
  12.3 0.0 copy-start.6
  12.3 0.0 copy-done.7
  12.3 0.6 %copy-done.4 = s32[64]{0:T(128)S(1)} copy-done((s32[64]{0:T(128)S(1)}, s32[64]{0:T(128)}, u32[]{:S(2)}) %copy-start.4) | copy-done | bytes 280
  13.0 0.0 copy-done.5
  13.0 0.0 copy-done.6
  13.0 0.2 shard_map.82.weight_ref
  13.2 8.4 %all-to-all-done = bf16[16,2,1,32,256]{4,3,1,2,0:T(8,128)(2,1)S(1)} async-done(((bf16[16,2,1,32,256]{4,3,1,2,0:T(8,128)(2,1)}), bf16[16,2,1,32,256]{4,3,1,2,0:T(8,128)(2,1)S(1)}, u32[]{:S(2)}, u32[]{:S(2)}) %all-to-all-start) | async-done | bytes 524320 | tf_op jit(solution)/shard_map/all_to_all | solution.py:187
  21.6 0.0 copy-done.2
  21.6 0.0 copy-done.3
  21.6 2.5 %shard_map.85 = bf16[8,2,32,256]{3,2,1,0:T(8,128)(2,1)S(1)} custom-call(bf16[8,256,256]{2,1,0:T(8,128)(2,1)S(1)} %copy-done.2, bf16[8,256,256]{2,1,0:T(8,128)(2,1)S(1)} %copy-done.3, bf16[128,256]{1,0:T(8,128)(2,1)S(1)} %shard_map.82.weight_ref, bf16[4,4,2,32,256]{4,3,2,1,0:T(8,128)(2,1)S(1)} %bitcast.11), custom_call_target="tpu_custom_call" | custom-call | flops 5000000000 | bytes 4000000 | tf_op jit(solution)/shard_map/pallas_call | solution.py:160
  24.1 14.1 %all_to_all.10 = bf16[8,2,32,256]{3,2,1,0:T(8,128)(2,1)S(1)} all-to-all(bf16[8,2,32,256]{3,2,1,0:T(8,128)(2,1)S(1)} %shard_map.85), channel_id=1, replica_groups=mesh['sec'=4,'op'=8] {'op'}, dimensions={0} | all-to-all | bytes 524288 | tf_op jit(solution)/shard_map/all_to_all | solution.py:193
  38.2 0.7 %convert_reduce_fusion = f32[2,32,256]{2,1,0:T(8,128)} fusion(bf16[8,2,32,256]{3,2,1,0:T(8,128)(2,1)S(1)} %all_to_all.10), kind=kLoop, calls=%fused_computation | loop fusion | flops 245760 | bytes 327680 | tf_op jit(solution)/shard_map/reduce_sum | solution.py:194
  (3 shorter events, 0.0 us)
Async XLA Ops:
  0.0 6.6 %copy-start = (bf16[2,32,256]{2,1,0:T(8,128)(2,1)S(1)}, bf16[2,32,256]{2,1,0:T(8,128)(2,1)}, u32[]{:S(2)}) copy-start(bf16[2,32,256]{2,1,0:T(8,128)(2,1)} %near_ref.1) | copy-start | bytes 98308
  0.0 6.6 %collective-permute-start = (bf16[2,32,256]{2,1,0:T(8,128)(2,1)}, bf16[2,32,256]{2,1,0:T(8,128)(2,1)S(1)}, u32[]{:S(2)}, u32[]{:S(2)}) collective-permute-start(bf16[2,32,256]{2,1,0:T(8,128)(2,1)} %near_ref.1), channel_id=1, source_target_pairs={{0,4},{1,5},{2,6},{3,7},{4,0},{5,1},{6,2},{7,3},{8,12},{9,13},{10,... | collective-permute-start | bytes 98312 | tf_op jit(solution)/shard_map/ppermute | solution.py:181
  4.1 0.7 %copy-start.1 = (s32[4,8,4,1]{1,3,2,0:T(1,128)S(1)}, s32[4,8,4,1]{1,3,2,0:T(1,128)}, u32[]{:S(2)}) copy-start(s32[4,8,4,1]{1,3,2,0:T(1,128)} %param.11) | copy-start | bytes 1540
  7.4 4.9 %copy-start.7 = (s32[64]{0:T(128)S(1)}, s32[64]{0:T(128)}, u32[]{:S(2)}) copy-start(s32[64]{0:T(128)} %param.15) | copy-start | bytes 772
  7.4 14.2 %all-to-all-start = ((bf16[16,2,1,32,256]{4,3,1,2,0:T(8,128)(2,1)}), bf16[16,2,1,32,256]{4,3,1,2,0:T(8,128)(2,1)S(1)}, u32[]{:S(2)}, u32[]{:S(2)}) async-start(bf16[16,2,1,32,256]{4,3,1,2,0:T(8,128)(2,1)} %bitcast.8), calls=%async_computation | async-start | bytes 1048576 | tf_op jit(solution)/shard_map/all_to_all | solution.py:187
  12.3 0.7 %copy-start.4 = (s32[64]{0:T(128)S(1)}, s32[64]{0:T(128)}, u32[]{:S(2)}) copy-start(s32[64]{0:T(128)} %param.12) | copy-start | bytes 772
  12.3 0.7 %copy-start.5 = (s32[64]{0:T(128)S(1)}, s32[64]{0:T(128)}, u32[]{:S(2)}) copy-start(s32[64]{0:T(128)} %param.13) | copy-start | bytes 772
  12.3 0.7 %copy-start.6 = (s32[64]{0:T(128)S(1)}, s32[64]{0:T(128)}, u32[]{:S(2)}) copy-start(s32[64]{0:T(128)} %param.14) | copy-start | bytes 772
  13.0 8.6 %copy-start.2 = (bf16[8,256,256]{2,1,0:T(8,128)(2,1)S(1)}, bf16[8,256,256]{2,1,0:T(8,128)(2,1)}, u32[]{:S(2)}) copy-start(bf16[8,256,256]{2,1,0:T(8,128)(2,1)} %left_ref.1) | copy-start | bytes 3145732
  13.0 8.6 %copy-start.3 = (bf16[8,256,256]{2,1,0:T(8,128)(2,1)S(1)}, bf16[8,256,256]{2,1,0:T(8,128)(2,1)}, u32[]{:S(2)}) copy-start(bf16[8,256,256]{2,1,0:T(8,128)(2,1)} %right_ref.1) | copy-start | bytes 3145732

commit v3 on v2

v3 whole, which is shorter than its diff:
```python
import functools

import jax
import jax.numpy as jnp
from jax import lax
from jax.experimental import pallas as pl
from jax.experimental.pallas import tpu as pltpu
from jax.sharding import PartitionSpec as P

CHUNK = 8
VMEM = pl.BlockSpec(memory_space=pltpu.VMEM)
SMEM = pl.BlockSpec(memory_space=pltpu.SMEM)
ANY = pl.BlockSpec(memory_space=pl.ANY)
NT = (((1,), (1,)), ((), ()))
BF16 = jnp.bfloat16


def choose_kernel(listed_ref, psi_ref, near_ref, choice_ref):
    held = psi_ref.shape[0]
    near_ref[...] = psi_ref[...]
    me, my_op = lax.axis_index("sec"), lax.axis_index("op")
    core = lax.rem(me, 2)
    for t in range(2):
        for y in range(choice_ref.shape[1]):
            source = 2 * y + core
            choice = listed_ref[source, jnp.bitwise_xor(me, t), 0, my_op] - source * held
            choice_ref[t, y] = jnp.full(choice_ref.shape[2:], choice.astype(jnp.float32)).astype(BF16)


def choose(send_list, psi):
    n_sec = send_list.shape[0]
    return pl.pallas_call(
        choose_kernel,
        out_shape=[
            jax.ShapeDtypeStruct(psi.shape, psi.dtype),
            jax.ShapeDtypeStruct((2, n_sec // 2) + psi.shape[1:], BF16),
        ],
        in_specs=[SMEM, VMEM],
        out_specs=[VMEM, VMEM],
        compiler_params=pltpu.CompilerParams(vmem_limit_bytes=4 * 1024 * 1024),
        cost_estimate=pl.CostEstimate(flops=10**6, bytes_accessed=10**6, transcendentals=0),
    )(send_list.transpose(0, 2, 3, 1), psi)


def weight_kernel(n_left, n_right, slot_hbm, out_id_hbm, left_id_hbm, right_id_hbm, weight_ref, ids_ref, sems):
    n_pair, n_cell = weight_ref.shape[1] // CHUNK, weight_ref.shape[0] // CHUNK
    copies = [pltpu.make_async_copy(x, ids_ref.at[i], sems.at[i])
              for i, x in enumerate((slot_hbm, out_id_hbm, left_id_hbm, right_id_hbm))]
    for copy in copies:
        copy.start()
    for copy in copies:
        copy.wait()

    cell = ids_ref[1] * n_right + ids_ref[3]
    slot = ids_ref[0]
    other = jnp.bitwise_xor(lax.rem(slot, 2), lax.rem(lax.axis_index("sec"), 2))
    pair = (other * (n_pair // (2 * n_left)) + lax.div(slot, 2)) * n_left + ids_ref[2]
    n_term = cell.shape[1]
    row_cell = lax.broadcasted_iota(jnp.int32, (n_cell * CHUNK, n_term), 0) // CHUNK
    row_pair = lax.broadcasted_iota(jnp.int32, (n_pair * CHUNK, n_term), 0) // CHUNK
    in_cell = jnp.where(row_cell == cell, 1.0, 0.0).astype(BF16)
    in_pair = jnp.where(row_pair == pair, 1.0, 0.0).astype(BF16)
    count = lax.dot_general(in_cell, in_pair, NT, preferred_element_type=jnp.float32)
    a = lax.broadcasted_iota(jnp.int32, count.shape, 0) % CHUNK
    b = lax.broadcasted_iota(jnp.int32, count.shape, 1) % CHUNK
    weight_ref[...] = jnp.where(a == b, count, 0.0).astype(BF16)


def weights(n_slot, n_left, n_right, held, term_slot, term_out, left_pick, right_pick):
    n_pair, n_cell = n_slot * n_left, held * n_right
    n_term = term_slot.shape[0]
    ids = [x.reshape(1, n_term) for x in (term_slot, term_out, left_pick, right_pick)]
    return pl.pallas_call(
        functools.partial(weight_kernel, n_left, n_right),
        out_shape=jax.ShapeDtypeStruct((n_cell * CHUNK, n_pair * CHUNK), BF16),
        in_specs=[ANY] * 4,
        out_specs=VMEM,
        scratch_shapes=[pltpu.VMEM((4, 1, n_term), jnp.int32), pltpu.SemaphoreType.DMA((4,))],
        compiler_params=pltpu.CompilerParams(vmem_limit_bytes=8 * 1024 * 1024),
        cost_estimate=pl.CostEstimate(flops=10**9, bytes_accessed=8 * 10**6, transcendentals=0),
    )(*ids)


def stack_kernel(*refs):
    for k, ref in enumerate(refs[:-1]):
        refs[-1][k] = ref[...]


def stack(blocks):
    return pl.pallas_call(
        stack_kernel,
        out_shape=jax.ShapeDtypeStruct((len(blocks),) + blocks[0].shape, blocks[0].dtype),
        in_specs=[VMEM] * len(blocks),
        out_specs=VMEM,
        compiler_params=pltpu.CompilerParams(vmem_limit_bytes=4 * 1024 * 1024),
        cost_estimate=pl.CostEstimate(flops=1, bytes_accessed=10**6, transcendentals=0),
    )(*blocks)


def split_kernel(n_lo, choice_ref, *refs):
    pieces, (keep_ref, give_ref) = refs[:-2], refs[-2:]
    n_hi, held = pieces[0].shape[:2]
    my_y = lax.div(lax.axis_index("sec"), 2)
    my_op = lax.axis_index("op")
    for q, piece in enumerate(pieces):
        y = jnp.bitwise_xor(my_y, q // n_lo)
        choices = [choice_ref[t, y] for t in range(2)]
        for k in range(n_hi):
            o = jnp.bitwise_xor(my_op, k * n_lo + q % n_lo)
            for choice, out_ref in zip(choices, (keep_ref, give_ref)):
                block = piece[k, 0]
                for i in range(1, held):
                    block = jnp.where(choice == i, piece[k, i], block)
                out_ref[y, o] = block


def split(choice, pieces, n_lo):
    n_hi, held, rows, width = pieces[0].shape
    out = jax.ShapeDtypeStruct((choice.shape[1], n_hi * n_lo, rows, width), BF16)
    return pl.pallas_call(
        functools.partial(split_kernel, n_lo),
        out_shape=[out, out],
        in_specs=[VMEM] * (1 + len(pieces)),
        out_specs=[VMEM] * 2,
        compiler_params=pltpu.CompilerParams(vmem_limit_bytes=8 * 1024 * 1024),
        cost_estimate=pl.CostEstimate(flops=10**6, bytes_accessed=2 * 10**6, transcendentals=0),
    )(choice, *pieces)


def halves(left_ref, table_ref, half_ref):
    n_left, width = left_ref.shape[0], left_ref.shape[1]
    for s in range(table_ref.shape[0]):
        for l in range(0, n_left, 2):
            two = [jnp.dot(left_ref[l + i], table_ref[s], preferred_element_type=jnp.float32) for i in range(2)]
            p = s * n_left + l
            for m in range(width // CHUNK):
                piece = jnp.concatenate([x[m * CHUNK:(m + 1) * CHUNK, :] for x in two], axis=0)
                half_ref[m, p * CHUNK:(p + 2) * CHUNK, :] = piece.astype(BF16)


def first_halves(table, left):
    n_slot, width, _ = table.shape
    n_left = left.shape[0]
    return pl.pallas_call(
        halves,
        out_shape=jax.ShapeDtypeStruct((width // CHUNK, n_slot * n_left * CHUNK, width), BF16),
        in_specs=[VMEM] * 2,
        out_specs=VMEM,
        compiler_params=pltpu.CompilerParams(vmem_limit_bytes=8 * 1024 * 1024),
        cost_estimate=pl.CostEstimate(flops=2 * n_slot * n_left * width**3, bytes_accessed=10**6, transcendentals=0),
    )(left, table)


def terms_kernel(split_rows, left_ref, right_ref, weight_ref, first_ref, table_ref, out_ref, half_ref, sum_ref):
    width, n_right = left_ref.shape[1], right_ref.shape[0]
    held = sum_ref.shape[0] // width
    chunks = width // CHUNK
    halves(left_ref, table_ref, half_ref)

    for m in range(0, chunks, 2):
        two = [jnp.dot(weight_ref[...], jnp.concatenate([first_ref[m + i], half_ref[m + i]], axis=0),
                       preferred_element_type=jnp.float32) for i in range(2)]
        for j in range(held):
            for r in range(n_right):
                p = j * n_right + r
                piece = jnp.concatenate([x[p * CHUNK:(p + 1) * CHUNK, :] for x in two], axis=0)
                sum_ref[j * width + m * CHUNK:j * width + (m + 2) * CHUNK, r * width:(r + 1) * width] = piece.astype(BF16)

    for j in range(held):
        acc = None
        for r in range(n_right):
            part = lax.dot_general(
                sum_ref[j * width:(j + 1) * width, r * width:(r + 1) * width], right_ref[r], NT,
                preferred_element_type=jnp.float32)
            acc = part if acc is None else acc + part
        acc = acc.astype(out_ref.dtype)
        if split_rows:
            n_op, rows = out_ref.shape[0], out_ref.shape[2]
            for o in range(n_op):
                out_ref[o, j] = acc[o * rows:(o + 1) * rows, :]
        else:
            out_ref[j] = acc


def terms(first, table, left, right, weight, held, n_op):
    n_slot, width, _ = table.shape
    n_left, n_right = left.shape[0], right.shape[0]
    rows = width // n_op
    split_rows = rows % 16 == 0
    shape = (n_op, held, rows, width) if split_rows else (held, width, width)
    n_pair, n_cell = n_slot * n_left, held * n_right
    blocks = n_pair + n_cell + n_left + n_right + n_slot + 4 * held
    out = pl.pallas_call(
        functools.partial(terms_kernel, split_rows),
        out_shape=jax.ShapeDtypeStruct(shape, BF16),
        in_specs=[VMEM] * 5,
        out_specs=VMEM,
        scratch_shapes=[
            pltpu.VMEM((width // CHUNK, n_pair * CHUNK, width), BF16),
            pltpu.VMEM((held * width, n_right * width), BF16),
        ],
        compiler_params=pltpu.CompilerParams(vmem_limit_bytes=2 * width * width * blocks + 12 * 1024 * 1024),
        cost_estimate=pl.CostEstimate(flops=3 * 10**9, bytes_accessed=4 * 10**6, transcendentals=0),
    )(left, right, weight, first, table)
    if not split_rows:
        out = out.reshape(held, n_op, rows, width).transpose(1, 0, 2, 3)
    return out


def shards(psi, left_ops, right_ops, send_list, term_slot, term_out, left_pick, right_pick):
    held, rows, width = psi.shape
    n_sec, n_op = send_list.shape[:2]
    n_lo = 2
    n_hi, n_y = n_op // n_lo, n_sec // 2

    def swap(x, sec_bits, op_bits):
        pairs = [(s * n_op + o, (s ^ sec_bits) * n_op + (o ^ op_bits)) for s in range(n_sec) for o in range(n_op)]
        return lax.ppermute(x, ("sec", "op"), pairs)

    near, choice = choose(send_list, psi)
    mine = stack([near] + [swap(psi, 0, k * n_lo) for k in range(1, n_hi)])
    pieces = [mine] + [swap(mine, 2 * (q // n_lo), q % n_lo) for q in range(1, n_y * n_lo)]
    weight = weights(n_sec, left_ops.shape[0], right_ops.shape[0], held, term_slot, term_out, left_pick, right_pick)
    choice, weight = lax.optimization_barrier((choice, weight))
    keep, give = (x.reshape(n_y, width, width) for x in split(choice, pieces, n_lo))
    got = swap(give, 1, 0)
    first = first_halves(keep, left_ops)
    partial_sum = terms(first, got, left_ops, right_ops, weight, held, n_op)
    parts = lax.all_to_all(partial_sum, "op", 0, 0, tiled=True)
    return jnp.sum(parts.astype(jnp.float32), axis=0)


def solution(mesh):
    in_specs = (
        P("sec", "op", None),
        P(("sec", "op"), None, None),
        P(("sec", "op"), None, None),
        P(),
        P(("sec", "op")),
        P(("sec", "op")),
        P(("sec", "op")),
        P(("sec", "op")),
    )
    out_specs = P("sec", "op", None)
    return jax.shard_map(shards, mesh=mesh, in_specs=in_specs, out_specs=out_specs, check_vma=False)
```

time: 39.1 us -> 36.2 us (0.926)
  waiting for transfers between devices: 9.4 us -> 5.53 us
  local copies, waits for them, and re-layouts: 1.37 us -> 4.12 us
  blocking collectives: 14.1 us -> 12.6 us
  Pallas kernels: 4.28 us -> 3.65 us
    all_to_all x1 -> x0, waiting for transfers between devices: 8.37 us -> none  [shards(): lax.all_to_all(packed, ('sec', 'op'), 0, 0, tiled=True, axis_index_groups...]
    ppermute x1 -> x7, starting transfers between devices: 4.04 us -> 9.24 us  [swap(): return lax.ppermute(x, ('sec', 'op'), pairs)]
    all_to_all x1 -> x0, starting transfers between devices: 4.88 us -> none  [shards(): lax.all_to_all(packed, ('sec', 'op'), 0, 0, tiled=True, axis_index_groups...]
    ppermute x1 -> x7, waiting for transfers between devices: 1.03 us -> 5.53 us  [swap(): return lax.ppermute(x, ('sec', 'op'), pairs)]
    unnamed x16, local copies, waits for them, and re-layouts: 1.37 us -> 4.12 us
    all_to_all x1, blocking collectives: 14.1 us -> 12.6 us  [shards(): parts = lax.all_to_all(partial_sum, 'op', 0, 0, tiled=True)]
    pallas_call x3 -> x5, Pallas kernels: 4.05 us -> 3.41 us  [the longest x1 1.94 us: terms(): pl.pallas_call(functools.partial(terms_kernel, split_rows), out_shape=jax...]
  transfers between devices with their start and end apart: 2 -> 7, of which waited for: 2 -> 5; matrix products, arithmetic and copies ran while one was open for 0% -> 0% of each run, Pallas kernels for 2% -> 5%
where the time goes in v3:
time: 36.2 us; the launch traced here: 35.9 us
  blocking collectives  12.6 us (35%)
  starting transfers between devices  9.24 us (26%)
  waiting for transfers between devices  5.53 us (15%)
  local copies, waits for them, and re-layouts  4.12 us (11%)
  Pallas kernels  3.65 us (10%)
  other arithmetic  0.67 us (2%)
    all_to_all x1, blocking collectives, shards(): parts = lax.all_to_all(partial_sum, 'op', 0, 0, tiled=True)  12.6 us
    ppermute x7, starting transfers between devices, swap(): return lax.ppermute(x, ('sec', 'op'), pairs)  9.24 us
    ppermute x7, waiting for transfers between devices, swap(): return lax.ppermute(x, ('sec', 'op'), pairs)  5.53 us
    unnamed x16, local copies, waits for them, and re-layouts  4.12 us
    pallas_call x1, Pallas kernels, terms(): pl.pallas_call(functools.partial(terms_kernel, split_rows), out_shape=jax...  1.94 us
  transfers between devices with their start and end apart: 7, of which 5 were waited for; matrix products, arithmetic and copies ran while one was open for 0% of the time, Pallas kernels for 5%

profile of v3, /device:TPU:0, one launch (start us, length us, event | category | flops | bytes accessed | tf_op | source)
XLA Modules:
  0.0 35.9 jit_solution(8532185593214783691)
XLA Ops:
  0.0 3.0 %collective-permute-start = (bf16[2,32,256]{2,1,0:T(8,128)(2,1)}, bf16[2,32,256]{2,1,0:T(8,128)(2,1)S(1)}, u32[]{:S(2)}, u32[]{:S(2)}) collective-permute-start(bf16[2,32,256]{2,1,0:T(8,128)(2,1)} %psi_ref.1), channel_id=1, source_target_pairs={{0,2},{1,3},{2,0},{3,1},{4,6},{5,7},{6,4},{7,5},{8,10},{9,11},{10,... | collective-permute-start | bytes 98312 | tf_op jit(solution)/shard_map/ppermute | solution.py:218
  3.0 2.5 %collective-permute-start.2 = (bf16[2,32,256]{2,1,0:T(8,128)(2,1)}, bf16[2,32,256]{2,1,0:T(8,128)(2,1)S(1)}, u32[]{:S(2)}, u32[]{:S(2)}) collective-permute-start(bf16[2,32,256]{2,1,0:T(8,128)(2,1)} %psi_ref.1), channel_id=1, source_target_pairs={{0,6},{1,7},{2,4},{3,5},{4,2},{5,3},{6,0},{7,1},{8,14},{9,15},{10,... | collective-permute-start | bytes 98312 | tf_op jit(solution)/shard_map/ppermute | solution.py:218
  5.5 0.1 collective-permute-start.1
  5.6 0.8 %copy-done.1 = bf16[2,32,256]{2,1,0:T(8,128)(2,1)S(1)} copy-done((bf16[2,32,256]{2,1,0:T(8,128)(2,1)S(1)}, bf16[2,32,256]{2,1,0:T(8,128)(2,1)}, u32[]{:S(2)}) %copy-start.1) | copy-done | bytes 32792
  6.4 0.7 %copy-done.2 = s32[4,8,4,1]{1,3,2,0:T(1,128)S(1)} copy-done((s32[4,8,4,1]{1,3,2,0:T(1,128)S(1)}, s32[4,8,4,1]{1,3,2,0:T(1,128)}, u32[]{:S(2)}) %copy-start.2) | copy-done | bytes 536
  7.1 0.7 %shard_map.82 = (bf16[2,32,256]{2,1,0:T(8,128)(2,1)S(1)}, bf16[2,2,32,256]{3,2,1,0:T(8,128)(2,1)S(1)}) custom-call(s32[4,4,1,8]{3,2,1,0:T(1,128)S(1)} %bitcast.8, bf16[2,32,256]{2,1,0:T(8,128)(2,1)S(1)} %copy-done.1), custom_call_target="tpu_custom_call" | custom-call | flops 1000000 | bytes 1000000 | tf_op jit(solution)/shard_map/pallas_call | solution.py:32
  7.8 1.6 %collective-permute-done.2.refs_3_ = bf16[2,32,256]{2,1,0:T(8,128)(2,1)S(1)} collective-permute-done((bf16[2,32,256]{2,1,0:T(8,128)(2,1)}, bf16[2,32,256]{2,1,0:T(8,128)(2,1)S(1)}, u32[]{:S(2)}, u32[]{:S(2)}) %collective-permute-start.2) | collective-permute-done | bytes 32800 | tf_op jit(solution)/shard_map/ppermute | solution.py:218
  9.4 1.5 %collective-permute-done.1.refs_2_ = bf16[2,32,256]{2,1,0:T(8,128)(2,1)S(1)} collective-permute-done((bf16[2,32,256]{2,1,0:T(8,128)(2,1)}, bf16[2,32,256]{2,1,0:T(8,128)(2,1)S(1)}, u32[]{:S(2)}, u32[]{:S(2)}) %collective-permute-start.1) | collective-permute-done | bytes 32800 | tf_op jit(solution)/shard_map/ppermute | solution.py:218
  10.9 2.5 %collective-permute-start.5 = (bf16[4,2,32,256]{3,2,1,0:T(8,128)(2,1)S(1)}, bf16[4,2,32,256]{3,2,1,0:T(8,128)(2,1)S(1)}, u32[]{:S(2)}, u32[]{:S(2)}) collective-permute-start(bf16[4,2,32,256]{3,2,1,0:T(8,128)(2,1)S(1)} %shard_map.84.refs_0_), channel_id=1, source_target_pairs={{0,17},{1,16},{2,19},{3,18},{4,21},{5,20},{6,23},{7,22},{8,25},{9,... | collective-permute-start | bytes 393224 | tf_op jit(solution)/shard_map/ppermute | solution.py:218
  13.4 0.5 %collective-permute-start.4 = (bf16[4,2,32,256]{3,2,1,0:T(8,128)(2,1)S(1)}, bf16[4,2,32,256]{3,2,1,0:T(8,128)(2,1)S(1)}, u32[]{:S(2)}, u32[]{:S(2)}) collective-permute-start(bf16[4,2,32,256]{3,2,1,0:T(8,128)(2,1)S(1)} %shard_map.84.refs_0_), channel_id=1, source_target_pairs={{0,16},{1,17},{2,18},{3,19},{4,20},{5,21},{6,22},{7,23},{8,24},{9,... | collective-permute-start | bytes 393224 | tf_op jit(solution)/shard_map/ppermute | solution.py:218
  13.9 0.5 %collective-permute-start.3 = (bf16[4,2,32,256]{3,2,1,0:T(8,128)(2,1)S(1)}, bf16[4,2,32,256]{3,2,1,0:T(8,128)(2,1)S(1)}, u32[]{:S(2)}, u32[]{:S(2)}) collective-permute-start(bf16[4,2,32,256]{3,2,1,0:T(8,128)(2,1)S(1)} %shard_map.84.refs_0_), channel_id=1, source_target_pairs={{0,1},{1,0},{2,3},{3,2},{4,5},{5,4},{6,7},{7,6},{8,9},{9,8},{10,11... | collective-permute-start | bytes 393224 | tf_op jit(solution)/shard_map/ppermute | solution.py:218
  14.4 0.7 %copy-done.4 = s32[64]{0:T(128)S(1)} copy-done((s32[64]{0:T(128)S(1)}, s32[64]{0:T(128)}, u32[]{:S(2)}) %copy-start.4) | copy-done | bytes 280
  15.1 0.7 %copy-done.5 = s32[64]{0:T(128)S(1)} copy-done((s32[64]{0:T(128)S(1)}, s32[64]{0:T(128)}, u32[]{:S(2)}) %copy-start.5) | copy-done | bytes 280
  15.8 0.7 %copy-done.6 = s32[64]{0:T(128)S(1)} copy-done((s32[64]{0:T(128)S(1)}, s32[64]{0:T(128)}, u32[]{:S(2)}) %copy-start.6) | copy-done | bytes 280
  16.4 0.7 %copy-done.7 = s32[64]{0:T(128)S(1)} copy-done((s32[64]{0:T(128)S(1)}, s32[64]{0:T(128)}, u32[]{:S(2)}) %copy-start.7) | copy-done | bytes 280
  17.1 0.2 shard_map.83.weight_ref
  17.3 0.9 %collective-permute-done.5.refs_3_ = bf16[4,2,32,256]{3,2,1,0:T(8,128)(2,1)S(1)} collective-permute-done((bf16[4,2,32,256]{3,2,1,0:T(8,128)(2,1)S(1)}, bf16[4,2,32,256]{3,2,1,0:T(8,128)(2,1)S(1)}, u32[]{:S(2)}, u32[]{:S(2)}) %collective-permute-start.5) | collective-permute-done | bytes 131104 | tf_op jit(solution)/shard_map/ppermute | solution.py:218
  18.2 0.8 %collective-permute-done.4.refs_2_ = bf16[4,2,32,256]{3,2,1,0:T(8,128)(2,1)S(1)} collective-permute-done((bf16[4,2,32,256]{3,2,1,0:T(8,128)(2,1)S(1)}, bf16[4,2,32,256]{3,2,1,0:T(8,128)(2,1)S(1)}, u32[]{:S(2)}, u32[]{:S(2)}) %collective-permute-start.4) | collective-permute-done | bytes 131104 | tf_op jit(solution)/shard_map/ppermute | solution.py:218
  19.1 0.1 collective-permute-start.6
  19.2 0.7 %shard_map.86.first_ref = bf16[32,128,256]{2,1,0:T(8,128)(2,1)S(1)} custom-call(bf16[8,256,256]{2,1,0:T(8,128)(2,1)S(1)} %copy-done, bf16[2,256,256]{2,1,0:T(8,128)(2,1)S(1)} %bitcast.7), custom_call_target="tpu_custom_call" | custom-call | flops 536870912 | bytes 1000000 | tf_op jit(solution)/shard_map/pallas_call | solution.py:144
  19.9 0.8 %collective-permute-done.6.table_ref = bf16[2,256,256]{2,1,0:T(8,128)(2,1)S(1)} collective-permute-done((bf16[2,256,256]{2,1,0:T(8,128)(2,1)S(1)}, bf16[2,256,256]{2,1,0:T(8,128)(2,1)S(1)}, u32[]{:S(2)}, u32[]{:S(2)}) %collective-permute-start.6) | collective-permute-done | bytes 262176 | tf_op jit(solution)/shard_map/ppermute | solution.py:218
  20.7 1.9 %shard_map.87 = bf16[8,2,32,256]{3,2,1,0:T(8,128)(2,1)S(1)} custom-call(bf16[8,256,256]{2,1,0:T(8,128)(2,1)S(1)} %copy-done, bf16[8,256,256]{2,1,0:T(8,128)(2,1)S(1)} %copy-done.3, bf16[128,256]{1,0:T(8,128)(2,1)S(1)} %shard_map.83.weight_ref, bf16[32,128,256]{2,1,0:T(8,128)(2,1)S(1)} %shard_map.86.first_ref, ...), custom_call_target="tpu_custom_call" | custom-call | flops 3000000000 | bytes 4000000 | tf_op jit(solution)/shard_map/pallas_call | solution.py:193
  22.6 12.6 %all_to_all.5 = bf16[8,2,32,256]{3,2,1,0:T(8,128)(2,1)S(1)} all-to-all(bf16[8,2,32,256]{3,2,1,0:T(8,128)(2,1)S(1)} %shard_map.87), channel_id=1, replica_groups=mesh['sec'=4,'op'=8] {'op'}, dimensions={0} | all-to-all | bytes 524288 | tf_op jit(solution)/shard_map/all_to_all | solution.py:229
  35.3 0.7 %convert_reduce_fusion = f32[2,32,256]{2,1,0:T(8,128)} fusion(bf16[8,2,32,256]{3,2,1,0:T(8,128)(2,1)S(1)} %all_to_all.5), kind=kLoop, calls=%fused_computation | loop fusion | flops 245760 | bytes 327680 | tf_op jit(solution)/shard_map/reduce_sum | solution.py:230
  (14 shorter events, 0.1 us)
Async XLA Ops:
  0.0 7.8 %collective-permute-start = (bf16[2,32,256]{2,1,0:T(8,128)(2,1)}, bf16[2,32,256]{2,1,0:T(8,128)(2,1)S(1)}, u32[]{:S(2)}, u32[]{:S(2)}) collective-permute-start(bf16[2,32,256]{2,1,0:T(8,128)(2,1)} %psi_ref.1), channel_id=1, source_target_pairs={{0,2},{1,3},{2,0},{3,1},{4,6},{5,7},{6,4},{7,5},{8,10},{9,11},{10,... | collective-permute-start | bytes 98312 | tf_op jit(solution)/shard_map/ppermute | solution.py:218
  3.0 6.4 %collective-permute-start.2 = (bf16[2,32,256]{2,1,0:T(8,128)(2,1)}, bf16[2,32,256]{2,1,0:T(8,128)(2,1)S(1)}, u32[]{:S(2)}, u32[]{:S(2)}) collective-permute-start(bf16[2,32,256]{2,1,0:T(8,128)(2,1)} %psi_ref.1), channel_id=1, source_target_pairs={{0,6},{1,7},{2,4},{3,5},{4,2},{5,3},{6,0},{7,1},{8,14},{9,15},{10,... | collective-permute-start | bytes 98312 | tf_op jit(solution)/shard_map/ppermute | solution.py:218
  5.5 5.4 %collective-permute-start.1 = (bf16[2,32,256]{2,1,0:T(8,128)(2,1)}, bf16[2,32,256]{2,1,0:T(8,128)(2,1)S(1)}, u32[]{:S(2)}, u32[]{:S(2)}) collective-permute-start(bf16[2,32,256]{2,1,0:T(8,128)(2,1)} %psi_ref.1), channel_id=1, source_target_pairs={{0,4},{1,5},{2,6},{3,7},{4,0},{5,1},{6,2},{7,3},{8,12},{9,13},{10,... | collective-permute-start | bytes 98312 | tf_op jit(solution)/shard_map/ppermute | solution.py:218
  5.6 0.8 %copy-start.1 = (bf16[2,32,256]{2,1,0:T(8,128)(2,1)S(1)}, bf16[2,32,256]{2,1,0:T(8,128)(2,1)}, u32[]{:S(2)}) copy-start(bf16[2,32,256]{2,1,0:T(8,128)(2,1)} %psi_ref.1) | copy-start | bytes 98308
  6.4 0.7 %copy-start.2 = (s32[4,8,4,1]{1,3,2,0:T(1,128)S(1)}, s32[4,8,4,1]{1,3,2,0:T(1,128)}, u32[]{:S(2)}) copy-start(s32[4,8,4,1]{1,3,2,0:T(1,128)} %param.11) | copy-start | bytes 1540
  10.9 7.3 %collective-permute-start.5 = (bf16[4,2,32,256]{3,2,1,0:T(8,128)(2,1)S(1)}, bf16[4,2,32,256]{3,2,1,0:T(8,128)(2,1)S(1)}, u32[]{:S(2)}, u32[]{:S(2)}) collective-permute-start(bf16[4,2,32,256]{3,2,1,0:T(8,128)(2,1)S(1)} %shard_map.84.refs_0_), channel_id=1, source_target_pairs={{0,17},{1,16},{2,19},{3,18},{4,21},{5,20},{6,23},{7,22},{8,25},{9,... | collective-permute-start | bytes 393224 | tf_op jit(solution)/shard_map/ppermute | solution.py:218
  13.4 5.6 %collective-permute-start.4 = (bf16[4,2,32,256]{3,2,1,0:T(8,128)(2,1)S(1)}, bf16[4,2,32,256]{3,2,1,0:T(8,128)(2,1)S(1)}, u32[]{:S(2)}, u32[]{:S(2)}) collective-permute-start(bf16[4,2,32,256]{3,2,1,0:T(8,128)(2,1)S(1)} %shard_map.84.refs_0_), channel_id=1, source_target_pairs={{0,16},{1,17},{2,18},{3,19},{4,20},{5,21},{6,22},{7,23},{8,24},{9,... | collective-permute-start | bytes 393224 | tf_op jit(solution)/shard_map/ppermute | solution.py:218
  13.9 5.1 %collective-permute-start.3 = (bf16[4,2,32,256]{3,2,1,0:T(8,128)(2,1)S(1)}, bf16[4,2,32,256]{3,2,1,0:T(8,128)(2,1)S(1)}, u32[]{:S(2)}, u32[]{:S(2)}) collective-permute-start(bf16[4,2,32,256]{3,2,1,0:T(8,128)(2,1)S(1)} %shard_map.84.refs_0_), channel_id=1, source_target_pairs={{0,1},{1,0},{2,3},{3,2},{4,5},{5,4},{6,7},{7,6},{8,9},{9,8},{10,11... | collective-permute-start | bytes 393224 | tf_op jit(solution)/shard_map/ppermute | solution.py:218
  14.4 0.7 %copy-start.4 = (s32[64]{0:T(128)S(1)}, s32[64]{0:T(128)}, u32[]{:S(2)}) copy-start(s32[64]{0:T(128)} %param.12) | copy-start | bytes 772
  15.1 0.7 %copy-start.5 = (s32[64]{0:T(128)S(1)}, s32[64]{0:T(128)}, u32[]{:S(2)}) copy-start(s32[64]{0:T(128)} %param.13) | copy-start | bytes 772
  15.8 0.7 %copy-start.6 = (s32[64]{0:T(128)S(1)}, s32[64]{0:T(128)}, u32[]{:S(2)}) copy-start(s32[64]{0:T(128)} %param.14) | copy-start | bytes 772
  16.4 0.7 %copy-start.7 = (s32[64]{0:T(128)S(1)}, s32[64]{0:T(128)}, u32[]{:S(2)}) copy-start(s32[64]{0:T(128)} %param.15) | copy-start | bytes 772
  17.1 2.1 %copy-start = (bf16[8,256,256]{2,1,0:T(8,128)(2,1)S(1)}, bf16[8,256,256]{2,1,0:T(8,128)(2,1)}, u32[]{:S(2)}) copy-start(bf16[8,256,256]{2,1,0:T(8,128)(2,1)} %left_ref.3) | copy-start | bytes 3145732
  17.3 3.4 %copy-start.3 = (bf16[8,256,256]{2,1,0:T(8,128)(2,1)S(1)}, bf16[8,256,256]{2,1,0:T(8,128)(2,1)}, u32[]{:S(2)}) copy-start(bf16[8,256,256]{2,1,0:T(8,128)(2,1)} %right_ref.1) | copy-start | bytes 3145732
  19.1 1.6 %collective-permute-start.6 = (bf16[2,256,256]{2,1,0:T(8,128)(2,1)S(1)}, bf16[2,256,256]{2,1,0:T(8,128)(2,1)S(1)}, u32[]{:S(2)}, u32[]{:S(2)}) collective-permute-start(bf16[2,256,256]{2,1,0:T(8,128)(2,1)S(1)} %bitcast.9), channel_id=1, source_target_pairs={{0,8},{1,9},{2,10},{3,11},{4,12},{5,13},{6,14},{7,15},{8,0},{9,1},... | collective-permute-start | bytes 786440 | tf_op jit(solution)/shard_map/ppermute | solution.py:218

commit v4 on v3

--- a/solution.py
+++ b/solution.py
@@ -15,9 +15,26 @@
 BF16 = jnp.bfloat16
 
 
-def choose_kernel(listed_ref, psi_ref, near_ref, choice_ref):
-    held = psi_ref.shape[0]
-    near_ref[...] = psi_ref[...]
+def fetch_kernel(from_ref, to_ref, sem):
+    copy = pltpu.make_async_copy(from_ref, to_ref, sem)
+    copy.start()
+    copy.wait()
+
+
+def fetch(x):
+    return pl.pallas_call(
+        fetch_kernel,
+        out_shape=jax.ShapeDtypeStruct(x.shape, x.dtype),
+        in_specs=[ANY],
+        out_specs=VMEM,
+        scratch_shapes=[pltpu.SemaphoreType.DMA],
+        compiler_params=pltpu.CompilerParams(vmem_limit_bytes=4 * 1024 * 1024),
+        cost_estimate=pl.CostEstimate(flops=1, bytes_accessed=10**6, transcendentals=0),
+    )(x)
+
+
+def prepare_kernel(n_left, n_right, held, listed_ref, code_ref, choice_ref, weight_ref):
+    n_pair, n_cell = weight_ref.shape[1] // CHUNK, weight_ref.shape[0] // CHUNK
     me, my_op = lax.axis_index("sec"), lax.axis_index("op")
     core = lax.rem(me, 2)
     for t in range(2):
@@ -26,35 +43,11 @@
             choice = listed_ref[source, jnp.bitwise_xor(me, t), 0, my_op] - source * held
             choice_ref[t, y] = jnp.full(choice_ref.shape[2:], choice.astype(jnp.float32)).astype(BF16)
 
-
-def choose(send_list, psi):
-    n_sec = send_list.shape[0]
-    return pl.pallas_call(
-        choose_kernel,
-        out_shape=[
-            jax.ShapeDtypeStruct(psi.shape, psi.dtype),
-            jax.ShapeDtypeStruct((2, n_sec // 2) + psi.shape[1:], BF16),
-        ],
-        in_specs=[SMEM, VMEM],
-        out_specs=[VMEM, VMEM],
-        compiler_params=pltpu.CompilerParams(vmem_limit_bytes=4 * 1024 * 1024),
-        cost_estimate=pl.CostEstimate(flops=10**6, bytes_accessed=10**6, transcendentals=0),
-    )(send_list.transpose(0, 2, 3, 1), psi)
-
-
-def weight_kernel(n_left, n_right, slot_hbm, out_id_hbm, left_id_hbm, right_id_hbm, weight_ref, ids_ref, sems):
-    n_pair, n_cell = weight_ref.shape[1] // CHUNK, weight_ref.shape[0] // CHUNK
-    copies = [pltpu.make_async_copy(x, ids_ref.at[i], sems.at[i])
-              for i, x in enumerate((slot_hbm, out_id_hbm, left_id_hbm, right_id_hbm))]
-    for copy in copies:
-        copy.start()
-    for copy in copies:
-        copy.wait()
-
-    cell = ids_ref[1] * n_right + ids_ref[3]
-    slot = ids_ref[0]
-    other = jnp.bitwise_xor(lax.rem(slot, 2), lax.rem(lax.axis_index("sec"), 2))
-    pair = (other * (n_pair // (2 * n_left)) + lax.div(slot, 2)) * n_left + ids_ref[2]
+    code = code_ref[...]
+    cell, code = lax.rem(code, n_cell), lax.div(code, n_cell)
+    left, slot = lax.rem(code, n_left), lax.div(code, n_left)
+    other = jnp.bitwise_xor(lax.rem(slot, 2), core)
+    pair = (other * (n_pair // (2 * n_left)) + lax.div(slot, 2)) * n_left + left
     n_term = cell.shape[1]
     row_cell = lax.broadcasted_iota(jnp.int32, (n_cell * CHUNK, n_term), 0) // CHUNK
     row_pair = lax.broadcasted_iota(jnp.int32, (n_pair * CHUNK, n_term), 0) // CHUNK
@@ -66,35 +59,39 @@
     weight_ref[...] = jnp.where(a == b, count, 0.0).astype(BF16)
 
 
-def weights(n_slot, n_left, n_right, held, term_slot, term_out, left_pick, right_pick):
-    n_pair, n_cell = n_slot * n_left, held * n_right
+def prepare(send_list, term_slot, term_out, left_pick, right_pick, held, rows, width, n_left, n_right):
+    n_sec = send_list.shape[0]
+    n_pair, n_cell = n_sec * n_left, held * n_right
     n_term = term_slot.shape[0]
-    ids = [x.reshape(1, n_term) for x in (term_slot, term_out, left_pick, right_pick)]
-    return pl.pallas_call(
-        functools.partial(weight_kernel, n_left, n_right),
-        out_shape=jax.ShapeDtypeStruct((n_cell * CHUNK, n_pair * CHUNK), BF16),
-        in_specs=[ANY] * 4,
-        out_specs=VMEM,
-        scratch_shapes=[pltpu.VMEM((4, 1, n_term), jnp.int32), pltpu.SemaphoreType.DMA((4,))],
+    code = ((term_slot * n_left + left_pick) * held + term_out) * n_right + right_pick
+    return pl.pallas_call(
+        functools.partial(prepare_kernel, n_left, n_right, held),
+        out_shape=[
+            jax.ShapeDtypeStruct((2, n_sec // 2, rows, width), BF16),
+            jax.ShapeDtypeStruct((n_cell * CHUNK, n_pair * CHUNK), BF16),
+        ],
+        in_specs=[SMEM, VMEM],
+        out_specs=[VMEM] * 2,
         compiler_params=pltpu.CompilerParams(vmem_limit_bytes=8 * 1024 * 1024),
-        cost_estimate=pl.CostEstimate(flops=10**9, bytes_accessed=8 * 10**6, transcendentals=0),
-    )(*ids)
-
-
-def stack_kernel(*refs):
-    for k, ref in enumerate(refs[:-1]):
+        cost_estimate=pl.CostEstimate(flops=10**9, bytes_accessed=4 * 10**6, transcendentals=0),
+    )(send_list.transpose(0, 2, 3, 1), code.reshape(1, n_term))
+
+
+def stack_kernel(order, *refs):
+    for k, ref in zip(order, refs[:-1]):
         refs[-1][k] = ref[...]
 
 
 def stack(blocks):
-    return pl.pallas_call(
-        stack_kernel,
-        out_shape=jax.ShapeDtypeStruct((len(blocks),) + blocks[0].shape, blocks[0].dtype),
+    first = next(iter(blocks.values()))
+    return pl.pallas_call(
+        functools.partial(stack_kernel, tuple(blocks)),
+        out_shape=jax.ShapeDtypeStruct((len(blocks),) + first.shape, first.dtype),
         in_specs=[VMEM] * len(blocks),
         out_specs=VMEM,
         compiler_params=pltpu.CompilerParams(vmem_limit_bytes=4 * 1024 * 1024),
         cost_estimate=pl.CostEstimate(flops=1, bytes_accessed=10**6, transcendentals=0),
-    )(*blocks)
+    )(*blocks.values())
 
 
 def split_kernel(n_lo, choice_ref, *refs):
@@ -217,11 +214,11 @@
         pairs = [(s * n_op + o, (s ^ sec_bits) * n_op + (o ^ op_bits)) for s in range(n_sec) for o in range(n_op)]
         return lax.ppermute(x, ("sec", "op"), pairs)
 
-    near, choice = choose(send_list, psi)
-    mine = stack([near] + [swap(psi, 0, k * n_lo) for k in range(1, n_hi)])
+    near = fetch(psi)
+    mine = stack({0: near} | {k: swap(psi, 0, k * n_lo) for k in [n_hi - 1, *range(1, n_hi - 1)]})
     pieces = [mine] + [swap(mine, 2 * (q // n_lo), q % n_lo) for q in range(1, n_y * n_lo)]
-    weight = weights(n_sec, left_ops.shape[0], right_ops.shape[0], held, term_slot, term_out, left_pick, right_pick)
-    choice, weight = lax.optimization_barrier((choice, weight))
+    choice, weight = prepare(
+        send_list, term_slot, term_out, left_pick, right_pick, held, rows, width, left_ops.shape[0], right_ops.shape[0])
     keep, give = (x.reshape(n_y, width, width) for x in split(choice, pieces, n_lo))
     got = swap(give, 1, 0)
     first = first_halves(keep, left_ops)

time: 36.2 us -> 35.6 us (0.983)
  local copies, waits for them, and re-layouts: 4.12 us -> 1.5 us
  waiting for transfers between devices: 5.53 us -> 6.71 us
  other arithmetic: 0.67 us -> 1.38 us
    unnamed x16 -> x8, local copies, waits for them, and re-layouts: 4.12 us -> 1.5 us
    ppermute x7, waiting for transfers between devices: 5.53 us -> 6.71 us  [swap(): return lax.ppermute(x, ('sec', 'op'), pairs)]
    reshape x0 -> x1, other arithmetic: none -> 0.71 us  [prepare(): code.reshape(1, n_term)]
  transfers between devices with their start and end apart: 7 -> 7, of which waited for: 5 -> 5; matrix products, arithmetic and copies ran while one was open for 0% -> 2% of each run, Pallas kernels for 5% -> 4%
where the time goes in v4:
time: 35.6 us; the launch traced here: 35.4 us
  blocking collectives  12.9 us (36%)
  starting transfers between devices  9.24 us (26%)
  waiting for transfers between devices  6.71 us (19%)
  Pallas kernels  3.6 us (10%)
  local copies, waits for them, and re-layouts  1.5 us (4%)
  other arithmetic  1.38 us (4%)
    all_to_all x1, blocking collectives, shards(): parts = lax.all_to_all(partial_sum, 'op', 0, 0, tiled=True)  12.9 us
    ppermute x7, starting transfers between devices, swap(): return lax.ppermute(x, ('sec', 'op'), pairs)  9.24 us
    ppermute x7, waiting for transfers between devices, swap(): return lax.ppermute(x, ('sec', 'op'), pairs)  6.71 us
    pallas_call x1, Pallas kernels, terms(): pl.pallas_call(functools.partial(terms_kernel, split_rows), out_shape=jax...  1.94 us
    unnamed x8, local copies, waits for them, and re-layouts  1.5 us
    pallas_call x1, Pallas kernels, prepare(): pl.pallas_call(functools.partial(prepare_kernel, n_left, n_right, held),...  0.85 us
  transfers between devices with their start and end apart: 7, of which 5 were waited for; matrix products, arithmetic and copies ran while one was open for 2% of the time, Pallas kernels for 4%

profile of v4, /device:TPU:0, one launch (start us, length us, event | category | flops | bytes accessed | tf_op | source)
XLA Modules:
  0.0 35.4 jit_solution(10605106659017356537)
XLA Ops:
  0.0 5.0 %collective-permute-start = (bf16[2,32,256]{2,1,0:T(8,128)(2,1)}, bf16[2,32,256]{2,1,0:T(8,128)(2,1)S(1)}, u32[]{:S(2)}, u32[]{:S(2)}) collective-permute-start(bf16[2,32,256]{2,1,0:T(8,128)(2,1)} %from_ref.1), channel_id=1, source_target_pairs={{0,6},{1,7},{2,4},{3,5},{4,2},{5,3},{6,0},{7,1},{8,14},{9,15},{10,... | collective-permute-start | bytes 98312 | tf_op jit(solution)/shard_map/ppermute | solution.py:215
  5.0 0.0 collective-permute-start.2
  5.1 0.6 %collective-permute-start.1 = (bf16[2,32,256]{2,1,0:T(8,128)(2,1)}, bf16[2,32,256]{2,1,0:T(8,128)(2,1)S(1)}, u32[]{:S(2)}, u32[]{:S(2)}) collective-permute-start(bf16[2,32,256]{2,1,0:T(8,128)(2,1)} %from_ref.1), channel_id=1, source_target_pairs={{0,2},{1,3},{2,0},{3,1},{4,6},{5,7},{6,4},{7,5},{8,10},{9,11},{10,... | collective-permute-start | bytes 98312 | tf_op jit(solution)/shard_map/ppermute | solution.py:215
  5.6 0.8 %copy-done.1 = bf16[2,32,256]{2,1,0:T(8,128)(2,1)S(1)} copy-done((bf16[2,32,256]{2,1,0:T(8,128)(2,1)S(1)}, bf16[2,32,256]{2,1,0:T(8,128)(2,1)}, u32[]{:S(2)}) %copy-start.1) | copy-done | bytes 32792
  6.4 0.7 %collective-permute-done.refs_1_ = bf16[2,32,256]{2,1,0:T(8,128)(2,1)S(1)} collective-permute-done((bf16[2,32,256]{2,1,0:T(8,128)(2,1)}, bf16[2,32,256]{2,1,0:T(8,128)(2,1)S(1)}, u32[]{:S(2)}, u32[]{:S(2)}) %collective-permute-start) | collective-permute-done | bytes 32800 | tf_op jit(solution)/shard_map/ppermute | solution.py:215
  7.2 2.9 %collective-permute-done.2.refs_3_ = bf16[2,32,256]{2,1,0:T(8,128)(2,1)S(1)} collective-permute-done((bf16[2,32,256]{2,1,0:T(8,128)(2,1)}, bf16[2,32,256]{2,1,0:T(8,128)(2,1)S(1)}, u32[]{:S(2)}, u32[]{:S(2)}) %collective-permute-start.2) | collective-permute-done | bytes 32800 | tf_op jit(solution)/shard_map/ppermute | solution.py:215
  10.1 0.0 collective-permute-done.1.refs_2_
  10.1 2.5 %collective-permute-start.5 = (bf16[4,2,32,256]{3,2,1,0:T(8,128)(2,1)S(1)}, bf16[4,2,32,256]{3,2,1,0:T(8,128)(2,1)S(1)}, u32[]{:S(2)}, u32[]{:S(2)}) collective-permute-start(bf16[4,2,32,256]{3,2,1,0:T(8,128)(2,1)S(1)} %shard_map.84.refs_0_), channel_id=1, source_target_pairs={{0,17},{1,16},{2,19},{3,18},{4,21},{5,20},{6,23},{7,22},{8,25},{9,... | collective-permute-start | bytes 393224 | tf_op jit(solution)/shard_map/ppermute | solution.py:215
  12.6 0.5 %collective-permute-start.4 = (bf16[4,2,32,256]{3,2,1,0:T(8,128)(2,1)S(1)}, bf16[4,2,32,256]{3,2,1,0:T(8,128)(2,1)S(1)}, u32[]{:S(2)}, u32[]{:S(2)}) collective-permute-start(bf16[4,2,32,256]{3,2,1,0:T(8,128)(2,1)S(1)} %shard_map.84.refs_0_), channel_id=1, source_target_pairs={{0,16},{1,17},{2,18},{3,19},{4,20},{5,21},{6,22},{7,23},{8,24},{9,... | collective-permute-start | bytes 393224 | tf_op jit(solution)/shard_map/ppermute | solution.py:215
  13.1 0.5 %collective-permute-start.3 = (bf16[4,2,32,256]{3,2,1,0:T(8,128)(2,1)S(1)}, bf16[4,2,32,256]{3,2,1,0:T(8,128)(2,1)S(1)}, u32[]{:S(2)}, u32[]{:S(2)}) collective-permute-start(bf16[4,2,32,256]{3,2,1,0:T(8,128)(2,1)S(1)} %shard_map.84.refs_0_), channel_id=1, source_target_pairs={{0,1},{1,0},{2,3},{3,2},{4,5},{5,4},{6,7},{7,6},{8,9},{9,8},{10,11... | collective-permute-start | bytes 393224 | tf_op jit(solution)/shard_map/ppermute | solution.py:215
  13.6 0.7 %add_bitcast_fusion.code_ref = s32[1,64]{1,0:T(1,128)S(1)} fusion(s32[64]{0:T(128)} %param.15, s32[64]{0:T(128)} %param.13, s32[64]{0:T(128)} %param.14, s32[64]{0:T(128)} %param.12), kind=kLoop, calls=%fused_computation.1 | loop fusion | flops 384 | bytes 1280 | tf_op jit(solution)/shard_map/reshape | solution.py:77
  14.4 0.7 %copy-done.3 = s32[4,8,4,1]{1,3,2,0:T(1,128)S(1)} copy-done((s32[4,8,4,1]{1,3,2,0:T(1,128)S(1)}, s32[4,8,4,1]{1,3,2,0:T(1,128)}, u32[]{:S(2)}) %copy-start.3) | copy-done | bytes 536
  15.1 0.9 %shard_map.82 = (bf16[2,2,32,256]{3,2,1,0:T(8,128)(2,1)S(1)}, bf16[128,256]{1,0:T(8,128)(2,1)S(1)}) custom-call(s32[4,4,1,8]{3,2,1,0:T(1,128)S(1)} %bitcast.7, s32[1,64]{1,0:T(1,128)S(1)} %add_bitcast_fusion.code_ref), custom_call_target="tpu_custom_call" | custom-call | flops 1000000000 | bytes 4000000 | tf_op jit(solution)/shard_map/pallas_call | solution.py:67
  15.9 0.0 copy-start.2
  15.9 1.5 %collective-permute-done.5.refs_3_ = bf16[4,2,32,256]{3,2,1,0:T(8,128)(2,1)S(1)} collective-permute-done((bf16[4,2,32,256]{3,2,1,0:T(8,128)(2,1)S(1)}, bf16[4,2,32,256]{3,2,1,0:T(8,128)(2,1)S(1)}, u32[]{:S(2)}, u32[]{:S(2)}) %collective-permute-start.5) | collective-permute-done | bytes 131104 | tf_op jit(solution)/shard_map/ppermute | solution.py:215
  17.4 0.8 %collective-permute-done.4.refs_2_ = bf16[4,2,32,256]{3,2,1,0:T(8,128)(2,1)S(1)} collective-permute-done((bf16[4,2,32,256]{3,2,1,0:T(8,128)(2,1)S(1)}, bf16[4,2,32,256]{3,2,1,0:T(8,128)(2,1)S(1)}, u32[]{:S(2)}, u32[]{:S(2)}) %collective-permute-start.4) | collective-permute-done | bytes 131104 | tf_op jit(solution)/shard_map/ppermute | solution.py:215
  18.2 0.0 collective-permute-done.3.refs_1_
  18.2 0.1 shard_map.85
  18.3 0.1 collective-permute-start.6
  18.4 0.7 %shard_map.86.first_ref = bf16[32,128,256]{2,1,0:T(8,128)(2,1)S(1)} custom-call(bf16[8,256,256]{2,1,0:T(8,128)(2,1)S(1)} %copy-done, bf16[2,256,256]{2,1,0:T(8,128)(2,1)S(1)} %bitcast.5), custom_call_target="tpu_custom_call" | custom-call | flops 536870912 | bytes 1000000 | tf_op jit(solution)/shard_map/pallas_call | solution.py:141
  19.1 0.8 %collective-permute-done.6.table_ref = bf16[2,256,256]{2,1,0:T(8,128)(2,1)S(1)} collective-permute-done((bf16[2,256,256]{2,1,0:T(8,128)(2,1)S(1)}, bf16[2,256,256]{2,1,0:T(8,128)(2,1)S(1)}, u32[]{:S(2)}, u32[]{:S(2)}) %collective-permute-start.6) | collective-permute-done | bytes 262176 | tf_op jit(solution)/shard_map/ppermute | solution.py:215
  19.9 1.9 %shard_map.87 = bf16[8,2,32,256]{3,2,1,0:T(8,128)(2,1)S(1)} custom-call(bf16[8,256,256]{2,1,0:T(8,128)(2,1)S(1)} %copy-done, bf16[8,256,256]{2,1,0:T(8,128)(2,1)S(1)} %copy-done.2, bf16[128,256]{1,0:T(8,128)(2,1)S(1)} %get-tuple-element.9.weight_ref, bf16[32,128,256]{2,1,0:T(8,128)(2,1)S(1)} %shard_map.86.first_ref, ...), custom_call_target="tpu_custom_call" | custom-call | flops 3000000000 | bytes 4000000 | tf_op jit(solution)/shard_map/pallas_call | solution.py:190
  21.8 12.9 %all_to_all.5 = bf16[8,2,32,256]{3,2,1,0:T(8,128)(2,1)S(1)} all-to-all(bf16[8,2,32,256]{3,2,1,0:T(8,128)(2,1)S(1)} %shard_map.87), channel_id=1, replica_groups=mesh['sec'=4,'op'=8] {'op'}, dimensions={0} | all-to-all | bytes 524288 | tf_op jit(solution)/shard_map/all_to_all | solution.py:226
  34.7 0.7 %convert_reduce_fusion = f32[2,32,256]{2,1,0:T(8,128)} fusion(bf16[8,2,32,256]{3,2,1,0:T(8,128)(2,1)S(1)} %all_to_all.5), kind=kLoop, calls=%fused_computation | loop fusion | flops 245760 | bytes 327680 | tf_op jit(solution)/shard_map/reduce_sum | solution.py:227
  (7 shorter events, 0.0 us)
Async XLA Ops:
  0.0 7.2 %collective-permute-start = (bf16[2,32,256]{2,1,0:T(8,128)(2,1)}, bf16[2,32,256]{2,1,0:T(8,128)(2,1)S(1)}, u32[]{:S(2)}, u32[]{:S(2)}) collective-permute-start(bf16[2,32,256]{2,1,0:T(8,128)(2,1)} %from_ref.1), channel_id=1, source_target_pairs={{0,6},{1,7},{2,4},{3,5},{4,2},{5,3},{6,0},{7,1},{8,14},{9,15},{10,... | collective-permute-start | bytes 98312 | tf_op jit(solution)/shard_map/ppermute | solution.py:215
  5.0 5.0 %collective-permute-start.2 = (bf16[2,32,256]{2,1,0:T(8,128)(2,1)}, bf16[2,32,256]{2,1,0:T(8,128)(2,1)S(1)}, u32[]{:S(2)}, u32[]{:S(2)}) collective-permute-start(bf16[2,32,256]{2,1,0:T(8,128)(2,1)} %from_ref.1), channel_id=1, source_target_pairs={{0,4},{1,5},{2,6},{3,7},{4,0},{5,1},{6,2},{7,3},{8,12},{9,13},{10,... | collective-permute-start | bytes 98312 | tf_op jit(solution)/shard_map/ppermute | solution.py:215
  5.1 5.0 %collective-permute-start.1 = (bf16[2,32,256]{2,1,0:T(8,128)(2,1)}, bf16[2,32,256]{2,1,0:T(8,128)(2,1)S(1)}, u32[]{:S(2)}, u32[]{:S(2)}) collective-permute-start(bf16[2,32,256]{2,1,0:T(8,128)(2,1)} %from_ref.1), channel_id=1, source_target_pairs={{0,2},{1,3},{2,0},{3,1},{4,6},{5,7},{6,4},{7,5},{8,10},{9,11},{10,... | collective-permute-start | bytes 98312 | tf_op jit(solution)/shard_map/ppermute | solution.py:215
  5.6 0.8 %copy-start.1 = (bf16[2,32,256]{2,1,0:T(8,128)(2,1)S(1)}, bf16[2,32,256]{2,1,0:T(8,128)(2,1)}, u32[]{:S(2)}) copy-start(bf16[2,32,256]{2,1,0:T(8,128)(2,1)} %from_ref.1) | copy-start | bytes 98308
  10.1 7.3 %collective-permute-start.5 = (bf16[4,2,32,256]{3,2,1,0:T(8,128)(2,1)S(1)}, bf16[4,2,32,256]{3,2,1,0:T(8,128)(2,1)S(1)}, u32[]{:S(2)}, u32[]{:S(2)}) collective-permute-start(bf16[4,2,32,256]{3,2,1,0:T(8,128)(2,1)S(1)} %shard_map.84.refs_0_), channel_id=1, source_target_pairs={{0,17},{1,16},{2,19},{3,18},{4,21},{5,20},{6,23},{7,22},{8,25},{9,... | collective-permute-start | bytes 393224 | tf_op jit(solution)/shard_map/ppermute | solution.py:215
  12.6 5.6 %collective-permute-start.4 = (bf16[4,2,32,256]{3,2,1,0:T(8,128)(2,1)S(1)}, bf16[4,2,32,256]{3,2,1,0:T(8,128)(2,1)S(1)}, u32[]{:S(2)}, u32[]{:S(2)}) collective-permute-start(bf16[4,2,32,256]{3,2,1,0:T(8,128)(2,1)S(1)} %shard_map.84.refs_0_), channel_id=1, source_target_pairs={{0,16},{1,17},{2,18},{3,19},{4,20},{5,21},{6,22},{7,23},{8,24},{9,... | collective-permute-start | bytes 393224 | tf_op jit(solution)/shard_map/ppermute | solution.py:215
  13.1 5.1 %collective-permute-start.3 = (bf16[4,2,32,256]{3,2,1,0:T(8,128)(2,1)S(1)}, bf16[4,2,32,256]{3,2,1,0:T(8,128)(2,1)S(1)}, u32[]{:S(2)}, u32[]{:S(2)}) collective-permute-start(bf16[4,2,32,256]{3,2,1,0:T(8,128)(2,1)S(1)} %shard_map.84.refs_0_), channel_id=1, source_target_pairs={{0,1},{1,0},{2,3},{3,2},{4,5},{5,4},{6,7},{7,6},{8,9},{9,8},{10,11... | collective-permute-start | bytes 393224 | tf_op jit(solution)/shard_map/ppermute | solution.py:215
  14.4 0.7 %copy-start.3 = (s32[4,8,4,1]{1,3,2,0:T(1,128)S(1)}, s32[4,8,4,1]{1,3,2,0:T(1,128)}, u32[]{:S(2)}) copy-start(s32[4,8,4,1]{1,3,2,0:T(1,128)} %param.11) | copy-start | bytes 1540
  15.1 3.3 %copy-start = (bf16[8,256,256]{2,1,0:T(8,128)(2,1)S(1)}, bf16[8,256,256]{2,1,0:T(8,128)(2,1)}, u32[]{:S(2)}) copy-start(bf16[8,256,256]{2,1,0:T(8,128)(2,1)} %left_ref.3) | copy-start | bytes 3145732
  15.9 4.0 %copy-start.2 = (bf16[8,256,256]{2,1,0:T(8,128)(2,1)S(1)}, bf16[8,256,256]{2,1,0:T(8,128)(2,1)}, u32[]{:S(2)}) copy-start(bf16[8,256,256]{2,1,0:T(8,128)(2,1)} %right_ref.1) | copy-start | bytes 3145732
  18.3 1.6 %collective-permute-start.6 = (bf16[2,256,256]{2,1,0:T(8,128)(2,1)S(1)}, bf16[2,256,256]{2,1,0:T(8,128)(2,1)S(1)}, u32[]{:S(2)}, u32[]{:S(2)}) collective-permute-start(bf16[2,256,256]{2,1,0:T(8,128)(2,1)S(1)} %bitcast.6), channel_id=1, source_target_pairs={{0,8},{1,9},{2,10},{3,11},{4,12},{5,13},{6,14},{7,15},{8,0},{9,1},... | collective-permute-start | bytes 786440 | tf_op jit(solution)/shard_map/ppermute | solution.py:215

commit v5 on v4

--- a/solution.py
+++ b/solution.py
@@ -148,7 +148,8 @@
     )(left, table)
 
 
-def terms_kernel(split_rows, left_ref, right_ref, weight_ref, first_ref, table_ref, out_ref, half_ref, sum_ref):
+def terms_kernel(n_lo, left_ref, right_ref, weight_ref, first_ref, table_ref, *refs):
+    outs, (half_ref, sum_ref, total_ref) = refs[:-3], refs[-3:]
     width, n_right = left_ref.shape[1], right_ref.shape[0]
     held = sum_ref.shape[0] // width
     chunks = width // CHUNK
@@ -170,38 +171,66 @@
                 sum_ref[j * width:(j + 1) * width, r * width:(r + 1) * width], right_ref[r], NT,
                 preferred_element_type=jnp.float32)
             acc = part if acc is None else acc + part
-        acc = acc.astype(out_ref.dtype)
-        if split_rows:
-            n_op, rows = out_ref.shape[0], out_ref.shape[2]
-            for o in range(n_op):
-                out_ref[o, j] = acc[o * rows:(o + 1) * rows, :]
-        else:
-            out_ref[j] = acc
-
-
-def terms(first, table, left, right, weight, held, n_op):
+        total_ref[j] = acc
+    if len(outs) == 1:
+        outs[0][...] = total_ref[...]
+        return
+    half, _, rows, _ = outs[0].shape
+    me = lax.axis_index("op")
+    for p, out_ref in enumerate(outs):
+        i, low = p // 2, half * (1 - p % 2)
+        for k in range(half):
+            start = pl.multiple_of(jnp.bitwise_xor(me, (low + k) * n_lo + i) * rows, rows)
+            for j in range(held):
+                out_ref[k, j] = total_ref[j, pl.ds(start, rows), :].astype(out_ref.dtype)
+
+
+def terms(first, table, left, right, weight, held, n_op, n_lo):
     n_slot, width, _ = table.shape
     n_left, n_right = left.shape[0], right.shape[0]
-    rows = width // n_op
-    split_rows = rows % 16 == 0
-    shape = (n_op, held, rows, width) if split_rows else (held, width, width)
+    rows, n_hi = width // n_op, n_op // n_lo
+    if rows % 16 == 0:
+        shape = (n_hi // 2, held, rows, width)
+        out_shape = [jax.ShapeDtypeStruct(shape, x) for x in (jnp.float32, jnp.float32, BF16, BF16)]
+    else:
+        out_shape = [jax.ShapeDtypeStruct((held, width, width), jnp.float32)]
     n_pair, n_cell = n_slot * n_left, held * n_right
-    blocks = n_pair + n_cell + n_left + n_right + n_slot + 4 * held
-    out = pl.pallas_call(
-        functools.partial(terms_kernel, split_rows),
-        out_shape=jax.ShapeDtypeStruct(shape, BF16),
+    blocks = n_pair + n_cell + n_left + n_right + n_slot + 10 * held
+    outs = pl.pallas_call(
+        functools.partial(terms_kernel, n_lo),
+        out_shape=out_shape,
         in_specs=[VMEM] * 5,
-        out_specs=VMEM,
+        out_specs=[VMEM] * len(out_shape),
         scratch_shapes=[
             pltpu.VMEM((width // CHUNK, n_pair * CHUNK, width), BF16),
             pltpu.VMEM((held * width, n_right * width), BF16),
+            pltpu.VMEM((held, width, width), jnp.float32),
         ],
         compiler_params=pltpu.CompilerParams(vmem_limit_bytes=2 * width * width * blocks + 12 * 1024 * 1024),
         cost_estimate=pl.CostEstimate(flops=3 * 10**9, bytes_accessed=4 * 10**6, transcendentals=0),
     )(left, right, weight, first, table)
-    if not split_rows:
-        out = out.reshape(held, n_op, rows, width).transpose(1, 0, 2, 3)
-    return out
+    if rows % 16:
+        whole, me, half = outs[0].reshape(held, n_op, rows, width), lax.axis_index("op"), n_op // 2
+        part = [lax.dynamic_index_in_dim(whole, me ^ o, axis=1, keepdims=False) for o in range(n_op)]
+        outs = [jnp.stack(x) for x in (part[half::n_lo], part[:half:n_lo], part[half + 1::n_lo], part[1:half:n_lo])]
+        outs = [x.astype(BF16) if i > 1 else x for i, x in enumerate(outs)]
+    return outs
+
+
+def combine_kernel(own_ref, other_ref, *outs):
+    for k, out_ref in enumerate(outs):
+        out_ref[...] = (own_ref[k] + other_ref[k].astype(jnp.float32)).astype(out_ref.dtype)
+
+
+def combine(own, other, types):
+    return pl.pallas_call(
+        combine_kernel,
+        out_shape=[jax.ShapeDtypeStruct(own.shape[1:], x) for x in types],
+        in_specs=[VMEM] * 2,
+        out_specs=[VMEM] * len(types),
+        compiler_params=pltpu.CompilerParams(vmem_limit_bytes=8 * 1024 * 1024),
+        cost_estimate=pl.CostEstimate(flops=10**6, bytes_accessed=10**6, transcendentals=0),
+    )(own, other)
 
 
 def shards(psi, left_ops, right_ops, send_list, term_slot, term_out, left_pick, right_pick):
@@ -222,9 +251,15 @@
     keep, give = (x.reshape(n_y, width, width) for x in split(choice, pieces, n_lo))
     got = swap(give, 1, 0)
     first = first_halves(keep, left_ops)
-    partial_sum = terms(first, got, left_ops, right_ops, weight, held, n_op)
-    parts = lax.all_to_all(partial_sum, "op", 0, 0, tiled=True)
-    return jnp.sum(parts.astype(jnp.float32), axis=0)
+    own_far, own_near, far, near = terms(first, got, left_ops, right_ops, weight, held, n_op, n_lo)
+    half = n_hi // 2
+    far = combine(own_far, swap(far, 0, 1), [BF16] * half)
+    near = combine(own_near, swap(near, 0, 1), [jnp.float32] + [BF16] * (half - 1))
+    parts = near + far
+    total = swap(parts[n_hi - 1], 0, (n_hi - 1) * n_lo).astype(jnp.float32)
+    for k in range(n_hi - 2, 0, -1):
+        total = total + swap(parts[k], 0, k * n_lo).astype(jnp.float32)
+    return total + parts[0]
 
 
 def solution(mesh):

time: 35.6 us -> 34.3 us (0.963)
  blocking collectives: 12.9 us -> 0 us
  starting transfers between devices: 9.24 us -> 15.8 us
  waiting for transfers between devices: 6.71 us -> 11.6 us
    all_to_all x1 -> x0, blocking collectives: 12.9 us -> none  [shards(): parts = lax.all_to_all(partial_sum, 'op', 0, 0, tiled=True)]
    ppermute x7 -> x12, starting transfers between devices: 9.24 us -> 15.8 us  [swap(): return lax.ppermute(x, ('sec', 'op'), pairs)]
    ppermute x7 -> x12, waiting for transfers between devices: 6.71 us -> 11.6 us  [swap(): return lax.ppermute(x, ('sec', 'op'), pairs)]
    reduce_sum x1 -> x0, other arithmetic: 0.67 us -> none  [shards(): return jnp.sum(parts.astype(jnp.float32), axis=0)]
    add x0 -> x1, other arithmetic: none -> 0.65 us  [shards(): return total + parts[0]]
    pallas_call x1 -> x3, Pallas kernels: 1.94 us -> 2 us  [the longest x1 1.97 us: terms(): pl.pallas_call(functools.partial(terms_kernel, n_lo), out_shape=out_shape...]
  transfers between devices with their start and end apart: 7 -> 12, of which waited for: 5 -> 9; matrix products, arithmetic and copies ran while one was open for 2% -> 2% of each run, Pallas kernels for 4% -> 5%
where the time goes in v5:
time: 34.3 us; the launch traced here: 34 us
  starting transfers between devices  15.8 us (46%)
  waiting for transfers between devices  11.6 us (34%)
  Pallas kernels  3.66 us (11%)
  local copies, waits for them, and re-layouts  1.5 us (4%)
  other arithmetic  1.36 us (4%)
    ppermute x12, starting transfers between devices, swap(): return lax.ppermute(x, ('sec', 'op'), pairs)  15.8 us
    ppermute x12, waiting for transfers between devices, swap(): return lax.ppermute(x, ('sec', 'op'), pairs)  11.6 us
    pallas_call x1, Pallas kernels, terms(): pl.pallas_call(functools.partial(terms_kernel, n_lo), out_shape=out_shape...  1.97 us
    unnamed x8, local copies, waits for them, and re-layouts  1.5 us
    pallas_call x1, Pallas kernels, prepare(): pl.pallas_call(functools.partial(prepare_kernel, n_left, n_right, held),...  0.85 us
    reshape x1, other arithmetic, prepare(): code.reshape(1, n_term)  0.71 us
    pallas_call x1, Pallas kernels, first_halves(): pl.pallas_call(halves, out_shape=jax.ShapeDtypeStruct((width // CHUNK, n_...  0.71 us
  transfers between devices with their start and end apart: 12, of which 9 were waited for; matrix products, arithmetic and copies ran while one was open for 2% of the time, Pallas kernels for 5%

profile of v5, /device:TPU:0, one launch (start us, length us, event | category | flops | bytes accessed | tf_op | source)
XLA Modules:
  0.0 34.0 jit_solution(16920999363522407476)
XLA Ops:
  0.0 5.0 %collective-permute-start = (bf16[2,32,256]{2,1,0:T(8,128)(2,1)}, bf16[2,32,256]{2,1,0:T(8,128)(2,1)S(1)}, u32[]{:S(2)}, u32[]{:S(2)}) collective-permute-start(bf16[2,32,256]{2,1,0:T(8,128)(2,1)} %from_ref.1), channel_id=1, source_target_pairs={{0,6},{1,7},{2,4},{3,5},{4,2},{5,3},{6,0},{7,1},{8,14},{9,15},{10,... | collective-permute-start | bytes 98312 | tf_op jit(solution)/shard_map/ppermute | solution.py:244
  5.1 0.6 %collective-permute-start.1 = (bf16[2,32,256]{2,1,0:T(8,128)(2,1)}, bf16[2,32,256]{2,1,0:T(8,128)(2,1)S(1)}, u32[]{:S(2)}, u32[]{:S(2)}) collective-permute-start(bf16[2,32,256]{2,1,0:T(8,128)(2,1)} %from_ref.1), channel_id=1, source_target_pairs={{0,2},{1,3},{2,0},{3,1},{4,6},{5,7},{6,4},{7,5},{8,10},{9,11},{10,... | collective-permute-start | bytes 98312 | tf_op jit(solution)/shard_map/ppermute | solution.py:244
  5.6 0.8 %copy-done.1 = bf16[2,32,256]{2,1,0:T(8,128)(2,1)S(1)} copy-done((bf16[2,32,256]{2,1,0:T(8,128)(2,1)S(1)}, bf16[2,32,256]{2,1,0:T(8,128)(2,1)}, u32[]{:S(2)}) %copy-start.1) | copy-done | bytes 32792
  6.4 0.7 %collective-permute-done.refs_1_ = bf16[2,32,256]{2,1,0:T(8,128)(2,1)S(1)} collective-permute-done((bf16[2,32,256]{2,1,0:T(8,128)(2,1)}, bf16[2,32,256]{2,1,0:T(8,128)(2,1)S(1)}, u32[]{:S(2)}, u32[]{:S(2)}) %collective-permute-start) | collective-permute-done | bytes 32800 | tf_op jit(solution)/shard_map/ppermute | solution.py:244
  7.2 2.9 %collective-permute-done.2.refs_3_ = bf16[2,32,256]{2,1,0:T(8,128)(2,1)S(1)} collective-permute-done((bf16[2,32,256]{2,1,0:T(8,128)(2,1)}, bf16[2,32,256]{2,1,0:T(8,128)(2,1)S(1)}, u32[]{:S(2)}, u32[]{:S(2)}) %collective-permute-start.2) | collective-permute-done | bytes 32800 | tf_op jit(solution)/shard_map/ppermute | solution.py:244
  10.1 2.5 %collective-permute-start.5 = (bf16[4,2,32,256]{3,2,1,0:T(8,128)(2,1)S(1)}, bf16[4,2,32,256]{3,2,1,0:T(8,128)(2,1)S(1)}, u32[]{:S(2)}, u32[]{:S(2)}) collective-permute-start(bf16[4,2,32,256]{3,2,1,0:T(8,128)(2,1)S(1)} %shard_map.84.refs_0_), channel_id=1, source_target_pairs={{0,17},{1,16},{2,19},{3,18},{4,21},{5,20},{6,23},{7,22},{8,25},{9,... | collective-permute-start | bytes 393224 | tf_op jit(solution)/shard_map/ppermute | solution.py:244
  12.6 0.5 %collective-permute-start.4 = (bf16[4,2,32,256]{3,2,1,0:T(8,128)(2,1)S(1)}, bf16[4,2,32,256]{3,2,1,0:T(8,128)(2,1)S(1)}, u32[]{:S(2)}, u32[]{:S(2)}) collective-permute-start(bf16[4,2,32,256]{3,2,1,0:T(8,128)(2,1)S(1)} %shard_map.84.refs_0_), channel_id=1, source_target_pairs={{0,16},{1,17},{2,18},{3,19},{4,20},{5,21},{6,22},{7,23},{8,24},{9,... | collective-permute-start | bytes 393224 | tf_op jit(solution)/shard_map/ppermute | solution.py:244
  13.1 0.5 %collective-permute-start.3 = (bf16[4,2,32,256]{3,2,1,0:T(8,128)(2,1)S(1)}, bf16[4,2,32,256]{3,2,1,0:T(8,128)(2,1)S(1)}, u32[]{:S(2)}, u32[]{:S(2)}) collective-permute-start(bf16[4,2,32,256]{3,2,1,0:T(8,128)(2,1)S(1)} %shard_map.84.refs_0_), channel_id=1, source_target_pairs={{0,1},{1,0},{2,3},{3,2},{4,5},{5,4},{6,7},{7,6},{8,9},{9,8},{10,11... | collective-permute-start | bytes 393224 | tf_op jit(solution)/shard_map/ppermute | solution.py:244
  13.6 0.7 %add_bitcast_fusion.code_ref = s32[1,64]{1,0:T(1,128)S(1)} fusion(s32[64]{0:T(128)} %param.15, s32[64]{0:T(128)} %param.13, s32[64]{0:T(128)} %param.14, s32[64]{0:T(128)} %param.12), kind=kLoop, calls=%fused_computation.1 | loop fusion | flops 384 | bytes 1280 | tf_op jit(solution)/shard_map/reshape | solution.py:77
  14.4 0.7 %copy-done.3 = s32[4,8,4,1]{1,3,2,0:T(1,128)S(1)} copy-done((s32[4,8,4,1]{1,3,2,0:T(1,128)S(1)}, s32[4,8,4,1]{1,3,2,0:T(1,128)}, u32[]{:S(2)}) %copy-start.3) | copy-done | bytes 536
  15.1 0.9 %shard_map.82 = (bf16[2,2,32,256]{3,2,1,0:T(8,128)(2,1)S(1)}, bf16[128,256]{1,0:T(8,128)(2,1)S(1)}) custom-call(s32[4,4,1,8]{3,2,1,0:T(1,128)S(1)} %bitcast.7, s32[1,64]{1,0:T(1,128)S(1)} %add_bitcast_fusion.code_ref), custom_call_target="tpu_custom_call" | custom-call | flops 1000000000 | bytes 4000000 | tf_op jit(solution)/shard_map/pallas_call | solution.py:67
  15.9 1.5 %collective-permute-done.5.refs_3_ = bf16[4,2,32,256]{3,2,1,0:T(8,128)(2,1)S(1)} collective-permute-done((bf16[4,2,32,256]{3,2,1,0:T(8,128)(2,1)S(1)}, bf16[4,2,32,256]{3,2,1,0:T(8,128)(2,1)S(1)}, u32[]{:S(2)}, u32[]{:S(2)}) %collective-permute-start.5) | collective-permute-done | bytes 131104 | tf_op jit(solution)/shard_map/ppermute | solution.py:244
  17.4 0.8 %collective-permute-done.4.refs_2_ = bf16[4,2,32,256]{3,2,1,0:T(8,128)(2,1)S(1)} collective-permute-done((bf16[4,2,32,256]{3,2,1,0:T(8,128)(2,1)S(1)}, bf16[4,2,32,256]{3,2,1,0:T(8,128)(2,1)S(1)}, u32[]{:S(2)}, u32[]{:S(2)}) %collective-permute-start.4) | collective-permute-done | bytes 131104 | tf_op jit(solution)/shard_map/ppermute | solution.py:244
  18.4 0.7 %shard_map.86.first_ref = bf16[32,128,256]{2,1,0:T(8,128)(2,1)S(1)} custom-call(bf16[8,256,256]{2,1,0:T(8,128)(2,1)S(1)} %copy-done, bf16[2,256,256]{2,1,0:T(8,128)(2,1)S(1)} %bitcast.5), custom_call_target="tpu_custom_call" | custom-call | flops 536870912 | bytes 1000000 | tf_op jit(solution)/shard_map/pallas_call | solution.py:141
  19.1 0.8 %collective-permute-done.6.table_ref = bf16[2,256,256]{2,1,0:T(8,128)(2,1)S(1)} collective-permute-done((bf16[2,256,256]{2,1,0:T(8,128)(2,1)S(1)}, bf16[2,256,256]{2,1,0:T(8,128)(2,1)S(1)}, u32[]{:S(2)}, u32[]{:S(2)}) %collective-permute-start.6) | collective-permute-done | bytes 262176 | tf_op jit(solution)/shard_map/ppermute | solution.py:244
  19.9 2.0 %shard_map.87 = (f32[2,2,32,256]{3,2,1,0:T(8,128)S(1)}, f32[2,2,32,256]{3,2,1,0:T(8,128)S(1)}, bf16[2,2,32,256]{3,2,1,0:T(8,128)(2,1)S(1)}, bf16[2,2,32,256]{3,2,1,0:T(8,128)(2,1)S(1)}) custom-call(bf16[8,256,256]{2,1,0:T(8,128)(2,1)S(1)} %copy-done, bf16[8,256,256]{2,1,0:T(8,128)(2,1)S(1)} %copy-done.2, bf16[128,256]{1,0:T(8,128)(2,1)S(1)} %get-tuple-element.17.weight_ref, ...), custom_call_target="tpu_custom_call" | custom-call | flops 3000000000 | bytes 4000000 | tf_op jit(solution)/shard_map/pallas_call | solution.py:199
  21.9 1.2 %collective-permute-start.7 = (bf16[2,2,32,256]{3,2,1,0:T(8,128)(2,1)S(1)}, bf16[2,2,32,256]{3,2,1,0:T(8,128)(2,1)S(1)}, u32[]{:S(2)}, u32[]{:S(2)}) collective-permute-start(bf16[2,2,32,256]{3,2,1,0:T(8,128)(2,1)S(1)} %get-tuple-element.22), channel_id=1, source_target_pairs={{0,1},{1,0},{2,3},{3,2},{4,5},{5,4},{6,7},{7,6},{8,9},{9,8},{10,11... | collective-permute-start | bytes 196616 | tf_op jit(solution)/shard_map/ppermute | solution.py:244
  23.0 0.9 %collective-permute-start.10 = (bf16[2,2,32,256]{3,2,1,0:T(8,128)(2,1)S(1)}, bf16[2,2,32,256]{3,2,1,0:T(8,128)(2,1)S(1)}, u32[]{:S(2)}, u32[]{:S(2)}) collective-permute-start(bf16[2,2,32,256]{3,2,1,0:T(8,128)(2,1)S(1)} %get-tuple-element.26), channel_id=1, source_target_pairs={{0,1},{1,0},{2,3},{3,2},{4,5},{5,4},{6,7},{7,6},{8,9},{9,8},{10,11... | collective-permute-start | bytes 196616 | tf_op jit(solution)/shard_map/ppermute | solution.py:244
  23.9 2.9 %collective-permute-done.7.other_ref = bf16[2,2,32,256]{3,2,1,0:T(8,128)(2,1)S(1)} collective-permute-done((bf16[2,2,32,256]{3,2,1,0:T(8,128)(2,1)S(1)}, bf16[2,2,32,256]{3,2,1,0:T(8,128)(2,1)S(1)}, u32[]{:S(2)}, u32[]{:S(2)}) %collective-permute-start.7) | collective-permute-done | bytes 65568 | tf_op jit(solution)/shard_map/ppermute | solution.py:244
  26.9 1.2 %collective-permute-start.8 = (bf16[2,32,256]{2,1,0:T(8,128)(2,1)S(1)}, bf16[2,32,256]{2,1,0:T(8,128)(2,1)S(1)}, u32[]{:S(2)}, u32[]{:S(2)}) collective-permute-start(bf16[2,32,256]{2,1,0:T(8,128)(2,1)S(1)} %get-tuple-element.23), channel_id=1, source_target_pairs={{0,6},{1,7},{2,4},{3,5},{4,2},{5,3},{6,0},{7,1},{8,14},{9,15},{10,... | collective-permute-start | bytes 98312 | tf_op jit(solution)/shard_map/ppermute | solution.py:244
  28.1 1.0 %collective-permute-start.9 = (bf16[2,32,256]{2,1,0:T(8,128)(2,1)S(1)}, bf16[2,32,256]{2,1,0:T(8,128)(2,1)S(1)}, u32[]{:S(2)}, u32[]{:S(2)}) collective-permute-start(bf16[2,32,256]{2,1,0:T(8,128)(2,1)S(1)} %get-tuple-element.24), channel_id=1, source_target_pairs={{0,4},{1,5},{2,6},{3,7},{4,0},{5,1},{6,2},{7,3},{8,12},{9,13},{10,... | collective-permute-start | bytes 98312 | tf_op jit(solution)/shard_map/ppermute | solution.py:244
  29.1 2.4 %collective-permute-start.11 = (bf16[2,32,256]{2,1,0:T(8,128)(2,1)S(1)}, bf16[2,32,256]{2,1,0:T(8,128)(2,1)S(1)}, u32[]{:S(2)}, u32[]{:S(2)}) collective-permute-start(bf16[2,32,256]{2,1,0:T(8,128)(2,1)S(1)} %get-tuple-element.27), channel_id=1, source_target_pairs={{0,2},{1,3},{2,0},{3,1},{4,6},{5,7},{6,4},{7,5},{8,10},{9,11},{10,... | collective-permute-start | bytes 98312 | tf_op jit(solution)/shard_map/ppermute | solution.py:244
  31.4 1.2 %collective-permute-done.8 = bf16[2,32,256]{2,1,0:T(8,128)(2,1)S(1)} collective-permute-done((bf16[2,32,256]{2,1,0:T(8,128)(2,1)S(1)}, bf16[2,32,256]{2,1,0:T(8,128)(2,1)S(1)}, u32[]{:S(2)}, u32[]{:S(2)}) %collective-permute-start.8) | collective-permute-done | bytes 32800 | tf_op jit(solution)/shard_map/ppermute | solution.py:244
  33.4 0.6 %add_add_fusion = f32[2,32,256]{2,1,0:T(8,128)} fusion(f32[2,32,256]{2,1,0:T(8,128)S(1)} %get-tuple-element.28, bf16[2,32,256]{2,1,0:T(8,128)(2,1)S(1)} %collective-permute-done.11, bf16[2,32,256]{2,1,0:T(8,128)(2,1)S(1)} %collective-permute-done.9, bf16[2,32,256]{2,1,0:T(8,128)(2,1)S(1)} %collective-permute-done.8), kind=kLoop, calls=%fused_computation | loop fusion | flops 98304 | bytes 229376 | tf_op jit(solution)/shard_map/add | solution.py:262
  (18 shorter events, 0.9 us)
Async XLA Ops:
  0.0 7.2 %collective-permute-start = (bf16[2,32,256]{2,1,0:T(8,128)(2,1)}, bf16[2,32,256]{2,1,0:T(8,128)(2,1)S(1)}, u32[]{:S(2)}, u32[]{:S(2)}) collective-permute-start(bf16[2,32,256]{2,1,0:T(8,128)(2,1)} %from_ref.1), channel_id=1, source_target_pairs={{0,6},{1,7},{2,4},{3,5},{4,2},{5,3},{6,0},{7,1},{8,14},{9,15},{10,... | collective-permute-start | bytes 98312 | tf_op jit(solution)/shard_map/ppermute | solution.py:244
  5.0 5.0 %collective-permute-start.2 = (bf16[2,32,256]{2,1,0:T(8,128)(2,1)}, bf16[2,32,256]{2,1,0:T(8,128)(2,1)S(1)}, u32[]{:S(2)}, u32[]{:S(2)}) collective-permute-start(bf16[2,32,256]{2,1,0:T(8,128)(2,1)} %from_ref.1), channel_id=1, source_target_pairs={{0,4},{1,5},{2,6},{3,7},{4,0},{5,1},{6,2},{7,3},{8,12},{9,13},{10,... | collective-permute-start | bytes 98312 | tf_op jit(solution)/shard_map/ppermute | solution.py:244
  5.1 5.0 %collective-permute-start.1 = (bf16[2,32,256]{2,1,0:T(8,128)(2,1)}, bf16[2,32,256]{2,1,0:T(8,128)(2,1)S(1)}, u32[]{:S(2)}, u32[]{:S(2)}) collective-permute-start(bf16[2,32,256]{2,1,0:T(8,128)(2,1)} %from_ref.1), channel_id=1, source_target_pairs={{0,2},{1,3},{2,0},{3,1},{4,6},{5,7},{6,4},{7,5},{8,10},{9,11},{10,... | collective-permute-start | bytes 98312 | tf_op jit(solution)/shard_map/ppermute | solution.py:244
  5.6 0.8 %copy-start.1 = (bf16[2,32,256]{2,1,0:T(8,128)(2,1)S(1)}, bf16[2,32,256]{2,1,0:T(8,128)(2,1)}, u32[]{:S(2)}) copy-start(bf16[2,32,256]{2,1,0:T(8,128)(2,1)} %from_ref.1) | copy-start | bytes 98308
  10.1 7.3 %collective-permute-start.5 = (bf16[4,2,32,256]{3,2,1,0:T(8,128)(2,1)S(1)}, bf16[4,2,32,256]{3,2,1,0:T(8,128)(2,1)S(1)}, u32[]{:S(2)}, u32[]{:S(2)}) collective-permute-start(bf16[4,2,32,256]{3,2,1,0:T(8,128)(2,1)S(1)} %shard_map.84.refs_0_), channel_id=1, source_target_pairs={{0,17},{1,16},{2,19},{3,18},{4,21},{5,20},{6,23},{7,22},{8,25},{9,... | collective-permute-start | bytes 393224 | tf_op jit(solution)/shard_map/ppermute | solution.py:244
  12.6 5.6 %collective-permute-start.4 = (bf16[4,2,32,256]{3,2,1,0:T(8,128)(2,1)S(1)}, bf16[4,2,32,256]{3,2,1,0:T(8,128)(2,1)S(1)}, u32[]{:S(2)}, u32[]{:S(2)}) collective-permute-start(bf16[4,2,32,256]{3,2,1,0:T(8,128)(2,1)S(1)} %shard_map.84.refs_0_), channel_id=1, source_target_pairs={{0,16},{1,17},{2,18},{3,19},{4,20},{5,21},{6,22},{7,23},{8,24},{9,... | collective-permute-start | bytes 393224 | tf_op jit(solution)/shard_map/ppermute | solution.py:244
  13.1 5.1 %collective-permute-start.3 = (bf16[4,2,32,256]{3,2,1,0:T(8,128)(2,1)S(1)}, bf16[4,2,32,256]{3,2,1,0:T(8,128)(2,1)S(1)}, u32[]{:S(2)}, u32[]{:S(2)}) collective-permute-start(bf16[4,2,32,256]{3,2,1,0:T(8,128)(2,1)S(1)} %shard_map.84.refs_0_), channel_id=1, source_target_pairs={{0,1},{1,0},{2,3},{3,2},{4,5},{5,4},{6,7},{7,6},{8,9},{9,8},{10,11... | collective-permute-start | bytes 393224 | tf_op jit(solution)/shard_map/ppermute | solution.py:244
  14.4 0.7 %copy-start.3 = (s32[4,8,4,1]{1,3,2,0:T(1,128)S(1)}, s32[4,8,4,1]{1,3,2,0:T(1,128)}, u32[]{:S(2)}) copy-start(s32[4,8,4,1]{1,3,2,0:T(1,128)} %param.11) | copy-start | bytes 1540
  15.1 3.3 %copy-start = (bf16[8,256,256]{2,1,0:T(8,128)(2,1)S(1)}, bf16[8,256,256]{2,1,0:T(8,128)(2,1)}, u32[]{:S(2)}) copy-start(bf16[8,256,256]{2,1,0:T(8,128)(2,1)} %left_ref.3) | copy-start | bytes 3145732
  15.9 4.0 %copy-start.2 = (bf16[8,256,256]{2,1,0:T(8,128)(2,1)S(1)}, bf16[8,256,256]{2,1,0:T(8,128)(2,1)}, u32[]{:S(2)}) copy-start(bf16[8,256,256]{2,1,0:T(8,128)(2,1)} %right_ref.1) | copy-start | bytes 3145732
  18.3 1.6 %collective-permute-start.6 = (bf16[2,256,256]{2,1,0:T(8,128)(2,1)S(1)}, bf16[2,256,256]{2,1,0:T(8,128)(2,1)S(1)}, u32[]{:S(2)}, u32[]{:S(2)}) collective-permute-start(bf16[2,256,256]{2,1,0:T(8,128)(2,1)S(1)} %bitcast.6), channel_id=1, source_target_pairs={{0,8},{1,9},{2,10},{3,11},{4,12},{5,13},{6,14},{7,15},{8,0},{9,1},... | collective-permute-start | bytes 786440 | tf_op jit(solution)/shard_map/ppermute | solution.py:244
  21.9 5.0 %collective-permute-start.7 = (bf16[2,2,32,256]{3,2,1,0:T(8,128)(2,1)S(1)}, bf16[2,2,32,256]{3,2,1,0:T(8,128)(2,1)S(1)}, u32[]{:S(2)}, u32[]{:S(2)}) collective-permute-start(bf16[2,2,32,256]{3,2,1,0:T(8,128)(2,1)S(1)} %get-tuple-element.22), channel_id=1, source_target_pairs={{0,1},{1,0},{2,3},{3,2},{4,5},{5,4},{6,7},{7,6},{8,9},{9,8},{10,11... | collective-permute-start | bytes 196616 | tf_op jit(solution)/shard_map/ppermute | solution.py:244
  23.0 6.0 %collective-permute-start.10 = (bf16[2,2,32,256]{3,2,1,0:T(8,128)(2,1)S(1)}, bf16[2,2,32,256]{3,2,1,0:T(8,128)(2,1)S(1)}, u32[]{:S(2)}, u32[]{:S(2)}) collective-permute-start(bf16[2,2,32,256]{3,2,1,0:T(8,128)(2,1)S(1)} %get-tuple-element.26), channel_id=1, source_target_pairs={{0,1},{1,0},{2,3},{3,2},{4,5},{5,4},{6,7},{7,6},{8,9},{9,8},{10,11... | collective-permute-start | bytes 196616 | tf_op jit(solution)/shard_map/ppermute | solution.py:244
  26.9 5.8 %collective-permute-start.8 = (bf16[2,32,256]{2,1,0:T(8,128)(2,1)S(1)}, bf16[2,32,256]{2,1,0:T(8,128)(2,1)S(1)}, u32[]{:S(2)}, u32[]{:S(2)}) collective-permute-start(bf16[2,32,256]{2,1,0:T(8,128)(2,1)S(1)} %get-tuple-element.23), channel_id=1, source_target_pairs={{0,6},{1,7},{2,4},{3,5},{4,2},{5,3},{6,0},{7,1},{8,14},{9,15},{10,... | collective-permute-start | bytes 98312 | tf_op jit(solution)/shard_map/ppermute | solution.py:244
  28.1 5.0 %collective-permute-start.9 = (bf16[2,32,256]{2,1,0:T(8,128)(2,1)S(1)}, bf16[2,32,256]{2,1,0:T(8,128)(2,1)S(1)}, u32[]{:S(2)}, u32[]{:S(2)}) collective-permute-start(bf16[2,32,256]{2,1,0:T(8,128)(2,1)S(1)} %get-tuple-element.24), channel_id=1, source_target_pairs={{0,4},{1,5},{2,6},{3,7},{4,0},{5,1},{6,2},{7,3},{8,12},{9,13},{10,... | collective-permute-start | bytes 98312 | tf_op jit(solution)/shard_map/ppermute | solution.py:244
  29.1 4.3 %collective-permute-start.11 = (bf16[2,32,256]{2,1,0:T(8,128)(2,1)S(1)}, bf16[2,32,256]{2,1,0:T(8,128)(2,1)S(1)}, u32[]{:S(2)}, u32[]{:S(2)}) collective-permute-start(bf16[2,32,256]{2,1,0:T(8,128)(2,1)S(1)} %get-tuple-element.27), channel_id=1, source_target_pairs={{0,2},{1,3},{2,0},{3,1},{4,6},{5,7},{6,4},{7,5},{8,10},{9,11},{10,... | collective-permute-start | bytes 98312 | tf_op jit(solution)/shard_map/ppermute | solution.py:244

commit v6 on v5

--- a/solution.py
+++ b/solution.py
@@ -148,7 +148,7 @@
     )(left, table)
 
 
-def terms_kernel(n_lo, left_ref, right_ref, weight_ref, first_ref, table_ref, *refs):
+def terms_kernel(n_lo, keys, left_ref, right_ref, weight_ref, first_ref, table_ref, *refs):
     outs, (half_ref, sum_ref, total_ref) = refs[:-3], refs[-3:]
     width, n_right = left_ref.shape[1], right_ref.shape[0]
     held = sum_ref.shape[0] // width
@@ -172,32 +172,33 @@
                 preferred_element_type=jnp.float32)
             acc = part if acc is None else acc + part
         total_ref[j] = acc
-    if len(outs) == 1:
+    if not keys:
         outs[0][...] = total_ref[...]
         return
-    half, _, rows, _ = outs[0].shape
     me = lax.axis_index("op")
-    for p, out_ref in enumerate(outs):
-        i, low = p // 2, half * (1 - p % 2)
-        for k in range(half):
-            start = pl.multiple_of(jnp.bitwise_xor(me, (low + k) * n_lo + i) * rows, rows)
-            for j in range(held):
-                out_ref[k, j] = total_ref[j, pl.ds(start, rows), :].astype(out_ref.dtype)
-
-
-def terms(first, table, left, right, weight, held, n_op, n_lo):
+    for (k, i), (out_ref, place) in zip(keys, [(x, p) for x in outs for p in range(x.shape[0])]):
+        rows = out_ref.shape[2]
+        start = pl.multiple_of(jnp.bitwise_xor(me, k * n_lo + i) * rows, rows)
+        for j in range(held):
+            out_ref[place, j] = total_ref[j, pl.ds(start, rows), :].astype(out_ref.dtype)
+
+
+def terms(first, table, left, right, weight, held, n_op, n_lo, staged, direct):
     n_slot, width, _ = table.shape
     n_left, n_right = left.shape[0], right.shape[0]
     rows, n_hi = width // n_op, n_op // n_lo
+    groups = [[(k, i) for k in staged] for i in range(n_lo)] + [[(direct, i)] for i in range(n_lo)]
+    types = [BF16 if p else jnp.float32 for p in range(len(groups))]
     if rows % 16 == 0:
-        shape = (n_hi // 2, held, rows, width)
-        out_shape = [jax.ShapeDtypeStruct(shape, x) for x in (jnp.float32, jnp.float32, BF16, BF16)]
+        keys = sum(groups, [])
+        out_shape = [jax.ShapeDtypeStruct((len(group), held, rows, width), x) for group, x in zip(groups, types)]
     else:
+        keys = []
         out_shape = [jax.ShapeDtypeStruct((held, width, width), jnp.float32)]
     n_pair, n_cell = n_slot * n_left, held * n_right
     blocks = n_pair + n_cell + n_left + n_right + n_slot + 10 * held
     outs = pl.pallas_call(
-        functools.partial(terms_kernel, n_lo),
+        functools.partial(terms_kernel, n_lo, keys),
         out_shape=out_shape,
         in_specs=[VMEM] * 5,
         out_specs=[VMEM] * len(out_shape),
@@ -209,26 +210,25 @@
         compiler_params=pltpu.CompilerParams(vmem_limit_bytes=2 * width * width * blocks + 12 * 1024 * 1024),
         cost_estimate=pl.CostEstimate(flops=3 * 10**9, bytes_accessed=4 * 10**6, transcendentals=0),
     )(left, right, weight, first, table)
-    if rows % 16:
-        whole, me, half = outs[0].reshape(held, n_op, rows, width), lax.axis_index("op"), n_op // 2
+    if not keys:
+        whole, me = outs[0].reshape(held, n_op, rows, width), lax.axis_index("op")
         part = [lax.dynamic_index_in_dim(whole, me ^ o, axis=1, keepdims=False) for o in range(n_op)]
-        outs = [jnp.stack(x) for x in (part[half::n_lo], part[:half:n_lo], part[half + 1::n_lo], part[1:half:n_lo])]
-        outs = [x.astype(BF16) if i > 1 else x for i, x in enumerate(outs)]
+        outs = [jnp.stack([part[k * n_lo + i] for k, i in group]).astype(x) for group, x in zip(groups, types)]
     return outs
 
 
 def combine_kernel(own_ref, other_ref, *outs):
-    for k, out_ref in enumerate(outs):
-        out_ref[...] = (own_ref[k] + other_ref[k].astype(jnp.float32)).astype(out_ref.dtype)
-
-
-def combine(own, other, types):
+    for k, out_ref in enumerate(outs, start=1):
+        out_ref[...] = (own_ref[k] + other_ref[k].astype(jnp.float32)).astype(BF16)
+
+
+def combine(own, other):
     return pl.pallas_call(
         combine_kernel,
-        out_shape=[jax.ShapeDtypeStruct(own.shape[1:], x) for x in types],
+        out_shape=[jax.ShapeDtypeStruct(own.shape[1:], BF16)] * (own.shape[0] - 1),
         in_specs=[VMEM] * 2,
-        out_specs=[VMEM] * len(types),
-        compiler_params=pltpu.CompilerParams(vmem_limit_bytes=8 * 1024 * 1024),
+        out_specs=[VMEM] * (own.shape[0] - 1),
+        compiler_params=pltpu.CompilerParams(vmem_limit_bytes=4 * 1024 * 1024),
         cost_estimate=pl.CostEstimate(flops=10**6, bytes_accessed=10**6, transcendentals=0),
     )(own, other)
 
@@ -251,15 +251,18 @@
     keep, give = (x.reshape(n_y, width, width) for x in split(choice, pieces, n_lo))
     got = swap(give, 1, 0)
     first = first_halves(keep, left_ops)
-    own_far, own_near, far, near = terms(first, got, left_ops, right_ops, weight, held, n_op, n_lo)
-    half = n_hi // 2
-    far = combine(own_far, swap(far, 0, 1), [BF16] * half)
-    near = combine(own_near, swap(near, 0, 1), [jnp.float32] + [BF16] * (half - 1))
-    parts = near + far
-    total = swap(parts[n_hi - 1], 0, (n_hi - 1) * n_lo).astype(jnp.float32)
-    for k in range(n_hi - 2, 0, -1):
-        total = total + swap(parts[k], 0, k * n_lo).astype(jnp.float32)
-    return total + parts[0]
+    direct = n_hi - 1
+    staged = [k for k in range(n_hi) if k != direct]
+    own, other, *far = terms(first, got, left_ops, right_ops, weight, held, n_op, n_lo, staged, direct)
+    total = None
+    for i in range(n_lo - 1, -1, -1):
+        part = swap(far[i][0], 0, direct * n_lo + i).astype(jnp.float32)
+        total = part if total is None else total + part
+    other = swap(other, 0, 1)
+    sums = dict(zip(staged[1:], combine(own, other)))
+    for k in staged[1:]:
+        total = total + swap(sums[k], 0, k * n_lo).astype(jnp.float32)
+    return total + own[0] + other[0].astype(jnp.float32)
 
 
 def solution(mesh):

time: 34.3 us -> 33.1 us (0.965)
  waiting for transfers between devices: 11.6 us -> 9.61 us
  starting transfers between devices: 15.8 us -> 16.6 us
    ppermute x12, waiting for transfers between devices: 11.6 us -> 9.61 us  [swap(): return lax.ppermute(x, ('sec', 'op'), pairs)]
    ppermute x12, starting transfers between devices: 15.8 us -> 16.6 us  [swap(): return lax.ppermute(x, ('sec', 'op'), pairs)]
  transfers between devices with their start and end apart: 12 -> 12, of which waited for: 9 -> 7; matrix products, arithmetic and copies ran while one was open for 2% -> 2% of each run, Pallas kernels for 5% -> 5%
where the time goes in v6:
time: 33.1 us; the launch traced here: 32.8 us
  starting transfers between devices  16.6 us (50%)
  waiting for transfers between devices  9.61 us (29%)
  Pallas kernels  3.64 us (11%)
  local copies, waits for them, and re-layouts  1.5 us (5%)
  other arithmetic  1.37 us (4%)
    ppermute x12, starting transfers between devices, swap(): return lax.ppermute(x, ('sec', 'op'), pairs)  16.6 us
    ppermute x12, waiting for transfers between devices, swap(): return lax.ppermute(x, ('sec', 'op'), pairs)  9.61 us
    pallas_call x1, Pallas kernels, terms(): pl.pallas_call(functools.partial(terms_kernel, n_lo, keys), out_shape=out...  1.97 us
    unnamed x8, local copies, waits for them, and re-layouts  1.5 us
    pallas_call x1, Pallas kernels, prepare(): pl.pallas_call(functools.partial(prepare_kernel, n_left, n_right, held),...  0.85 us
    reshape x1, other arithmetic, prepare(): code.reshape(1, n_term)  0.71 us
    pallas_call x1, Pallas kernels, first_halves(): pl.pallas_call(halves, out_shape=jax.ShapeDtypeStruct((width // CHUNK, n_...  0.71 us
  transfers between devices with their start and end apart: 12, of which 7 were waited for; matrix products, arithmetic and copies ran while one was open for 2% of the time, Pallas kernels for 5%

profile of v6, /device:TPU:0, one launch (start us, length us, event | category | flops | bytes accessed | tf_op | source)
XLA Modules:
  0.0 32.8 jit_solution(4776762922702025485)
XLA Ops:
  0.0 5.0 %collective-permute-start = (bf16[2,32,256]{2,1,0:T(8,128)(2,1)}, bf16[2,32,256]{2,1,0:T(8,128)(2,1)S(1)}, u32[]{:S(2)}, u32[]{:S(2)}) collective-permute-start(bf16[2,32,256]{2,1,0:T(8,128)(2,1)} %from_ref.1), channel_id=1, source_target_pairs={{0,6},{1,7},{2,4},{3,5},{4,2},{5,3},{6,0},{7,1},{8,14},{9,15},{10,... | collective-permute-start | bytes 98312 | tf_op jit(solution)/shard_map/ppermute | solution.py:244
  5.1 0.6 %collective-permute-start.1 = (bf16[2,32,256]{2,1,0:T(8,128)(2,1)}, bf16[2,32,256]{2,1,0:T(8,128)(2,1)S(1)}, u32[]{:S(2)}, u32[]{:S(2)}) collective-permute-start(bf16[2,32,256]{2,1,0:T(8,128)(2,1)} %from_ref.1), channel_id=1, source_target_pairs={{0,2},{1,3},{2,0},{3,1},{4,6},{5,7},{6,4},{7,5},{8,10},{9,11},{10,... | collective-permute-start | bytes 98312 | tf_op jit(solution)/shard_map/ppermute | solution.py:244
  5.6 0.8 %copy-done.1 = bf16[2,32,256]{2,1,0:T(8,128)(2,1)S(1)} copy-done((bf16[2,32,256]{2,1,0:T(8,128)(2,1)S(1)}, bf16[2,32,256]{2,1,0:T(8,128)(2,1)}, u32[]{:S(2)}) %copy-start.1) | copy-done | bytes 32792
  6.4 0.7 %collective-permute-done.refs_1_ = bf16[2,32,256]{2,1,0:T(8,128)(2,1)S(1)} collective-permute-done((bf16[2,32,256]{2,1,0:T(8,128)(2,1)}, bf16[2,32,256]{2,1,0:T(8,128)(2,1)S(1)}, u32[]{:S(2)}, u32[]{:S(2)}) %collective-permute-start) | collective-permute-done | bytes 32800 | tf_op jit(solution)/shard_map/ppermute | solution.py:244
  7.2 2.9 %collective-permute-done.2.refs_3_ = bf16[2,32,256]{2,1,0:T(8,128)(2,1)S(1)} collective-permute-done((bf16[2,32,256]{2,1,0:T(8,128)(2,1)}, bf16[2,32,256]{2,1,0:T(8,128)(2,1)S(1)}, u32[]{:S(2)}, u32[]{:S(2)}) %collective-permute-start.2) | collective-permute-done | bytes 32800 | tf_op jit(solution)/shard_map/ppermute | solution.py:244
  10.1 2.5 %collective-permute-start.5 = (bf16[4,2,32,256]{3,2,1,0:T(8,128)(2,1)S(1)}, bf16[4,2,32,256]{3,2,1,0:T(8,128)(2,1)S(1)}, u32[]{:S(2)}, u32[]{:S(2)}) collective-permute-start(bf16[4,2,32,256]{3,2,1,0:T(8,128)(2,1)S(1)} %shard_map.84.refs_0_), channel_id=1, source_target_pairs={{0,17},{1,16},{2,19},{3,18},{4,21},{5,20},{6,23},{7,22},{8,25},{9,... | collective-permute-start | bytes 393224 | tf_op jit(solution)/shard_map/ppermute | solution.py:244
  12.6 0.5 %collective-permute-start.4 = (bf16[4,2,32,256]{3,2,1,0:T(8,128)(2,1)S(1)}, bf16[4,2,32,256]{3,2,1,0:T(8,128)(2,1)S(1)}, u32[]{:S(2)}, u32[]{:S(2)}) collective-permute-start(bf16[4,2,32,256]{3,2,1,0:T(8,128)(2,1)S(1)} %shard_map.84.refs_0_), channel_id=1, source_target_pairs={{0,16},{1,17},{2,18},{3,19},{4,20},{5,21},{6,22},{7,23},{8,24},{9,... | collective-permute-start | bytes 393224 | tf_op jit(solution)/shard_map/ppermute | solution.py:244
  13.1 0.5 %collective-permute-start.3 = (bf16[4,2,32,256]{3,2,1,0:T(8,128)(2,1)S(1)}, bf16[4,2,32,256]{3,2,1,0:T(8,128)(2,1)S(1)}, u32[]{:S(2)}, u32[]{:S(2)}) collective-permute-start(bf16[4,2,32,256]{3,2,1,0:T(8,128)(2,1)S(1)} %shard_map.84.refs_0_), channel_id=1, source_target_pairs={{0,1},{1,0},{2,3},{3,2},{4,5},{5,4},{6,7},{7,6},{8,9},{9,8},{10,11... | collective-permute-start | bytes 393224 | tf_op jit(solution)/shard_map/ppermute | solution.py:244
  13.6 0.7 %add_bitcast_fusion.code_ref = s32[1,64]{1,0:T(1,128)S(1)} fusion(s32[64]{0:T(128)} %param.15, s32[64]{0:T(128)} %param.13, s32[64]{0:T(128)} %param.14, s32[64]{0:T(128)} %param.12), kind=kLoop, calls=%fused_computation.3 | loop fusion | flops 384 | bytes 1280 | tf_op jit(solution)/shard_map/reshape | solution.py:77
  14.4 0.7 %copy-done.3 = s32[4,8,4,1]{1,3,2,0:T(1,128)S(1)} copy-done((s32[4,8,4,1]{1,3,2,0:T(1,128)S(1)}, s32[4,8,4,1]{1,3,2,0:T(1,128)}, u32[]{:S(2)}) %copy-start.3) | copy-done | bytes 536
  15.1 0.9 %shard_map.82 = (bf16[2,2,32,256]{3,2,1,0:T(8,128)(2,1)S(1)}, bf16[128,256]{1,0:T(8,128)(2,1)S(1)}) custom-call(s32[4,4,1,8]{3,2,1,0:T(1,128)S(1)} %bitcast.20, s32[1,64]{1,0:T(1,128)S(1)} %add_bitcast_fusion.code_ref), custom_call_target="tpu_custom_call" | custom-call | flops 1000000000 | bytes 4000000 | tf_op jit(solution)/shard_map/pallas_call | solution.py:67
  15.9 1.5 %collective-permute-done.5.refs_3_ = bf16[4,2,32,256]{3,2,1,0:T(8,128)(2,1)S(1)} collective-permute-done((bf16[4,2,32,256]{3,2,1,0:T(8,128)(2,1)S(1)}, bf16[4,2,32,256]{3,2,1,0:T(8,128)(2,1)S(1)}, u32[]{:S(2)}, u32[]{:S(2)}) %collective-permute-start.5) | collective-permute-done | bytes 131104 | tf_op jit(solution)/shard_map/ppermute | solution.py:244
  17.4 0.8 %collective-permute-done.4.refs_2_ = bf16[4,2,32,256]{3,2,1,0:T(8,128)(2,1)S(1)} collective-permute-done((bf16[4,2,32,256]{3,2,1,0:T(8,128)(2,1)S(1)}, bf16[4,2,32,256]{3,2,1,0:T(8,128)(2,1)S(1)}, u32[]{:S(2)}, u32[]{:S(2)}) %collective-permute-start.4) | collective-permute-done | bytes 131104 | tf_op jit(solution)/shard_map/ppermute | solution.py:244
  18.4 0.7 %shard_map.86.first_ref = bf16[32,128,256]{2,1,0:T(8,128)(2,1)S(1)} custom-call(bf16[8,256,256]{2,1,0:T(8,128)(2,1)S(1)} %copy-done, bf16[2,256,256]{2,1,0:T(8,128)(2,1)S(1)} %bitcast.16), custom_call_target="tpu_custom_call" | custom-call | flops 536870912 | bytes 1000000 | tf_op jit(solution)/shard_map/pallas_call | solution.py:141
  19.1 0.8 %collective-permute-done.6.table_ref = bf16[2,256,256]{2,1,0:T(8,128)(2,1)S(1)} collective-permute-done((bf16[2,256,256]{2,1,0:T(8,128)(2,1)S(1)}, bf16[2,256,256]{2,1,0:T(8,128)(2,1)S(1)}, u32[]{:S(2)}, u32[]{:S(2)}) %collective-permute-start.6) | collective-permute-done | bytes 262176 | tf_op jit(solution)/shard_map/ppermute | solution.py:244
  19.9 2.0 %shard_map.87 = (f32[3,2,32,256]{3,2,1,0:T(8,128)S(1)}, bf16[3,2,32,256]{3,2,1,0:T(8,128)(2,1)S(1)}, bf16[1,2,32,256]{3,2,1,0:T(8,128)(2,1)S(1)}, bf16[1,2,32,256]{3,2,1,0:T(8,128)(2,1)S(1)}) custom-call(bf16[8,256,256]{2,1,0:T(8,128)(2,1)S(1)} %copy-done, bf16[8,256,256]{2,1,0:T(8,128)(2,1)S(1)} %copy-done.2, ...), custom_call_target="tpu_custom_call" | custom-call | flops 3000000000 | bytes 4000000 | tf_op jit(solution)/shard_map/pallas_call | solution.py:200
  21.9 1.2 %collective-permute-start.9 = (bf16[3,2,32,256]{3,2,1,0:T(8,128)(2,1)S(1)}, bf16[3,2,32,256]{3,2,1,0:T(8,128)(2,1)S(1)}, u32[]{:S(2)}, u32[]{:S(2)}) collective-permute-start(bf16[3,2,32,256]{3,2,1,0:T(8,128)(2,1)S(1)} %get-tuple-element.22), channel_id=1, source_target_pairs={{0,1},{1,0},{2,3},{3,2},{4,5},{5,4},{6,7},{7,6},{8,9},{9,8},{10,11... | collective-permute-start | bytes 294920 | tf_op jit(solution)/shard_map/ppermute | solution.py:244
  23.0 1.8 %collective-permute-start.8 = (bf16[2,32,256]{2,1,0:T(8,128)(2,1)S(1)}, bf16[2,32,256]{2,1,0:T(8,128)(2,1)S(1)}, u32[]{:S(2)}, u32[]{:S(2)}) collective-permute-start(bf16[2,32,256]{2,1,0:T(8,128)(2,1)S(1)} %bitcast.19), channel_id=1, source_target_pairs={{0,6},{1,7},{2,4},{3,5},{4,2},{5,3},{6,0},{7,1},{8,14},{9,15},{10,... | collective-permute-start | bytes 98312 | tf_op jit(solution)/shard_map/ppermute | solution.py:244
  24.8 2.4 %collective-permute-start.7 = (bf16[2,32,256]{2,1,0:T(8,128)(2,1)S(1)}, bf16[2,32,256]{2,1,0:T(8,128)(2,1)S(1)}, u32[]{:S(2)}, u32[]{:S(2)}) collective-permute-start(bf16[2,32,256]{2,1,0:T(8,128)(2,1)S(1)} %bitcast.18), channel_id=1, source_target_pairs={{0,7},{1,6},{2,5},{3,4},{4,3},{5,2},{6,1},{7,0},{8,15},{9,14},{10,... | collective-permute-start | bytes 98312 | tf_op jit(solution)/shard_map/ppermute | solution.py:244
  27.2 0.1 collective-permute-start.10
  27.3 2.0 %collective-permute-start.11 = (bf16[2,32,256]{2,1,0:T(8,128)(2,1)S(1)}, bf16[2,32,256]{2,1,0:T(8,128)(2,1)S(1)}, u32[]{:S(2)}, u32[]{:S(2)}) collective-permute-start(bf16[2,32,256]{2,1,0:T(8,128)(2,1)S(1)} %get-tuple-element.24), channel_id=1, source_target_pairs={{0,4},{1,5},{2,6},{3,7},{4,0},{5,1},{6,2},{7,3},{8,12},{9,13},{10,... | collective-permute-start | bytes 98312 | tf_op jit(solution)/shard_map/ppermute | solution.py:244
  29.3 2.2 %collective-permute-done.7 = bf16[2,32,256]{2,1,0:T(8,128)(2,1)S(1)} collective-permute-done((bf16[2,32,256]{2,1,0:T(8,128)(2,1)S(1)}, bf16[2,32,256]{2,1,0:T(8,128)(2,1)S(1)}, u32[]{:S(2)}, u32[]{:S(2)}) %collective-permute-start.7) | collective-permute-done | bytes 32800 | tf_op jit(solution)/shard_map/ppermute | solution.py:244
  31.5 0.7 %collective-permute-done.11 = bf16[2,32,256]{2,1,0:T(8,128)(2,1)S(1)} collective-permute-done((bf16[2,32,256]{2,1,0:T(8,128)(2,1)S(1)}, bf16[2,32,256]{2,1,0:T(8,128)(2,1)S(1)}, u32[]{:S(2)}, u32[]{:S(2)}) %collective-permute-start.11) | collective-permute-done | bytes 32800 | tf_op jit(solution)/shard_map/ppermute | solution.py:244
  32.2 0.7 %convert_add_fusion = f32[2,32,256]{2,1,0:T(8,128)} fusion(f32[3,2,32,256]{3,2,1,0:T(8,128)S(1)} %get-tuple-element.21.own_ref, bf16[2,32,256]{2,1,0:T(8,128)(2,1)S(1)} %collective-permute-done.11, bf16[2,32,256]{2,1,0:T(8,128)(2,1)S(1)} %collective-permute-done.10, bf16[2,32,256]{2,1,0:T(8,128)(2,1)S(1)} %collective-permute-done.8, ...), kind=kLoop, calls=%fused_computation | loop fusion | flops 163840 | bytes 294912 | tf_op jit(solution)/shard_map/add | solution.py:265
  (17 shorter events, 0.2 us)
Async XLA Ops:
  0.0 7.2 %collective-permute-start = (bf16[2,32,256]{2,1,0:T(8,128)(2,1)}, bf16[2,32,256]{2,1,0:T(8,128)(2,1)S(1)}, u32[]{:S(2)}, u32[]{:S(2)}) collective-permute-start(bf16[2,32,256]{2,1,0:T(8,128)(2,1)} %from_ref.1), channel_id=1, source_target_pairs={{0,6},{1,7},{2,4},{3,5},{4,2},{5,3},{6,0},{7,1},{8,14},{9,15},{10,... | collective-permute-start | bytes 98312 | tf_op jit(solution)/shard_map/ppermute | solution.py:244
  5.0 5.0 %collective-permute-start.2 = (bf16[2,32,256]{2,1,0:T(8,128)(2,1)}, bf16[2,32,256]{2,1,0:T(8,128)(2,1)S(1)}, u32[]{:S(2)}, u32[]{:S(2)}) collective-permute-start(bf16[2,32,256]{2,1,0:T(8,128)(2,1)} %from_ref.1), channel_id=1, source_target_pairs={{0,4},{1,5},{2,6},{3,7},{4,0},{5,1},{6,2},{7,3},{8,12},{9,13},{10,... | collective-permute-start | bytes 98312 | tf_op jit(solution)/shard_map/ppermute | solution.py:244
  5.1 5.0 %collective-permute-start.1 = (bf16[2,32,256]{2,1,0:T(8,128)(2,1)}, bf16[2,32,256]{2,1,0:T(8,128)(2,1)S(1)}, u32[]{:S(2)}, u32[]{:S(2)}) collective-permute-start(bf16[2,32,256]{2,1,0:T(8,128)(2,1)} %from_ref.1), channel_id=1, source_target_pairs={{0,2},{1,3},{2,0},{3,1},{4,6},{5,7},{6,4},{7,5},{8,10},{9,11},{10,... | collective-permute-start | bytes 98312 | tf_op jit(solution)/shard_map/ppermute | solution.py:244
  5.6 0.8 %copy-start.1 = (bf16[2,32,256]{2,1,0:T(8,128)(2,1)S(1)}, bf16[2,32,256]{2,1,0:T(8,128)(2,1)}, u32[]{:S(2)}) copy-start(bf16[2,32,256]{2,1,0:T(8,128)(2,1)} %from_ref.1) | copy-start | bytes 98308
  10.1 7.3 %collective-permute-start.5 = (bf16[4,2,32,256]{3,2,1,0:T(8,128)(2,1)S(1)}, bf16[4,2,32,256]{3,2,1,0:T(8,128)(2,1)S(1)}, u32[]{:S(2)}, u32[]{:S(2)}) collective-permute-start(bf16[4,2,32,256]{3,2,1,0:T(8,128)(2,1)S(1)} %shard_map.84.refs_0_), channel_id=1, source_target_pairs={{0,17},{1,16},{2,19},{3,18},{4,21},{5,20},{6,23},{7,22},{8,25},{9,... | collective-permute-start | bytes 393224 | tf_op jit(solution)/shard_map/ppermute | solution.py:244
  12.6 5.6 %collective-permute-start.4 = (bf16[4,2,32,256]{3,2,1,0:T(8,128)(2,1)S(1)}, bf16[4,2,32,256]{3,2,1,0:T(8,128)(2,1)S(1)}, u32[]{:S(2)}, u32[]{:S(2)}) collective-permute-start(bf16[4,2,32,256]{3,2,1,0:T(8,128)(2,1)S(1)} %shard_map.84.refs_0_), channel_id=1, source_target_pairs={{0,16},{1,17},{2,18},{3,19},{4,20},{5,21},{6,22},{7,23},{8,24},{9,... | collective-permute-start | bytes 393224 | tf_op jit(solution)/shard_map/ppermute | solution.py:244
  13.1 5.1 %collective-permute-start.3 = (bf16[4,2,32,256]{3,2,1,0:T(8,128)(2,1)S(1)}, bf16[4,2,32,256]{3,2,1,0:T(8,128)(2,1)S(1)}, u32[]{:S(2)}, u32[]{:S(2)}) collective-permute-start(bf16[4,2,32,256]{3,2,1,0:T(8,128)(2,1)S(1)} %shard_map.84.refs_0_), channel_id=1, source_target_pairs={{0,1},{1,0},{2,3},{3,2},{4,5},{5,4},{6,7},{7,6},{8,9},{9,8},{10,11... | collective-permute-start | bytes 393224 | tf_op jit(solution)/shard_map/ppermute | solution.py:244
  14.4 0.7 %copy-start.3 = (s32[4,8,4,1]{1,3,2,0:T(1,128)S(1)}, s32[4,8,4,1]{1,3,2,0:T(1,128)}, u32[]{:S(2)}) copy-start(s32[4,8,4,1]{1,3,2,0:T(1,128)} %param.11) | copy-start | bytes 1540
  15.1 3.3 %copy-start = (bf16[8,256,256]{2,1,0:T(8,128)(2,1)S(1)}, bf16[8,256,256]{2,1,0:T(8,128)(2,1)}, u32[]{:S(2)}) copy-start(bf16[8,256,256]{2,1,0:T(8,128)(2,1)} %left_ref.3) | copy-start | bytes 3145732
  15.9 4.0 %copy-start.2 = (bf16[8,256,256]{2,1,0:T(8,128)(2,1)S(1)}, bf16[8,256,256]{2,1,0:T(8,128)(2,1)}, u32[]{:S(2)}) copy-start(bf16[8,256,256]{2,1,0:T(8,128)(2,1)} %right_ref.1) | copy-start | bytes 3145732
  18.3 1.6 %collective-permute-start.6 = (bf16[2,256,256]{2,1,0:T(8,128)(2,1)S(1)}, bf16[2,256,256]{2,1,0:T(8,128)(2,1)S(1)}, u32[]{:S(2)}, u32[]{:S(2)}) collective-permute-start(bf16[2,256,256]{2,1,0:T(8,128)(2,1)S(1)} %bitcast.17), channel_id=1, source_target_pairs={{0,8},{1,9},{2,10},{3,11},{4,12},{5,13},{6,14},{7,15},{8,0},{9,1},... | collective-permute-start | bytes 786440 | tf_op jit(solution)/shard_map/ppermute | solution.py:244
  21.9 5.4 %collective-permute-start.9 = (bf16[3,2,32,256]{3,2,1,0:T(8,128)(2,1)S(1)}, bf16[3,2,32,256]{3,2,1,0:T(8,128)(2,1)S(1)}, u32[]{:S(2)}, u32[]{:S(2)}) collective-permute-start(bf16[3,2,32,256]{3,2,1,0:T(8,128)(2,1)S(1)} %get-tuple-element.22), channel_id=1, source_target_pairs={{0,1},{1,0},{2,3},{3,2},{4,5},{5,4},{6,7},{7,6},{8,9},{9,8},{10,11... | collective-permute-start | bytes 294920 | tf_op jit(solution)/shard_map/ppermute | solution.py:244
  23.0 6.3 %collective-permute-start.8 = (bf16[2,32,256]{2,1,0:T(8,128)(2,1)S(1)}, bf16[2,32,256]{2,1,0:T(8,128)(2,1)S(1)}, u32[]{:S(2)}, u32[]{:S(2)}) collective-permute-start(bf16[2,32,256]{2,1,0:T(8,128)(2,1)S(1)} %bitcast.19), channel_id=1, source_target_pairs={{0,6},{1,7},{2,4},{3,5},{4,2},{5,3},{6,0},{7,1},{8,14},{9,15},{10,... | collective-permute-start | bytes 98312 | tf_op jit(solution)/shard_map/ppermute | solution.py:244
  24.8 6.6 %collective-permute-start.7 = (bf16[2,32,256]{2,1,0:T(8,128)(2,1)S(1)}, bf16[2,32,256]{2,1,0:T(8,128)(2,1)S(1)}, u32[]{:S(2)}, u32[]{:S(2)}) collective-permute-start(bf16[2,32,256]{2,1,0:T(8,128)(2,1)S(1)} %bitcast.18), channel_id=1, source_target_pairs={{0,7},{1,6},{2,5},{3,4},{4,3},{5,2},{6,1},{7,0},{8,15},{9,14},{10,... | collective-permute-start | bytes 98312 | tf_op jit(solution)/shard_map/ppermute | solution.py:244
  27.2 4.2 %collective-permute-start.10 = (bf16[2,32,256]{2,1,0:T(8,128)(2,1)S(1)}, bf16[2,32,256]{2,1,0:T(8,128)(2,1)S(1)}, u32[]{:S(2)}, u32[]{:S(2)}) collective-permute-start(bf16[2,32,256]{2,1,0:T(8,128)(2,1)S(1)} %get-tuple-element.23), channel_id=1, source_target_pairs={{0,2},{1,3},{2,0},{3,1},{4,6},{5,7},{6,4},{7,5},{8,10},{9,11},{10,... | collective-permute-start | bytes 98312 | tf_op jit(solution)/shard_map/ppermute | solution.py:244
  27.3 4.9 %collective-permute-start.11 = (bf16[2,32,256]{2,1,0:T(8,128)(2,1)S(1)}, bf16[2,32,256]{2,1,0:T(8,128)(2,1)S(1)}, u32[]{:S(2)}, u32[]{:S(2)}) collective-permute-start(bf16[2,32,256]{2,1,0:T(8,128)(2,1)S(1)} %get-tuple-element.24), channel_id=1, source_target_pairs={{0,4},{1,5},{2,6},{3,7},{4,0},{5,1},{6,2},{7,3},{8,12},{9,13},{10,... | collective-permute-start | bytes 98312 | tf_op jit(solution)/shard_map/ppermute | solution.py:244

commit v7 on v6

--- a/solution.py
+++ b/solution.py
@@ -36,18 +36,17 @@
 def prepare_kernel(n_left, n_right, held, listed_ref, code_ref, choice_ref, weight_ref):
     n_pair, n_cell = weight_ref.shape[1] // CHUNK, weight_ref.shape[0] // CHUNK
     me, my_op = lax.axis_index("sec"), lax.axis_index("op")
-    core = lax.rem(me, 2)
     for t in range(2):
         for y in range(choice_ref.shape[1]):
-            source = 2 * y + core
+            source = jnp.bitwise_xor(me, 2 * y)
             choice = listed_ref[source, jnp.bitwise_xor(me, t), 0, my_op] - source * held
             choice_ref[t, y] = jnp.full(choice_ref.shape[2:], choice.astype(jnp.float32)).astype(BF16)
 
     code = code_ref[...]
     cell, code = lax.rem(code, n_cell), lax.div(code, n_cell)
     left, slot = lax.rem(code, n_left), lax.div(code, n_left)
-    other = jnp.bitwise_xor(lax.rem(slot, 2), core)
-    pair = (other * (n_pair // (2 * n_left)) + lax.div(slot, 2)) * n_left + left
+    slot = jnp.bitwise_xor(slot, me)
+    pair = (lax.rem(slot, 2) * (n_pair // (2 * n_left)) + lax.div(slot, 2)) * n_left + left
     n_term = cell.shape[1]
     row_cell = lax.broadcasted_iota(jnp.int32, (n_cell * CHUNK, n_term), 0) // CHUNK
     row_pair = lax.broadcasted_iota(jnp.int32, (n_pair * CHUNK, n_term), 0) // CHUNK
@@ -95,33 +94,34 @@
 
 
 def split_kernel(n_lo, choice_ref, *refs):
-    pieces, (keep_ref, give_ref) = refs[:-2], refs[-2:]
+    pieces, (keep_ref, first_ref, rest_ref) = refs[:-3], refs[-3:]
     n_hi, held = pieces[0].shape[:2]
-    my_y = lax.div(lax.axis_index("sec"), 2)
     my_op = lax.axis_index("op")
     for q, piece in enumerate(pieces):
-        y = jnp.bitwise_xor(my_y, q // n_lo)
+        y = q // n_lo
         choices = [choice_ref[t, y] for t in range(2)]
+        give = (first_ref, 0) if y == 0 else (rest_ref, y - 1)
         for k in range(n_hi):
             o = jnp.bitwise_xor(my_op, k * n_lo + q % n_lo)
-            for choice, out_ref in zip(choices, (keep_ref, give_ref)):
+            for choice, (out_ref, place) in zip(choices, ((keep_ref, y), give)):
                 block = piece[k, 0]
                 for i in range(1, held):
                     block = jnp.where(choice == i, piece[k, i], block)
-                out_ref[y, o] = block
+                out_ref[place, o] = block
 
 
 def split(choice, pieces, n_lo):
     n_hi, held, rows, width = pieces[0].shape
-    out = jax.ShapeDtypeStruct((choice.shape[1], n_hi * n_lo, rows, width), BF16)
-    return pl.pallas_call(
+    n_y = choice.shape[1]
+    outs = pl.pallas_call(
         functools.partial(split_kernel, n_lo),
-        out_shape=[out, out],
+        out_shape=[jax.ShapeDtypeStruct((y, n_hi * n_lo, rows, width), BF16) for y in (n_y, 1, n_y - 1)],
         in_specs=[VMEM] * (1 + len(pieces)),
-        out_specs=[VMEM] * 2,
+        out_specs=[VMEM] * 3,
         compiler_params=pltpu.CompilerParams(vmem_limit_bytes=8 * 1024 * 1024),
         cost_estimate=pl.CostEstimate(flops=10**6, bytes_accessed=2 * 10**6, transcendentals=0),
     )(choice, *pieces)
+    return [x.reshape(x.shape[0], width, width) for x in outs]
 
 
 def halves(left_ref, table_ref, half_ref):
@@ -148,7 +148,7 @@
     )(left, table)
 
 
-def terms_kernel(n_lo, keys, left_ref, right_ref, weight_ref, first_ref, table_ref, *refs):
+def terms_kernel(n_lo, keys, left_ref, right_ref, weight_ref, first_ref, second_ref, table_ref, *refs):
     outs, (half_ref, sum_ref, total_ref) = refs[:-3], refs[-3:]
     width, n_right = left_ref.shape[1], right_ref.shape[0]
     held = sum_ref.shape[0] // width
@@ -156,7 +156,7 @@
     halves(left_ref, table_ref, half_ref)
 
     for m in range(0, chunks, 2):
-        two = [jnp.dot(weight_ref[...], jnp.concatenate([first_ref[m + i], half_ref[m + i]], axis=0),
+        two = [jnp.dot(weight_ref[...], jnp.concatenate([x[m + i] for x in (first_ref, second_ref, half_ref)], axis=0),
                        preferred_element_type=jnp.float32) for i in range(2)]
         for j in range(held):
             for r in range(n_right):
@@ -176,18 +176,20 @@
         outs[0][...] = total_ref[...]
         return
     me = lax.axis_index("op")
-    for (k, i), (out_ref, place) in zip(keys, [(x, p) for x in outs for p in range(x.shape[0])]):
+    core = lax.rem(lax.axis_index("sec"), 2)
+    for (even, odd, i), (out_ref, place) in zip(keys, [(x, p) for x in outs for p in range(x.shape[0])]):
         rows = out_ref.shape[2]
+        k = jnp.where(core == 0, even, odd)
         start = pl.multiple_of(jnp.bitwise_xor(me, k * n_lo + i) * rows, rows)
         for j in range(held):
             out_ref[place, j] = total_ref[j, pl.ds(start, rows), :].astype(out_ref.dtype)
 
 
-def terms(first, table, left, right, weight, held, n_op, n_lo, staged, direct):
+def terms(first, second, table, left, right, weight, held, n_op, n_lo, staged, direct):
     n_slot, width, _ = table.shape
     n_left, n_right = left.shape[0], right.shape[0]
     rows, n_hi = width // n_op, n_op // n_lo
-    groups = [[(k, i) for k in staged] for i in range(n_lo)] + [[(direct, i)] for i in range(n_lo)]
+    groups = [[(*k, i) for k in staged] for i in range(n_lo)] + [[(*direct, i)] for i in range(n_lo)]
     types = [BF16 if p else jnp.float32 for p in range(len(groups))]
     if rows % 16 == 0:
         keys = sum(groups, [])
@@ -200,7 +202,7 @@
     outs = pl.pallas_call(
         functools.partial(terms_kernel, n_lo, keys),
         out_shape=out_shape,
-        in_specs=[VMEM] * 5,
+        in_specs=[VMEM] * 6,
         out_specs=[VMEM] * len(out_shape),
         scratch_shapes=[
             pltpu.VMEM((width // CHUNK, n_pair * CHUNK, width), BF16),
@@ -209,11 +211,16 @@
         ],
         compiler_params=pltpu.CompilerParams(vmem_limit_bytes=2 * width * width * blocks + 12 * 1024 * 1024),
         cost_estimate=pl.CostEstimate(flops=3 * 10**9, bytes_accessed=4 * 10**6, transcendentals=0),
-    )(left, right, weight, first, table)
+    )(left, right, weight, first, second, table)
     if not keys:
         whole, me = outs[0].reshape(held, n_op, rows, width), lax.axis_index("op")
-        part = [lax.dynamic_index_in_dim(whole, me ^ o, axis=1, keepdims=False) for o in range(n_op)]
-        outs = [jnp.stack([part[k * n_lo + i] for k, i in group]).astype(x) for group, x in zip(groups, types)]
+        core = lax.rem(lax.axis_index("sec"), 2)
+
+        def part(even, odd, i):
+            o = me ^ (jnp.where(core == 0, even, odd) * n_lo + i)
+            return lax.dynamic_index_in_dim(whole, o, axis=1, keepdims=False)
+
+        outs = [jnp.stack([part(*key) for key in group]).astype(x) for group, x in zip(groups, types)]
     return outs
 
 
@@ -248,20 +255,23 @@
     pieces = [mine] + [swap(mine, 2 * (q // n_lo), q % n_lo) for q in range(1, n_y * n_lo)]
     choice, weight = prepare(
         send_list, term_slot, term_out, left_pick, right_pick, held, rows, width, left_ops.shape[0], right_ops.shape[0])
-    keep, give = (x.reshape(n_y, width, width) for x in split(choice, pieces, n_lo))
-    got = swap(give, 1, 0)
-    first = first_halves(keep, left_ops)
-    direct = n_hi - 1
-    staged = [k for k in range(n_hi) if k != direct]
-    own, other, *far = terms(first, got, left_ops, right_ops, weight, held, n_op, n_lo, staged, direct)
+    keep, *give = split(choice, pieces, n_lo)
+    got = [swap(x, 1, 0) for x in give]
+    first, second = first_halves(keep, left_ops), first_halves(got[0], left_ops)
+    def meet(x, k, i):
+        pairs = [(s * n_op + o, s * n_op + (o ^ (k[s % 2] * n_lo + i))) for s in range(n_sec) for o in range(n_op)]
+        return lax.ppermute(x, ("sec", "op"), pairs)
+
+    direct = (n_hi - 1, 1)
+    staged = list(zip(range(n_hi - 1), [0, *range(n_hi - 1, 1, -1)]))
+    own, other, *far = terms(first, second, got[1], left_ops, right_ops, weight, held, n_op, n_lo, staged, direct)
     total = None
     for i in range(n_lo - 1, -1, -1):
-        part = swap(far[i][0], 0, direct * n_lo + i).astype(jnp.float32)
+        part = meet(far[i][0], direct, i).astype(jnp.float32)
         total = part if total is None else total + part
     other = swap(other, 0, 1)
-    sums = dict(zip(staged[1:], combine(own, other)))
-    for k in staged[1:]:
-        total = total + swap(sums[k], 0, k * n_lo).astype(jnp.float32)
+    for k, part in zip(staged[1:], combine(own, other)):
+        total = total + meet(part, k, 0).astype(jnp.float32)
     return total + own[0] + other[0].astype(jnp.float32)
 
 

time: 33.1 us -> 33.1 us (level)
  waiting for transfers between devices: 9.61 us -> 8.95 us
  starting transfers between devices: 16.6 us -> 17.1 us
    ppermute x0 -> x4, starting transfers between devices: none -> 6.25 us  [meet(): return lax.ppermute(x, ('sec', 'op'), pairs)]
    ppermute x12 -> x9, starting transfers between devices: 16.6 us -> 10.9 us  [swap(): return lax.ppermute(x, ('sec', 'op'), pairs)]
    ppermute x12 -> x9, waiting for transfers between devices: 9.61 us -> 6.06 us  [swap(): return lax.ppermute(x, ('sec', 'op'), pairs)]
    ppermute x0 -> x4, waiting for transfers between devices: none -> 2.89 us  [meet(): return lax.ppermute(x, ('sec', 'op'), pairs)]
    pallas_call x1 -> x2, Pallas kernels: 0.71 us -> 1.14 us  [first_halves(): pl.pallas_call(halves, out_shape=jax.ShapeDtypeStruct((width // CHUNK, n_...]
  transfers between devices with their start and end apart: 12 -> 13, of which waited for: 7 -> 7; matrix products, arithmetic and copies ran while one was open for 2% -> 2% of each run, Pallas kernels for 5% -> 6%
where the time goes in v7:
time: 33.1 us; the launch traced here: 32.8 us
  starting transfers between devices  17.1 us (52%)
  waiting for transfers between devices  8.95 us (27%)
  Pallas kernels  3.8 us (11%)
  local copies, waits for them, and re-layouts  1.49 us (5%)
  other arithmetic  1.37 us (4%)
    ppermute x9, starting transfers between devices, swap(): return lax.ppermute(x, ('sec', 'op'), pairs)  10.9 us
    ppermute x4, starting transfers between devices, meet(): return lax.ppermute(x, ('sec', 'op'), pairs)  6.25 us
    ppermute x9, waiting for transfers between devices, swap(): return lax.ppermute(x, ('sec', 'op'), pairs)  6.06 us
    ppermute x4, waiting for transfers between devices, meet(): return lax.ppermute(x, ('sec', 'op'), pairs)  2.89 us
    pallas_call x1, Pallas kernels, terms(): pl.pallas_call(functools.partial(terms_kernel, n_lo, keys), out_shape=out...  1.7 us
    unnamed x8, local copies, waits for them, and re-layouts  1.49 us
    pallas_call x2, Pallas kernels, first_halves(): pl.pallas_call(halves, out_shape=jax.ShapeDtypeStruct((width // CHUNK, n_...  1.14 us
    pallas_call x1, Pallas kernels, prepare(): pl.pallas_call(functools.partial(prepare_kernel, n_left, n_right, held),...  0.85 us
  transfers between devices with their start and end apart: 13, of which 7 were waited for; matrix products, arithmetic and copies ran while one was open for 2% of the time, Pallas kernels for 6%

profile of v7, /device:TPU:0, one launch (start us, length us, event | category | flops | bytes accessed | tf_op | source)
XLA Modules:
  0.0 32.8 jit_solution(3297325177102745219)
XLA Ops:
  0.0 5.0 %collective-permute-start = (bf16[2,32,256]{2,1,0:T(8,128)(2,1)}, bf16[2,32,256]{2,1,0:T(8,128)(2,1)S(1)}, u32[]{:S(2)}, u32[]{:S(2)}) collective-permute-start(bf16[2,32,256]{2,1,0:T(8,128)(2,1)} %from_ref.1), channel_id=1, source_target_pairs={{0,6},{1,7},{2,4},{3,5},{4,2},{5,3},{6,0},{7,1},{8,14},{9,15},{10,... | collective-permute-start | bytes 98312 | tf_op jit(solution)/shard_map/ppermute | solution.py:251
  5.1 0.6 %collective-permute-start.1 = (bf16[2,32,256]{2,1,0:T(8,128)(2,1)}, bf16[2,32,256]{2,1,0:T(8,128)(2,1)S(1)}, u32[]{:S(2)}, u32[]{:S(2)}) collective-permute-start(bf16[2,32,256]{2,1,0:T(8,128)(2,1)} %from_ref.1), channel_id=1, source_target_pairs={{0,2},{1,3},{2,0},{3,1},{4,6},{5,7},{6,4},{7,5},{8,10},{9,11},{10,... | collective-permute-start | bytes 98312 | tf_op jit(solution)/shard_map/ppermute | solution.py:251
  5.6 0.8 %copy-done.1 = bf16[2,32,256]{2,1,0:T(8,128)(2,1)S(1)} copy-done((bf16[2,32,256]{2,1,0:T(8,128)(2,1)S(1)}, bf16[2,32,256]{2,1,0:T(8,128)(2,1)}, u32[]{:S(2)}) %copy-start.1) | copy-done | bytes 32792
  6.4 0.7 %collective-permute-done.refs_1_ = bf16[2,32,256]{2,1,0:T(8,128)(2,1)S(1)} collective-permute-done((bf16[2,32,256]{2,1,0:T(8,128)(2,1)}, bf16[2,32,256]{2,1,0:T(8,128)(2,1)S(1)}, u32[]{:S(2)}, u32[]{:S(2)}) %collective-permute-start) | collective-permute-done | bytes 32800 | tf_op jit(solution)/shard_map/ppermute | solution.py:251
  7.2 2.9 %collective-permute-done.2.refs_3_ = bf16[2,32,256]{2,1,0:T(8,128)(2,1)S(1)} collective-permute-done((bf16[2,32,256]{2,1,0:T(8,128)(2,1)}, bf16[2,32,256]{2,1,0:T(8,128)(2,1)S(1)}, u32[]{:S(2)}, u32[]{:S(2)}) %collective-permute-start.2) | collective-permute-done | bytes 32800 | tf_op jit(solution)/shard_map/ppermute | solution.py:251
  10.1 2.5 %collective-permute-start.5 = (bf16[4,2,32,256]{3,2,1,0:T(8,128)(2,1)S(1)}, bf16[4,2,32,256]{3,2,1,0:T(8,128)(2,1)S(1)}, u32[]{:S(2)}, u32[]{:S(2)}) collective-permute-start(bf16[4,2,32,256]{3,2,1,0:T(8,128)(2,1)S(1)} %shard_map.84.refs_0_), channel_id=1, source_target_pairs={{0,17},{1,16},{2,19},{3,18},{4,21},{5,20},{6,23},{7,22},{8,25},{9,... | collective-permute-start | bytes 393224 | tf_op jit(solution)/shard_map/ppermute | solution.py:251
  12.6 0.5 %collective-permute-start.4 = (bf16[4,2,32,256]{3,2,1,0:T(8,128)(2,1)S(1)}, bf16[4,2,32,256]{3,2,1,0:T(8,128)(2,1)S(1)}, u32[]{:S(2)}, u32[]{:S(2)}) collective-permute-start(bf16[4,2,32,256]{3,2,1,0:T(8,128)(2,1)S(1)} %shard_map.84.refs_0_), channel_id=1, source_target_pairs={{0,16},{1,17},{2,18},{3,19},{4,20},{5,21},{6,22},{7,23},{8,24},{9,... | collective-permute-start | bytes 393224 | tf_op jit(solution)/shard_map/ppermute | solution.py:251
  13.1 0.5 %collective-permute-start.3 = (bf16[4,2,32,256]{3,2,1,0:T(8,128)(2,1)S(1)}, bf16[4,2,32,256]{3,2,1,0:T(8,128)(2,1)S(1)}, u32[]{:S(2)}, u32[]{:S(2)}) collective-permute-start(bf16[4,2,32,256]{3,2,1,0:T(8,128)(2,1)S(1)} %shard_map.84.refs_0_), channel_id=1, source_target_pairs={{0,1},{1,0},{2,3},{3,2},{4,5},{5,4},{6,7},{7,6},{8,9},{9,8},{10,11... | collective-permute-start | bytes 393224 | tf_op jit(solution)/shard_map/ppermute | solution.py:251
  13.6 0.7 %add_bitcast_fusion.code_ref = s32[1,64]{1,0:T(1,128)S(1)} fusion(s32[64]{0:T(128)} %param.15, s32[64]{0:T(128)} %param.13, s32[64]{0:T(128)} %param.14, s32[64]{0:T(128)} %param.12), kind=kLoop, calls=%fused_computation.3 | loop fusion | flops 384 | bytes 1280 | tf_op jit(solution)/shard_map/reshape | solution.py:76
  14.4 0.7 %copy-done.3 = s32[4,8,4,1]{1,3,2,0:T(1,128)S(1)} copy-done((s32[4,8,4,1]{1,3,2,0:T(1,128)S(1)}, s32[4,8,4,1]{1,3,2,0:T(1,128)}, u32[]{:S(2)}) %copy-start.3) | copy-done | bytes 536
  15.1 0.9 %shard_map.82 = (bf16[2,2,32,256]{3,2,1,0:T(8,128)(2,1)S(1)}, bf16[128,256]{1,0:T(8,128)(2,1)S(1)}) custom-call(s32[4,4,1,8]{3,2,1,0:T(1,128)S(1)} %bitcast.22, s32[1,64]{1,0:T(1,128)S(1)} %add_bitcast_fusion.code_ref), custom_call_target="tpu_custom_call" | custom-call | flops 1000000000 | bytes 4000000 | tf_op jit(solution)/shard_map/pallas_call | solution.py:66
  15.9 1.5 %collective-permute-done.5.refs_3_ = bf16[4,2,32,256]{3,2,1,0:T(8,128)(2,1)S(1)} collective-permute-done((bf16[4,2,32,256]{3,2,1,0:T(8,128)(2,1)S(1)}, bf16[4,2,32,256]{3,2,1,0:T(8,128)(2,1)S(1)}, u32[]{:S(2)}, u32[]{:S(2)}) %collective-permute-start.5) | collective-permute-done | bytes 131104 | tf_op jit(solution)/shard_map/ppermute | solution.py:251
  17.4 0.8 %collective-permute-done.4.refs_2_ = bf16[4,2,32,256]{3,2,1,0:T(8,128)(2,1)S(1)} collective-permute-done((bf16[4,2,32,256]{3,2,1,0:T(8,128)(2,1)S(1)}, bf16[4,2,32,256]{3,2,1,0:T(8,128)(2,1)S(1)}, u32[]{:S(2)}, u32[]{:S(2)}) %collective-permute-start.4) | collective-permute-done | bytes 131104 | tf_op jit(solution)/shard_map/ppermute | solution.py:251
  18.3 0.5 %collective-permute-start.7 = (bf16[1,256,256]{2,1,0:T(8,128)(2,1)S(1)}, bf16[1,256,256]{2,1,0:T(8,128)(2,1)S(1)}, u32[]{:S(2)}, u32[]{:S(2)}) collective-permute-start(bf16[1,256,256]{2,1,0:T(8,128)(2,1)S(1)} %bitcast.18), channel_id=1, source_target_pairs={{0,8},{1,9},{2,10},{3,11},{4,12},{5,13},{6,14},{7,15},{8,0},{9,1},... | collective-permute-start | bytes 393224 | tf_op jit(solution)/shard_map/ppermute | solution.py:251
  18.9 0.7 %shard_map.86.first_ref = bf16[32,128,256]{2,1,0:T(8,128)(2,1)S(1)} custom-call(bf16[8,256,256]{2,1,0:T(8,128)(2,1)S(1)} %copy-done, bf16[2,256,256]{2,1,0:T(8,128)(2,1)S(1)} %bitcast.17), custom_call_target="tpu_custom_call" | custom-call | flops 536870912 | bytes 1000000 | tf_op jit(solution)/shard_map/pallas_call | solution.py:141
  19.7 0.4 %shard_map.87.second_ref = bf16[32,64,256]{2,1,0:T(8,128)(2,1)S(1)} custom-call(bf16[8,256,256]{2,1,0:T(8,128)(2,1)S(1)} %copy-done, bf16[1,256,256]{2,1,0:T(8,128)(2,1)S(1)} %collective-permute-done.6.table_ref), custom_call_target="tpu_custom_call" | custom-call | flops 268435456 | bytes 1000000 | tf_op jit(solution)/shard_map/pallas_call | solution.py:141
  20.1 1.7 %shard_map.88 = (f32[3,2,32,256]{3,2,1,0:T(8,128)S(1)}, bf16[3,2,32,256]{3,2,1,0:T(8,128)(2,1)S(1)}, bf16[1,2,32,256]{3,2,1,0:T(8,128)(2,1)S(1)}, bf16[1,2,32,256]{3,2,1,0:T(8,128)(2,1)S(1)}) custom-call(bf16[8,256,256]{2,1,0:T(8,128)(2,1)S(1)} %copy-done, bf16[8,256,256]{2,1,0:T(8,128)(2,1)S(1)} %copy-done.2, ...), custom_call_target="tpu_custom_call" | custom-call | flops 3000000000 | bytes 4000000 | tf_op jit(solution)/shard_map/pallas_call | solution.py:202
  21.9 1.2 %collective-permute-start.10 = (bf16[3,2,32,256]{3,2,1,0:T(8,128)(2,1)S(1)}, bf16[3,2,32,256]{3,2,1,0:T(8,128)(2,1)S(1)}, u32[]{:S(2)}, u32[]{:S(2)}) collective-permute-start(bf16[3,2,32,256]{3,2,1,0:T(8,128)(2,1)S(1)} %get-tuple-element.24), channel_id=1, source_target_pairs={{0,1},{1,0},{2,3},{3,2},{4,5},{5,4},{6,7},{7,6},{8,9},{9,8},{10,11... | collective-permute-start | bytes 294920 | tf_op jit(solution)/shard_map/ppermute | solution.py:251
  23.0 1.8 %collective-permute-start.9 = (bf16[2,32,256]{2,1,0:T(8,128)(2,1)S(1)}, bf16[2,32,256]{2,1,0:T(8,128)(2,1)S(1)}, u32[]{:S(2)}, u32[]{:S(2)}) collective-permute-start(bf16[2,32,256]{2,1,0:T(8,128)(2,1)S(1)} %bitcast.21), channel_id=1, source_target_pairs={{0,6},{1,7},{2,4},{3,5},{4,2},{5,3},{6,0},{7,1},{8,10},{9,11},{10,... | collective-permute-start | bytes 98312 | tf_op jit(solution)/shard_map/ppermute | solution.py:263
  24.8 2.4 %collective-permute-start.8 = (bf16[2,32,256]{2,1,0:T(8,128)(2,1)S(1)}, bf16[2,32,256]{2,1,0:T(8,128)(2,1)S(1)}, u32[]{:S(2)}, u32[]{:S(2)}) collective-permute-start(bf16[2,32,256]{2,1,0:T(8,128)(2,1)S(1)} %bitcast.20), channel_id=1, source_target_pairs={{0,7},{1,6},{2,5},{3,4},{4,3},{5,2},{6,1},{7,0},{8,11},{9,10},{10,... | collective-permute-start | bytes 98312 | tf_op jit(solution)/shard_map/ppermute | solution.py:263
  27.3 2.0 %collective-permute-start.12 = (bf16[2,32,256]{2,1,0:T(8,128)(2,1)S(1)}, bf16[2,32,256]{2,1,0:T(8,128)(2,1)S(1)}, u32[]{:S(2)}, u32[]{:S(2)}) collective-permute-start(bf16[2,32,256]{2,1,0:T(8,128)(2,1)S(1)} %get-tuple-element.26), channel_id=1, source_target_pairs={{0,4},{1,5},{2,6},{3,7},{4,0},{5,1},{6,2},{7,3},{8,12},{9,13},{10,... | collective-permute-start | bytes 98312 | tf_op jit(solution)/shard_map/ppermute | solution.py:263
  29.3 2.5 %collective-permute-done.8 = bf16[2,32,256]{2,1,0:T(8,128)(2,1)S(1)} collective-permute-done((bf16[2,32,256]{2,1,0:T(8,128)(2,1)S(1)}, bf16[2,32,256]{2,1,0:T(8,128)(2,1)S(1)}, u32[]{:S(2)}, u32[]{:S(2)}) %collective-permute-start.8) | collective-permute-done | bytes 32800 | tf_op jit(solution)/shard_map/ppermute | solution.py:263
  31.8 0.4 %collective-permute-done.12 = bf16[2,32,256]{2,1,0:T(8,128)(2,1)S(1)} collective-permute-done((bf16[2,32,256]{2,1,0:T(8,128)(2,1)S(1)}, bf16[2,32,256]{2,1,0:T(8,128)(2,1)S(1)}, u32[]{:S(2)}, u32[]{:S(2)}) %collective-permute-start.12) | collective-permute-done | bytes 32800 | tf_op jit(solution)/shard_map/ppermute | solution.py:263
  32.2 0.7 %convert_add_fusion = f32[2,32,256]{2,1,0:T(8,128)} fusion(f32[3,2,32,256]{3,2,1,0:T(8,128)S(1)} %get-tuple-element.23.own_ref, bf16[2,32,256]{2,1,0:T(8,128)(2,1)S(1)} %collective-permute-done.12, bf16[2,32,256]{2,1,0:T(8,128)(2,1)S(1)} %collective-permute-done.11, bf16[2,32,256]{2,1,0:T(8,128)(2,1)S(1)} %collective-permute-done.9, ...), kind=kLoop, calls=%fused_computation | loop fusion | flops 163840 | bytes 294912 | tf_op jit(solution)/shard_map/add | solution.py:275
  (20 shorter events, 0.4 us)
Async XLA Ops:
  0.0 7.2 %collective-permute-start = (bf16[2,32,256]{2,1,0:T(8,128)(2,1)}, bf16[2,32,256]{2,1,0:T(8,128)(2,1)S(1)}, u32[]{:S(2)}, u32[]{:S(2)}) collective-permute-start(bf16[2,32,256]{2,1,0:T(8,128)(2,1)} %from_ref.1), channel_id=1, source_target_pairs={{0,6},{1,7},{2,4},{3,5},{4,2},{5,3},{6,0},{7,1},{8,14},{9,15},{10,... | collective-permute-start | bytes 98312 | tf_op jit(solution)/shard_map/ppermute | solution.py:251
  5.0 5.0 %collective-permute-start.2 = (bf16[2,32,256]{2,1,0:T(8,128)(2,1)}, bf16[2,32,256]{2,1,0:T(8,128)(2,1)S(1)}, u32[]{:S(2)}, u32[]{:S(2)}) collective-permute-start(bf16[2,32,256]{2,1,0:T(8,128)(2,1)} %from_ref.1), channel_id=1, source_target_pairs={{0,4},{1,5},{2,6},{3,7},{4,0},{5,1},{6,2},{7,3},{8,12},{9,13},{10,... | collective-permute-start | bytes 98312 | tf_op jit(solution)/shard_map/ppermute | solution.py:251
  5.1 5.0 %collective-permute-start.1 = (bf16[2,32,256]{2,1,0:T(8,128)(2,1)}, bf16[2,32,256]{2,1,0:T(8,128)(2,1)S(1)}, u32[]{:S(2)}, u32[]{:S(2)}) collective-permute-start(bf16[2,32,256]{2,1,0:T(8,128)(2,1)} %from_ref.1), channel_id=1, source_target_pairs={{0,2},{1,3},{2,0},{3,1},{4,6},{5,7},{6,4},{7,5},{8,10},{9,11},{10,... | collective-permute-start | bytes 98312 | tf_op jit(solution)/shard_map/ppermute | solution.py:251
  5.6 0.8 %copy-start.1 = (bf16[2,32,256]{2,1,0:T(8,128)(2,1)S(1)}, bf16[2,32,256]{2,1,0:T(8,128)(2,1)}, u32[]{:S(2)}) copy-start(bf16[2,32,256]{2,1,0:T(8,128)(2,1)} %from_ref.1) | copy-start | bytes 98308
  10.1 7.3 %collective-permute-start.5 = (bf16[4,2,32,256]{3,2,1,0:T(8,128)(2,1)S(1)}, bf16[4,2,32,256]{3,2,1,0:T(8,128)(2,1)S(1)}, u32[]{:S(2)}, u32[]{:S(2)}) collective-permute-start(bf16[4,2,32,256]{3,2,1,0:T(8,128)(2,1)S(1)} %shard_map.84.refs_0_), channel_id=1, source_target_pairs={{0,17},{1,16},{2,19},{3,18},{4,21},{5,20},{6,23},{7,22},{8,25},{9,... | collective-permute-start | bytes 393224 | tf_op jit(solution)/shard_map/ppermute | solution.py:251
  12.6 5.6 %collective-permute-start.4 = (bf16[4,2,32,256]{3,2,1,0:T(8,128)(2,1)S(1)}, bf16[4,2,32,256]{3,2,1,0:T(8,128)(2,1)S(1)}, u32[]{:S(2)}, u32[]{:S(2)}) collective-permute-start(bf16[4,2,32,256]{3,2,1,0:T(8,128)(2,1)S(1)} %shard_map.84.refs_0_), channel_id=1, source_target_pairs={{0,16},{1,17},{2,18},{3,19},{4,20},{5,21},{6,22},{7,23},{8,24},{9,... | collective-permute-start | bytes 393224 | tf_op jit(solution)/shard_map/ppermute | solution.py:251
  13.1 5.1 %collective-permute-start.3 = (bf16[4,2,32,256]{3,2,1,0:T(8,128)(2,1)S(1)}, bf16[4,2,32,256]{3,2,1,0:T(8,128)(2,1)S(1)}, u32[]{:S(2)}, u32[]{:S(2)}) collective-permute-start(bf16[4,2,32,256]{3,2,1,0:T(8,128)(2,1)S(1)} %shard_map.84.refs_0_), channel_id=1, source_target_pairs={{0,1},{1,0},{2,3},{3,2},{4,5},{5,4},{6,7},{7,6},{8,9},{9,8},{10,11... | collective-permute-start | bytes 393224 | tf_op jit(solution)/shard_map/ppermute | solution.py:251
  14.4 0.7 %copy-start.3 = (s32[4,8,4,1]{1,3,2,0:T(1,128)S(1)}, s32[4,8,4,1]{1,3,2,0:T(1,128)}, u32[]{:S(2)}) copy-start(s32[4,8,4,1]{1,3,2,0:T(1,128)} %param.11) | copy-start | bytes 1540
  15.1 3.8 %copy-start = (bf16[8,256,256]{2,1,0:T(8,128)(2,1)S(1)}, bf16[8,256,256]{2,1,0:T(8,128)(2,1)}, u32[]{:S(2)}) copy-start(bf16[8,256,256]{2,1,0:T(8,128)(2,1)} %left_ref.5) | copy-start | bytes 3145732
  18.3 1.4 %collective-permute-start.6 = (bf16[1,256,256]{2,1,0:T(8,128)(2,1)S(1)}, bf16[1,256,256]{2,1,0:T(8,128)(2,1)S(1)}, u32[]{:S(2)}, u32[]{:S(2)}) collective-permute-start(bf16[1,256,256]{2,1,0:T(8,128)(2,1)S(1)} %bitcast.19), channel_id=1, source_target_pairs={{0,8},{1,9},{2,10},{3,11},{4,12},{5,13},{6,14},{7,15},{8,0},{9,1},... | collective-permute-start | bytes 393224 | tf_op jit(solution)/shard_map/ppermute | solution.py:251
  18.3 1.8 %collective-permute-start.7 = (bf16[1,256,256]{2,1,0:T(8,128)(2,1)S(1)}, bf16[1,256,256]{2,1,0:T(8,128)(2,1)S(1)}, u32[]{:S(2)}, u32[]{:S(2)}) collective-permute-start(bf16[1,256,256]{2,1,0:T(8,128)(2,1)S(1)} %bitcast.18), channel_id=1, source_target_pairs={{0,8},{1,9},{2,10},{3,11},{4,12},{5,13},{6,14},{7,15},{8,0},{9,1},... | collective-permute-start | bytes 393224 | tf_op jit(solution)/shard_map/ppermute | solution.py:251
  18.8 1.3 %copy-start.2 = (bf16[8,256,256]{2,1,0:T(8,128)(2,1)S(1)}, bf16[8,256,256]{2,1,0:T(8,128)(2,1)}, u32[]{:S(2)}) copy-start(bf16[8,256,256]{2,1,0:T(8,128)(2,1)} %right_ref.1) | copy-start | bytes 3145732
  21.9 5.4 %collective-permute-start.10 = (bf16[3,2,32,256]{3,2,1,0:T(8,128)(2,1)S(1)}, bf16[3,2,32,256]{3,2,1,0:T(8,128)(2,1)S(1)}, u32[]{:S(2)}, u32[]{:S(2)}) collective-permute-start(bf16[3,2,32,256]{3,2,1,0:T(8,128)(2,1)S(1)} %get-tuple-element.24), channel_id=1, source_target_pairs={{0,1},{1,0},{2,3},{3,2},{4,5},{5,4},{6,7},{7,6},{8,9},{9,8},{10,11... | collective-permute-start | bytes 294920 | tf_op jit(solution)/shard_map/ppermute | solution.py:251
  23.0 6.3 %collective-permute-start.9 = (bf16[2,32,256]{2,1,0:T(8,128)(2,1)S(1)}, bf16[2,32,256]{2,1,0:T(8,128)(2,1)S(1)}, u32[]{:S(2)}, u32[]{:S(2)}) collective-permute-start(bf16[2,32,256]{2,1,0:T(8,128)(2,1)S(1)} %bitcast.21), channel_id=1, source_target_pairs={{0,6},{1,7},{2,4},{3,5},{4,2},{5,3},{6,0},{7,1},{8,10},{9,11},{10,... | collective-permute-start | bytes 98312 | tf_op jit(solution)/shard_map/ppermute | solution.py:263
  24.8 7.0 %collective-permute-start.8 = (bf16[2,32,256]{2,1,0:T(8,128)(2,1)S(1)}, bf16[2,32,256]{2,1,0:T(8,128)(2,1)S(1)}, u32[]{:S(2)}, u32[]{:S(2)}) collective-permute-start(bf16[2,32,256]{2,1,0:T(8,128)(2,1)S(1)} %bitcast.20), channel_id=1, source_target_pairs={{0,7},{1,6},{2,5},{3,4},{4,3},{5,2},{6,1},{7,0},{8,11},{9,10},{10,... | collective-permute-start | bytes 98312 | tf_op jit(solution)/shard_map/ppermute | solution.py:263
  27.2 4.6 %collective-permute-start.11 = (bf16[2,32,256]{2,1,0:T(8,128)(2,1)S(1)}, bf16[2,32,256]{2,1,0:T(8,128)(2,1)S(1)}, u32[]{:S(2)}, u32[]{:S(2)}) collective-permute-start(bf16[2,32,256]{2,1,0:T(8,128)(2,1)S(1)} %get-tuple-element.25), channel_id=1, source_target_pairs={{0,2},{1,3},{2,0},{3,1},{4,6},{5,7},{6,4},{7,5},{8,14},{9,15},{10,... | collective-permute-start | bytes 98312 | tf_op jit(solution)/shard_map/ppermute | solution.py:263
  27.3 4.9 %collective-permute-start.12 = (bf16[2,32,256]{2,1,0:T(8,128)(2,1)S(1)}, bf16[2,32,256]{2,1,0:T(8,128)(2,1)S(1)}, u32[]{:S(2)}, u32[]{:S(2)}) collective-permute-start(bf16[2,32,256]{2,1,0:T(8,128)(2,1)S(1)} %get-tuple-element.26), channel_id=1, source_target_pairs={{0,4},{1,5},{2,6},{3,7},{4,0},{5,1},{6,2},{7,3},{8,12},{9,13},{10,... | collective-permute-start | bytes 98312 | tf_op jit(solution)/shard_map/ppermute | solution.py:263

commit v8 on v6

--- a/solution.py
+++ b/solution.py
@@ -176,8 +176,10 @@
         outs[0][...] = total_ref[...]
         return
     me = lax.axis_index("op")
-    for (k, i), (out_ref, place) in zip(keys, [(x, p) for x in outs for p in range(x.shape[0])]):
+    core = lax.rem(lax.axis_index("sec"), 2)
+    for (even, odd, i), (out_ref, place) in zip(keys, [(x, p) for x in outs for p in range(x.shape[0])]):
         rows = out_ref.shape[2]
+        k = jnp.where(core == 0, even, odd)
         start = pl.multiple_of(jnp.bitwise_xor(me, k * n_lo + i) * rows, rows)
         for j in range(held):
             out_ref[place, j] = total_ref[j, pl.ds(start, rows), :].astype(out_ref.dtype)
@@ -187,7 +189,7 @@
     n_slot, width, _ = table.shape
     n_left, n_right = left.shape[0], right.shape[0]
     rows, n_hi = width // n_op, n_op // n_lo
-    groups = [[(k, i) for k in staged] for i in range(n_lo)] + [[(direct, i)] for i in range(n_lo)]
+    groups = [[(*k, i) for k in staged] for i in range(n_lo)] + [[(*direct, i)] for i in range(n_lo)]
     types = [BF16 if p else jnp.float32 for p in range(len(groups))]
     if rows % 16 == 0:
         keys = sum(groups, [])
@@ -212,8 +214,13 @@
     )(left, right, weight, first, table)
     if not keys:
         whole, me = outs[0].reshape(held, n_op, rows, width), lax.axis_index("op")
-        part = [lax.dynamic_index_in_dim(whole, me ^ o, axis=1, keepdims=False) for o in range(n_op)]
-        outs = [jnp.stack([part[k * n_lo + i] for k, i in group]).astype(x) for group, x in zip(groups, types)]
+        core = lax.rem(lax.axis_index("sec"), 2)
+
+        def part(even, odd, i):
+            o = me ^ (jnp.where(core == 0, even, odd) * n_lo + i)
+            return lax.dynamic_index_in_dim(whole, o, axis=1, keepdims=False)
+
+        outs = [jnp.stack([part(*key) for key in group]).astype(x) for group, x in zip(groups, types)]
     return outs
 
 
@@ -251,17 +258,20 @@
     keep, give = (x.reshape(n_y, width, width) for x in split(choice, pieces, n_lo))
     got = swap(give, 1, 0)
     first = first_halves(keep, left_ops)
-    direct = n_hi - 1
-    staged = [k for k in range(n_hi) if k != direct]
+    def meet(x, k, i):
+        pairs = [(s * n_op + o, s * n_op + (o ^ (k[s % 2] * n_lo + i))) for s in range(n_sec) for o in range(n_op)]
+        return lax.ppermute(x, ("sec", "op"), pairs)
+
+    direct = (n_hi - 1, 1)
+    staged = list(zip(range(n_hi - 1), [0, *range(n_hi - 1, 1, -1)]))
     own, other, *far = terms(first, got, left_ops, right_ops, weight, held, n_op, n_lo, staged, direct)
     total = None
     for i in range(n_lo - 1, -1, -1):
-        part = swap(far[i][0], 0, direct * n_lo + i).astype(jnp.float32)
+        part = meet(far[i][0], direct, i).astype(jnp.float32)
         total = part if total is None else total + part
     other = swap(other, 0, 1)
-    sums = dict(zip(staged[1:], combine(own, other)))
-    for k in staged[1:]:
-        total = total + swap(sums[k], 0, k * n_lo).astype(jnp.float32)
+    for k, part in zip(staged[1:], combine(own, other)):
+        total = total + meet(part, k, 0).astype(jnp.float32)
     return total + own[0] + other[0].astype(jnp.float32)
 
 

time: 33.1 us -> 33.1 us (level)
    ppermute x12 -> x8, starting transfers between devices: 16.6 us -> 10.4 us  [swap(): return lax.ppermute(x, ('sec', 'op'), pairs)]
    ppermute x0 -> x4, starting transfers between devices: none -> 6.24 us  [meet(): return lax.ppermute(x, ('sec', 'op'), pairs)]
    ppermute x0 -> x4, waiting for transfers between devices: none -> 2.89 us  [meet(): return lax.ppermute(x, ('sec', 'op'), pairs)]
    ppermute x12 -> x8, waiting for transfers between devices: 9.61 us -> 6.72 us  [swap(): return lax.ppermute(x, ('sec', 'op'), pairs)]
where the time goes in v8:
time: 33.1 us; the launch traced here: 32.8 us
  starting transfers between devices  16.6 us (50%)
  waiting for transfers between devices  9.61 us (29%)
  Pallas kernels  3.64 us (11%)
  local copies, waits for them, and re-layouts  1.5 us (5%)
  other arithmetic  1.37 us (4%)
    ppermute x8, starting transfers between devices, swap(): return lax.ppermute(x, ('sec', 'op'), pairs)  10.4 us
    ppermute x8, waiting for transfers between devices, swap(): return lax.ppermute(x, ('sec', 'op'), pairs)  6.72 us
    ppermute x4, starting transfers between devices, meet(): return lax.ppermute(x, ('sec', 'op'), pairs)  6.24 us
    ppermute x4, waiting for transfers between devices, meet(): return lax.ppermute(x, ('sec', 'op'), pairs)  2.89 us
    pallas_call x1, Pallas kernels, terms(): pl.pallas_call(functools.partial(terms_kernel, n_lo, keys), out_shape=out...  1.97 us
    unnamed x8, local copies, waits for them, and re-layouts  1.5 us
    pallas_call x1, Pallas kernels, prepare(): pl.pallas_call(functools.partial(prepare_kernel, n_left, n_right, held),...  0.85 us
    reshape x1, other arithmetic, prepare(): code.reshape(1, n_term)  0.71 us
  transfers between devices with their start and end apart: 12, of which 7 were waited for; matrix products, arithmetic and copies ran while one was open for 2% of the time, Pallas kernels for 5%

profile of v8, /device:TPU:0, one launch (start us, length us, event | category | flops | bytes accessed | tf_op | source)
XLA Modules:
  0.0 32.8 jit_solution(13013000488875282094)
XLA Ops:
  0.0 5.0 %collective-permute-start = (bf16[2,32,256]{2,1,0:T(8,128)(2,1)}, bf16[2,32,256]{2,1,0:T(8,128)(2,1)S(1)}, u32[]{:S(2)}, u32[]{:S(2)}) collective-permute-start(bf16[2,32,256]{2,1,0:T(8,128)(2,1)} %from_ref.1), channel_id=1, source_target_pairs={{0,6},{1,7},{2,4},{3,5},{4,2},{5,3},{6,0},{7,1},{8,14},{9,15},{10,... | collective-permute-start | bytes 98312 | tf_op jit(solution)/shard_map/ppermute | solution.py:251
  5.1 0.6 %collective-permute-start.1 = (bf16[2,32,256]{2,1,0:T(8,128)(2,1)}, bf16[2,32,256]{2,1,0:T(8,128)(2,1)S(1)}, u32[]{:S(2)}, u32[]{:S(2)}) collective-permute-start(bf16[2,32,256]{2,1,0:T(8,128)(2,1)} %from_ref.1), channel_id=1, source_target_pairs={{0,2},{1,3},{2,0},{3,1},{4,6},{5,7},{6,4},{7,5},{8,10},{9,11},{10,... | collective-permute-start | bytes 98312 | tf_op jit(solution)/shard_map/ppermute | solution.py:251
  5.6 0.8 %copy-done.1 = bf16[2,32,256]{2,1,0:T(8,128)(2,1)S(1)} copy-done((bf16[2,32,256]{2,1,0:T(8,128)(2,1)S(1)}, bf16[2,32,256]{2,1,0:T(8,128)(2,1)}, u32[]{:S(2)}) %copy-start.1) | copy-done | bytes 32792
  6.4 0.7 %collective-permute-done.refs_1_ = bf16[2,32,256]{2,1,0:T(8,128)(2,1)S(1)} collective-permute-done((bf16[2,32,256]{2,1,0:T(8,128)(2,1)}, bf16[2,32,256]{2,1,0:T(8,128)(2,1)S(1)}, u32[]{:S(2)}, u32[]{:S(2)}) %collective-permute-start) | collective-permute-done | bytes 32800 | tf_op jit(solution)/shard_map/ppermute | solution.py:251
  7.2 2.9 %collective-permute-done.2.refs_3_ = bf16[2,32,256]{2,1,0:T(8,128)(2,1)S(1)} collective-permute-done((bf16[2,32,256]{2,1,0:T(8,128)(2,1)}, bf16[2,32,256]{2,1,0:T(8,128)(2,1)S(1)}, u32[]{:S(2)}, u32[]{:S(2)}) %collective-permute-start.2) | collective-permute-done | bytes 32800 | tf_op jit(solution)/shard_map/ppermute | solution.py:251
  10.1 2.5 %collective-permute-start.5 = (bf16[4,2,32,256]{3,2,1,0:T(8,128)(2,1)S(1)}, bf16[4,2,32,256]{3,2,1,0:T(8,128)(2,1)S(1)}, u32[]{:S(2)}, u32[]{:S(2)}) collective-permute-start(bf16[4,2,32,256]{3,2,1,0:T(8,128)(2,1)S(1)} %shard_map.84.refs_0_), channel_id=1, source_target_pairs={{0,17},{1,16},{2,19},{3,18},{4,21},{5,20},{6,23},{7,22},{8,25},{9,... | collective-permute-start | bytes 393224 | tf_op jit(solution)/shard_map/ppermute | solution.py:251
  12.6 0.5 %collective-permute-start.4 = (bf16[4,2,32,256]{3,2,1,0:T(8,128)(2,1)S(1)}, bf16[4,2,32,256]{3,2,1,0:T(8,128)(2,1)S(1)}, u32[]{:S(2)}, u32[]{:S(2)}) collective-permute-start(bf16[4,2,32,256]{3,2,1,0:T(8,128)(2,1)S(1)} %shard_map.84.refs_0_), channel_id=1, source_target_pairs={{0,16},{1,17},{2,18},{3,19},{4,20},{5,21},{6,22},{7,23},{8,24},{9,... | collective-permute-start | bytes 393224 | tf_op jit(solution)/shard_map/ppermute | solution.py:251
  13.1 0.5 %collective-permute-start.3 = (bf16[4,2,32,256]{3,2,1,0:T(8,128)(2,1)S(1)}, bf16[4,2,32,256]{3,2,1,0:T(8,128)(2,1)S(1)}, u32[]{:S(2)}, u32[]{:S(2)}) collective-permute-start(bf16[4,2,32,256]{3,2,1,0:T(8,128)(2,1)S(1)} %shard_map.84.refs_0_), channel_id=1, source_target_pairs={{0,1},{1,0},{2,3},{3,2},{4,5},{5,4},{6,7},{7,6},{8,9},{9,8},{10,11... | collective-permute-start | bytes 393224 | tf_op jit(solution)/shard_map/ppermute | solution.py:251
  13.6 0.7 %add_bitcast_fusion.code_ref = s32[1,64]{1,0:T(1,128)S(1)} fusion(s32[64]{0:T(128)} %param.15, s32[64]{0:T(128)} %param.13, s32[64]{0:T(128)} %param.14, s32[64]{0:T(128)} %param.12), kind=kLoop, calls=%fused_computation.3 | loop fusion | flops 384 | bytes 1280 | tf_op jit(solution)/shard_map/reshape | solution.py:77
  14.4 0.7 %copy-done.3 = s32[4,8,4,1]{1,3,2,0:T(1,128)S(1)} copy-done((s32[4,8,4,1]{1,3,2,0:T(1,128)S(1)}, s32[4,8,4,1]{1,3,2,0:T(1,128)}, u32[]{:S(2)}) %copy-start.3) | copy-done | bytes 536
  15.1 0.9 %shard_map.82 = (bf16[2,2,32,256]{3,2,1,0:T(8,128)(2,1)S(1)}, bf16[128,256]{1,0:T(8,128)(2,1)S(1)}) custom-call(s32[4,4,1,8]{3,2,1,0:T(1,128)S(1)} %bitcast.20, s32[1,64]{1,0:T(1,128)S(1)} %add_bitcast_fusion.code_ref), custom_call_target="tpu_custom_call" | custom-call | flops 1000000000 | bytes 4000000 | tf_op jit(solution)/shard_map/pallas_call | solution.py:67
  15.9 1.5 %collective-permute-done.5.refs_3_ = bf16[4,2,32,256]{3,2,1,0:T(8,128)(2,1)S(1)} collective-permute-done((bf16[4,2,32,256]{3,2,1,0:T(8,128)(2,1)S(1)}, bf16[4,2,32,256]{3,2,1,0:T(8,128)(2,1)S(1)}, u32[]{:S(2)}, u32[]{:S(2)}) %collective-permute-start.5) | collective-permute-done | bytes 131104 | tf_op jit(solution)/shard_map/ppermute | solution.py:251
  17.4 0.8 %collective-permute-done.4.refs_2_ = bf16[4,2,32,256]{3,2,1,0:T(8,128)(2,1)S(1)} collective-permute-done((bf16[4,2,32,256]{3,2,1,0:T(8,128)(2,1)S(1)}, bf16[4,2,32,256]{3,2,1,0:T(8,128)(2,1)S(1)}, u32[]{:S(2)}, u32[]{:S(2)}) %collective-permute-start.4) | collective-permute-done | bytes 131104 | tf_op jit(solution)/shard_map/ppermute | solution.py:251
  18.4 0.7 %shard_map.86.first_ref = bf16[32,128,256]{2,1,0:T(8,128)(2,1)S(1)} custom-call(bf16[8,256,256]{2,1,0:T(8,128)(2,1)S(1)} %copy-done, bf16[2,256,256]{2,1,0:T(8,128)(2,1)S(1)} %bitcast.16), custom_call_target="tpu_custom_call" | custom-call | flops 536870912 | bytes 1000000 | tf_op jit(solution)/shard_map/pallas_call | solution.py:141
  19.1 0.8 %collective-permute-done.6.table_ref = bf16[2,256,256]{2,1,0:T(8,128)(2,1)S(1)} collective-permute-done((bf16[2,256,256]{2,1,0:T(8,128)(2,1)S(1)}, bf16[2,256,256]{2,1,0:T(8,128)(2,1)S(1)}, u32[]{:S(2)}, u32[]{:S(2)}) %collective-permute-start.6) | collective-permute-done | bytes 262176 | tf_op jit(solution)/shard_map/ppermute | solution.py:251
  19.9 2.0 %shard_map.87 = (f32[3,2,32,256]{3,2,1,0:T(8,128)S(1)}, bf16[3,2,32,256]{3,2,1,0:T(8,128)(2,1)S(1)}, bf16[1,2,32,256]{3,2,1,0:T(8,128)(2,1)S(1)}, bf16[1,2,32,256]{3,2,1,0:T(8,128)(2,1)S(1)}) custom-call(bf16[8,256,256]{2,1,0:T(8,128)(2,1)S(1)} %copy-done, bf16[8,256,256]{2,1,0:T(8,128)(2,1)S(1)} %copy-done.2, ...), custom_call_target="tpu_custom_call" | custom-call | flops 3000000000 | bytes 4000000 | tf_op jit(solution)/shard_map/pallas_call | solution.py:202
  21.9 1.2 %collective-permute-start.9 = (bf16[3,2,32,256]{3,2,1,0:T(8,128)(2,1)S(1)}, bf16[3,2,32,256]{3,2,1,0:T(8,128)(2,1)S(1)}, u32[]{:S(2)}, u32[]{:S(2)}) collective-permute-start(bf16[3,2,32,256]{3,2,1,0:T(8,128)(2,1)S(1)} %get-tuple-element.22), channel_id=1, source_target_pairs={{0,1},{1,0},{2,3},{3,2},{4,5},{5,4},{6,7},{7,6},{8,9},{9,8},{10,11... | collective-permute-start | bytes 294920 | tf_op jit(solution)/shard_map/ppermute | solution.py:251
  23.0 1.8 %collective-permute-start.8 = (bf16[2,32,256]{2,1,0:T(8,128)(2,1)S(1)}, bf16[2,32,256]{2,1,0:T(8,128)(2,1)S(1)}, u32[]{:S(2)}, u32[]{:S(2)}) collective-permute-start(bf16[2,32,256]{2,1,0:T(8,128)(2,1)S(1)} %bitcast.19), channel_id=1, source_target_pairs={{0,6},{1,7},{2,4},{3,5},{4,2},{5,3},{6,0},{7,1},{8,10},{9,11},{10,... | collective-permute-start | bytes 98312 | tf_op jit(solution)/shard_map/ppermute | solution.py:263
  24.8 2.4 %collective-permute-start.7 = (bf16[2,32,256]{2,1,0:T(8,128)(2,1)S(1)}, bf16[2,32,256]{2,1,0:T(8,128)(2,1)S(1)}, u32[]{:S(2)}, u32[]{:S(2)}) collective-permute-start(bf16[2,32,256]{2,1,0:T(8,128)(2,1)S(1)} %bitcast.18), channel_id=1, source_target_pairs={{0,7},{1,6},{2,5},{3,4},{4,3},{5,2},{6,1},{7,0},{8,11},{9,10},{10,... | collective-permute-start | bytes 98312 | tf_op jit(solution)/shard_map/ppermute | solution.py:263
  27.2 0.1 collective-permute-start.10
  27.3 2.0 %collective-permute-start.11 = (bf16[2,32,256]{2,1,0:T(8,128)(2,1)S(1)}, bf16[2,32,256]{2,1,0:T(8,128)(2,1)S(1)}, u32[]{:S(2)}, u32[]{:S(2)}) collective-permute-start(bf16[2,32,256]{2,1,0:T(8,128)(2,1)S(1)} %get-tuple-element.24), channel_id=1, source_target_pairs={{0,4},{1,5},{2,6},{3,7},{4,0},{5,1},{6,2},{7,3},{8,12},{9,13},{10,... | collective-permute-start | bytes 98312 | tf_op jit(solution)/shard_map/ppermute | solution.py:263
  29.3 2.5 %collective-permute-done.7 = bf16[2,32,256]{2,1,0:T(8,128)(2,1)S(1)} collective-permute-done((bf16[2,32,256]{2,1,0:T(8,128)(2,1)S(1)}, bf16[2,32,256]{2,1,0:T(8,128)(2,1)S(1)}, u32[]{:S(2)}, u32[]{:S(2)}) %collective-permute-start.7) | collective-permute-done | bytes 32800 | tf_op jit(solution)/shard_map/ppermute | solution.py:263
  31.8 0.4 %collective-permute-done.11 = bf16[2,32,256]{2,1,0:T(8,128)(2,1)S(1)} collective-permute-done((bf16[2,32,256]{2,1,0:T(8,128)(2,1)S(1)}, bf16[2,32,256]{2,1,0:T(8,128)(2,1)S(1)}, u32[]{:S(2)}, u32[]{:S(2)}) %collective-permute-start.11) | collective-permute-done | bytes 32800 | tf_op jit(solution)/shard_map/ppermute | solution.py:263
  32.2 0.7 %convert_add_fusion = f32[2,32,256]{2,1,0:T(8,128)} fusion(f32[3,2,32,256]{3,2,1,0:T(8,128)S(1)} %get-tuple-element.21.own_ref, bf16[2,32,256]{2,1,0:T(8,128)(2,1)S(1)} %collective-permute-done.11, bf16[2,32,256]{2,1,0:T(8,128)(2,1)S(1)} %collective-permute-done.10, bf16[2,32,256]{2,1,0:T(8,128)(2,1)S(1)} %collective-permute-done.8, ...), kind=kLoop, calls=%fused_computation | loop fusion | flops 163840 | bytes 294912 | tf_op jit(solution)/shard_map/add | solution.py:275
  (17 shorter events, 0.2 us)
Async XLA Ops:
  0.0 7.2 %collective-permute-start = (bf16[2,32,256]{2,1,0:T(8,128)(2,1)}, bf16[2,32,256]{2,1,0:T(8,128)(2,1)S(1)}, u32[]{:S(2)}, u32[]{:S(2)}) collective-permute-start(bf16[2,32,256]{2,1,0:T(8,128)(2,1)} %from_ref.1), channel_id=1, source_target_pairs={{0,6},{1,7},{2,4},{3,5},{4,2},{5,3},{6,0},{7,1},{8,14},{9,15},{10,... | collective-permute-start | bytes 98312 | tf_op jit(solution)/shard_map/ppermute | solution.py:251
  5.0 5.0 %collective-permute-start.2 = (bf16[2,32,256]{2,1,0:T(8,128)(2,1)}, bf16[2,32,256]{2,1,0:T(8,128)(2,1)S(1)}, u32[]{:S(2)}, u32[]{:S(2)}) collective-permute-start(bf16[2,32,256]{2,1,0:T(8,128)(2,1)} %from_ref.1), channel_id=1, source_target_pairs={{0,4},{1,5},{2,6},{3,7},{4,0},{5,1},{6,2},{7,3},{8,12},{9,13},{10,... | collective-permute-start | bytes 98312 | tf_op jit(solution)/shard_map/ppermute | solution.py:251
  5.1 5.0 %collective-permute-start.1 = (bf16[2,32,256]{2,1,0:T(8,128)(2,1)}, bf16[2,32,256]{2,1,0:T(8,128)(2,1)S(1)}, u32[]{:S(2)}, u32[]{:S(2)}) collective-permute-start(bf16[2,32,256]{2,1,0:T(8,128)(2,1)} %from_ref.1), channel_id=1, source_target_pairs={{0,2},{1,3},{2,0},{3,1},{4,6},{5,7},{6,4},{7,5},{8,10},{9,11},{10,... | collective-permute-start | bytes 98312 | tf_op jit(solution)/shard_map/ppermute | solution.py:251
  5.6 0.8 %copy-start.1 = (bf16[2,32,256]{2,1,0:T(8,128)(2,1)S(1)}, bf16[2,32,256]{2,1,0:T(8,128)(2,1)}, u32[]{:S(2)}) copy-start(bf16[2,32,256]{2,1,0:T(8,128)(2,1)} %from_ref.1) | copy-start | bytes 98308
  10.1 7.3 %collective-permute-start.5 = (bf16[4,2,32,256]{3,2,1,0:T(8,128)(2,1)S(1)}, bf16[4,2,32,256]{3,2,1,0:T(8,128)(2,1)S(1)}, u32[]{:S(2)}, u32[]{:S(2)}) collective-permute-start(bf16[4,2,32,256]{3,2,1,0:T(8,128)(2,1)S(1)} %shard_map.84.refs_0_), channel_id=1, source_target_pairs={{0,17},{1,16},{2,19},{3,18},{4,21},{5,20},{6,23},{7,22},{8,25},{9,... | collective-permute-start | bytes 393224 | tf_op jit(solution)/shard_map/ppermute | solution.py:251
  12.6 5.6 %collective-permute-start.4 = (bf16[4,2,32,256]{3,2,1,0:T(8,128)(2,1)S(1)}, bf16[4,2,32,256]{3,2,1,0:T(8,128)(2,1)S(1)}, u32[]{:S(2)}, u32[]{:S(2)}) collective-permute-start(bf16[4,2,32,256]{3,2,1,0:T(8,128)(2,1)S(1)} %shard_map.84.refs_0_), channel_id=1, source_target_pairs={{0,16},{1,17},{2,18},{3,19},{4,20},{5,21},{6,22},{7,23},{8,24},{9,... | collective-permute-start | bytes 393224 | tf_op jit(solution)/shard_map/ppermute | solution.py:251
  13.1 5.1 %collective-permute-start.3 = (bf16[4,2,32,256]{3,2,1,0:T(8,128)(2,1)S(1)}, bf16[4,2,32,256]{3,2,1,0:T(8,128)(2,1)S(1)}, u32[]{:S(2)}, u32[]{:S(2)}) collective-permute-start(bf16[4,2,32,256]{3,2,1,0:T(8,128)(2,1)S(1)} %shard_map.84.refs_0_), channel_id=1, source_target_pairs={{0,1},{1,0},{2,3},{3,2},{4,5},{5,4},{6,7},{7,6},{8,9},{9,8},{10,11... | collective-permute-start | bytes 393224 | tf_op jit(solution)/shard_map/ppermute | solution.py:251
  14.4 0.7 %copy-start.3 = (s32[4,8,4,1]{1,3,2,0:T(1,128)S(1)}, s32[4,8,4,1]{1,3,2,0:T(1,128)}, u32[]{:S(2)}) copy-start(s32[4,8,4,1]{1,3,2,0:T(1,128)} %param.11) | copy-start | bytes 1540
  15.1 3.3 %copy-start = (bf16[8,256,256]{2,1,0:T(8,128)(2,1)S(1)}, bf16[8,256,256]{2,1,0:T(8,128)(2,1)}, u32[]{:S(2)}) copy-start(bf16[8,256,256]{2,1,0:T(8,128)(2,1)} %left_ref.3) | copy-start | bytes 3145732
  15.9 4.0 %copy-start.2 = (bf16[8,256,256]{2,1,0:T(8,128)(2,1)S(1)}, bf16[8,256,256]{2,1,0:T(8,128)(2,1)}, u32[]{:S(2)}) copy-start(bf16[8,256,256]{2,1,0:T(8,128)(2,1)} %right_ref.1) | copy-start | bytes 3145732
  18.3 1.6 %collective-permute-start.6 = (bf16[2,256,256]{2,1,0:T(8,128)(2,1)S(1)}, bf16[2,256,256]{2,1,0:T(8,128)(2,1)S(1)}, u32[]{:S(2)}, u32[]{:S(2)}) collective-permute-start(bf16[2,256,256]{2,1,0:T(8,128)(2,1)S(1)} %bitcast.17), channel_id=1, source_target_pairs={{0,8},{1,9},{2,10},{3,11},{4,12},{5,13},{6,14},{7,15},{8,0},{9,1},... | collective-permute-start | bytes 786440 | tf_op jit(solution)/shard_map/ppermute | solution.py:251
  21.9 5.4 %collective-permute-start.9 = (bf16[3,2,32,256]{3,2,1,0:T(8,128)(2,1)S(1)}, bf16[3,2,32,256]{3,2,1,0:T(8,128)(2,1)S(1)}, u32[]{:S(2)}, u32[]{:S(2)}) collective-permute-start(bf16[3,2,32,256]{3,2,1,0:T(8,128)(2,1)S(1)} %get-tuple-element.22), channel_id=1, source_target_pairs={{0,1},{1,0},{2,3},{3,2},{4,5},{5,4},{6,7},{7,6},{8,9},{9,8},{10,11... | collective-permute-start | bytes 294920 | tf_op jit(solution)/shard_map/ppermute | solution.py:251
  23.0 6.3 %collective-permute-start.8 = (bf16[2,32,256]{2,1,0:T(8,128)(2,1)S(1)}, bf16[2,32,256]{2,1,0:T(8,128)(2,1)S(1)}, u32[]{:S(2)}, u32[]{:S(2)}) collective-permute-start(bf16[2,32,256]{2,1,0:T(8,128)(2,1)S(1)} %bitcast.19), channel_id=1, source_target_pairs={{0,6},{1,7},{2,4},{3,5},{4,2},{5,3},{6,0},{7,1},{8,10},{9,11},{10,... | collective-permute-start | bytes 98312 | tf_op jit(solution)/shard_map/ppermute | solution.py:263
  24.8 7.0 %collective-permute-start.7 = (bf16[2,32,256]{2,1,0:T(8,128)(2,1)S(1)}, bf16[2,32,256]{2,1,0:T(8,128)(2,1)S(1)}, u32[]{:S(2)}, u32[]{:S(2)}) collective-permute-start(bf16[2,32,256]{2,1,0:T(8,128)(2,1)S(1)} %bitcast.18), channel_id=1, source_target_pairs={{0,7},{1,6},{2,5},{3,4},{4,3},{5,2},{6,1},{7,0},{8,11},{9,10},{10,... | collective-permute-start | bytes 98312 | tf_op jit(solution)/shard_map/ppermute | solution.py:263
  27.2 4.6 %collective-permute-start.10 = (bf16[2,32,256]{2,1,0:T(8,128)(2,1)S(1)}, bf16[2,32,256]{2,1,0:T(8,128)(2,1)S(1)}, u32[]{:S(2)}, u32[]{:S(2)}) collective-permute-start(bf16[2,32,256]{2,1,0:T(8,128)(2,1)S(1)} %get-tuple-element.23), channel_id=1, source_target_pairs={{0,2},{1,3},{2,0},{3,1},{4,6},{5,7},{6,4},{7,5},{8,14},{9,15},{10,... | collective-permute-start | bytes 98312 | tf_op jit(solution)/shard_map/ppermute | solution.py:263
  27.3 4.9 %collective-permute-start.11 = (bf16[2,32,256]{2,1,0:T(8,128)(2,1)S(1)}, bf16[2,32,256]{2,1,0:T(8,128)(2,1)S(1)}, u32[]{:S(2)}, u32[]{:S(2)}) collective-permute-start(bf16[2,32,256]{2,1,0:T(8,128)(2,1)S(1)} %get-tuple-element.24), channel_id=1, source_target_pairs={{0,4},{1,5},{2,6},{3,7},{4,0},{5,1},{6,2},{7,3},{8,12},{9,13},{10,... | collective-permute-start | bytes 98312 | tf_op jit(solution)/shard_map/ppermute | solution.py:263

commit v9 on v6

--- a/solution.py
+++ b/solution.py
@@ -148,7 +148,7 @@
     )(left, table)
 
 
-def terms_kernel(n_lo, keys, left_ref, right_ref, weight_ref, first_ref, table_ref, *refs):
+def terms_kernel(n_lo, direct, keys, left_ref, right_ref, weight_ref, first_ref, table_ref, *refs):
     outs, (half_ref, sum_ref, total_ref) = refs[:-3], refs[-3:]
     width, n_right = left_ref.shape[1], right_ref.shape[0]
     held = sum_ref.shape[0] // width
@@ -175,9 +175,11 @@
     if not keys:
         outs[0][...] = total_ref[...]
         return
-    me = lax.axis_index("op")
+    me, core = lax.axis_index("op"), lax.rem(lax.axis_index("sec"), 2)
     for (k, i), (out_ref, place) in zip(keys, [(x, p) for x in outs for p in range(x.shape[0])]):
         rows = out_ref.shape[2]
+        if k == direct:
+            i = jnp.where(core == 0, i, n_lo - 1 - i)
         start = pl.multiple_of(jnp.bitwise_xor(me, k * n_lo + i) * rows, rows)
         for j in range(held):
             out_ref[place, j] = total_ref[j, pl.ds(start, rows), :].astype(out_ref.dtype)
@@ -198,7 +200,7 @@
     n_pair, n_cell = n_slot * n_left, held * n_right
     blocks = n_pair + n_cell + n_left + n_right + n_slot + 10 * held
     outs = pl.pallas_call(
-        functools.partial(terms_kernel, n_lo, keys),
+        functools.partial(terms_kernel, n_lo, direct, keys),
         out_shape=out_shape,
         in_specs=[VMEM] * 5,
         out_specs=[VMEM] * len(out_shape),
@@ -254,9 +256,14 @@
     direct = n_hi - 1
     staged = [k for k in range(n_hi) if k != direct]
     own, other, *far = terms(first, got, left_ops, right_ops, weight, held, n_op, n_lo, staged, direct)
+    def meet(x, even, odd):
+        bits = [even, odd]
+        pairs = [(s * n_op + o, s * n_op + (o ^ bits[s % 2])) for s in range(n_sec) for o in range(n_op)]
+        return lax.ppermute(x, ("sec", "op"), pairs)
+
     total = None
     for i in range(n_lo - 1, -1, -1):
-        part = swap(far[i][0], 0, direct * n_lo + i).astype(jnp.float32)
+        part = meet(far[i][0], direct * n_lo + i, direct * n_lo + (n_lo - 1 - i)).astype(jnp.float32)
         total = part if total is None else total + part
     other = swap(other, 0, 1)
     sums = dict(zip(staged[1:], combine(own, other)))

time: 33.1 us -> 33.1 us (level)
    ppermute x0 -> x2, starting transfers between devices: none -> 4.18 us  [meet(): return lax.ppermute(x, ('sec', 'op'), pairs)]
    ppermute x12 -> x10, starting transfers between devices: 16.6 us -> 12.5 us  [swap(): return lax.ppermute(x, ('sec', 'op'), pairs)]
    ppermute x0 -> x2, waiting for transfers between devices: none -> 2.16 us  [meet(): return lax.ppermute(x, ('sec', 'op'), pairs)]
    ppermute x12 -> x10, waiting for transfers between devices: 9.61 us -> 7.45 us  [swap(): return lax.ppermute(x, ('sec', 'op'), pairs)]
where the time goes in v9:
time: 33.1 us; the launch traced here: 32.8 us
  starting transfers between devices  16.6 us (50%)
  waiting for transfers between devices  9.61 us (29%)
  Pallas kernels  3.64 us (11%)
  local copies, waits for them, and re-layouts  1.5 us (5%)
  other arithmetic  1.37 us (4%)
    ppermute x10, starting transfers between devices, swap(): return lax.ppermute(x, ('sec', 'op'), pairs)  12.5 us
    ppermute x10, waiting for transfers between devices, swap(): return lax.ppermute(x, ('sec', 'op'), pairs)  7.45 us
    ppermute x2, starting transfers between devices, meet(): return lax.ppermute(x, ('sec', 'op'), pairs)  4.18 us
    ppermute x2, waiting for transfers between devices, meet(): return lax.ppermute(x, ('sec', 'op'), pairs)  2.16 us
    pallas_call x1, Pallas kernels, terms(): pl.pallas_call(functools.partial(terms_kernel, n_lo, direct, keys), out_s...  1.97 us
    unnamed x8, local copies, waits for them, and re-layouts  1.5 us
    pallas_call x1, Pallas kernels, prepare(): pl.pallas_call(functools.partial(prepare_kernel, n_left, n_right, held),...  0.85 us
    reshape x1, other arithmetic, prepare(): code.reshape(1, n_term)  0.71 us
  transfers between devices with their start and end apart: 12, of which 7 were waited for; matrix products, arithmetic and copies ran while one was open for 2% of the time, Pallas kernels for 5%

profile of v9, /device:TPU:0, one launch (start us, length us, event | category | flops | bytes accessed | tf_op | source)
XLA Modules:
  0.0 32.8 jit_solution(3773236849808666949)
XLA Ops:
  0.0 5.0 %collective-permute-start = (bf16[2,32,256]{2,1,0:T(8,128)(2,1)}, bf16[2,32,256]{2,1,0:T(8,128)(2,1)S(1)}, u32[]{:S(2)}, u32[]{:S(2)}) collective-permute-start(bf16[2,32,256]{2,1,0:T(8,128)(2,1)} %from_ref.1), channel_id=1, source_target_pairs={{0,6},{1,7},{2,4},{3,5},{4,2},{5,3},{6,0},{7,1},{8,14},{9,15},{10,... | collective-permute-start | bytes 98312 | tf_op jit(solution)/shard_map/ppermute | solution.py:246
  5.1 0.6 %collective-permute-start.1 = (bf16[2,32,256]{2,1,0:T(8,128)(2,1)}, bf16[2,32,256]{2,1,0:T(8,128)(2,1)S(1)}, u32[]{:S(2)}, u32[]{:S(2)}) collective-permute-start(bf16[2,32,256]{2,1,0:T(8,128)(2,1)} %from_ref.1), channel_id=1, source_target_pairs={{0,2},{1,3},{2,0},{3,1},{4,6},{5,7},{6,4},{7,5},{8,10},{9,11},{10,... | collective-permute-start | bytes 98312 | tf_op jit(solution)/shard_map/ppermute | solution.py:246
  5.6 0.8 %copy-done.1 = bf16[2,32,256]{2,1,0:T(8,128)(2,1)S(1)} copy-done((bf16[2,32,256]{2,1,0:T(8,128)(2,1)S(1)}, bf16[2,32,256]{2,1,0:T(8,128)(2,1)}, u32[]{:S(2)}) %copy-start.1) | copy-done | bytes 32792
  6.4 0.7 %collective-permute-done.refs_1_ = bf16[2,32,256]{2,1,0:T(8,128)(2,1)S(1)} collective-permute-done((bf16[2,32,256]{2,1,0:T(8,128)(2,1)}, bf16[2,32,256]{2,1,0:T(8,128)(2,1)S(1)}, u32[]{:S(2)}, u32[]{:S(2)}) %collective-permute-start) | collective-permute-done | bytes 32800 | tf_op jit(solution)/shard_map/ppermute | solution.py:246
  7.2 2.9 %collective-permute-done.2.refs_3_ = bf16[2,32,256]{2,1,0:T(8,128)(2,1)S(1)} collective-permute-done((bf16[2,32,256]{2,1,0:T(8,128)(2,1)}, bf16[2,32,256]{2,1,0:T(8,128)(2,1)S(1)}, u32[]{:S(2)}, u32[]{:S(2)}) %collective-permute-start.2) | collective-permute-done | bytes 32800 | tf_op jit(solution)/shard_map/ppermute | solution.py:246
  10.1 2.5 %collective-permute-start.5 = (bf16[4,2,32,256]{3,2,1,0:T(8,128)(2,1)S(1)}, bf16[4,2,32,256]{3,2,1,0:T(8,128)(2,1)S(1)}, u32[]{:S(2)}, u32[]{:S(2)}) collective-permute-start(bf16[4,2,32,256]{3,2,1,0:T(8,128)(2,1)S(1)} %shard_map.84.refs_0_), channel_id=1, source_target_pairs={{0,17},{1,16},{2,19},{3,18},{4,21},{5,20},{6,23},{7,22},{8,25},{9,... | collective-permute-start | bytes 393224 | tf_op jit(solution)/shard_map/ppermute | solution.py:246
  12.6 0.5 %collective-permute-start.4 = (bf16[4,2,32,256]{3,2,1,0:T(8,128)(2,1)S(1)}, bf16[4,2,32,256]{3,2,1,0:T(8,128)(2,1)S(1)}, u32[]{:S(2)}, u32[]{:S(2)}) collective-permute-start(bf16[4,2,32,256]{3,2,1,0:T(8,128)(2,1)S(1)} %shard_map.84.refs_0_), channel_id=1, source_target_pairs={{0,16},{1,17},{2,18},{3,19},{4,20},{5,21},{6,22},{7,23},{8,24},{9,... | collective-permute-start | bytes 393224 | tf_op jit(solution)/shard_map/ppermute | solution.py:246
  13.1 0.5 %collective-permute-start.3 = (bf16[4,2,32,256]{3,2,1,0:T(8,128)(2,1)S(1)}, bf16[4,2,32,256]{3,2,1,0:T(8,128)(2,1)S(1)}, u32[]{:S(2)}, u32[]{:S(2)}) collective-permute-start(bf16[4,2,32,256]{3,2,1,0:T(8,128)(2,1)S(1)} %shard_map.84.refs_0_), channel_id=1, source_target_pairs={{0,1},{1,0},{2,3},{3,2},{4,5},{5,4},{6,7},{7,6},{8,9},{9,8},{10,11... | collective-permute-start | bytes 393224 | tf_op jit(solution)/shard_map/ppermute | solution.py:246
  13.6 0.7 %add_bitcast_fusion.code_ref = s32[1,64]{1,0:T(1,128)S(1)} fusion(s32[64]{0:T(128)} %param.15, s32[64]{0:T(128)} %param.13, s32[64]{0:T(128)} %param.14, s32[64]{0:T(128)} %param.12), kind=kLoop, calls=%fused_computation.3 | loop fusion | flops 384 | bytes 1280 | tf_op jit(solution)/shard_map/reshape | solution.py:77
  14.4 0.7 %copy-done.3 = s32[4,8,4,1]{1,3,2,0:T(1,128)S(1)} copy-done((s32[4,8,4,1]{1,3,2,0:T(1,128)S(1)}, s32[4,8,4,1]{1,3,2,0:T(1,128)}, u32[]{:S(2)}) %copy-start.3) | copy-done | bytes 536
  15.1 0.9 %shard_map.82 = (bf16[2,2,32,256]{3,2,1,0:T(8,128)(2,1)S(1)}, bf16[128,256]{1,0:T(8,128)(2,1)S(1)}) custom-call(s32[4,4,1,8]{3,2,1,0:T(1,128)S(1)} %bitcast.20, s32[1,64]{1,0:T(1,128)S(1)} %add_bitcast_fusion.code_ref), custom_call_target="tpu_custom_call" | custom-call | flops 1000000000 | bytes 4000000 | tf_op jit(solution)/shard_map/pallas_call | solution.py:67
  15.9 1.5 %collective-permute-done.5.refs_3_ = bf16[4,2,32,256]{3,2,1,0:T(8,128)(2,1)S(1)} collective-permute-done((bf16[4,2,32,256]{3,2,1,0:T(8,128)(2,1)S(1)}, bf16[4,2,32,256]{3,2,1,0:T(8,128)(2,1)S(1)}, u32[]{:S(2)}, u32[]{:S(2)}) %collective-permute-start.5) | collective-permute-done | bytes 131104 | tf_op jit(solution)/shard_map/ppermute | solution.py:246
  17.4 0.8 %collective-permute-done.4.refs_2_ = bf16[4,2,32,256]{3,2,1,0:T(8,128)(2,1)S(1)} collective-permute-done((bf16[4,2,32,256]{3,2,1,0:T(8,128)(2,1)S(1)}, bf16[4,2,32,256]{3,2,1,0:T(8,128)(2,1)S(1)}, u32[]{:S(2)}, u32[]{:S(2)}) %collective-permute-start.4) | collective-permute-done | bytes 131104 | tf_op jit(solution)/shard_map/ppermute | solution.py:246
  18.4 0.7 %shard_map.86.first_ref = bf16[32,128,256]{2,1,0:T(8,128)(2,1)S(1)} custom-call(bf16[8,256,256]{2,1,0:T(8,128)(2,1)S(1)} %copy-done, bf16[2,256,256]{2,1,0:T(8,128)(2,1)S(1)} %bitcast.16), custom_call_target="tpu_custom_call" | custom-call | flops 536870912 | bytes 1000000 | tf_op jit(solution)/shard_map/pallas_call | solution.py:141
  19.1 0.8 %collective-permute-done.6.table_ref = bf16[2,256,256]{2,1,0:T(8,128)(2,1)S(1)} collective-permute-done((bf16[2,256,256]{2,1,0:T(8,128)(2,1)S(1)}, bf16[2,256,256]{2,1,0:T(8,128)(2,1)S(1)}, u32[]{:S(2)}, u32[]{:S(2)}) %collective-permute-start.6) | collective-permute-done | bytes 262176 | tf_op jit(solution)/shard_map/ppermute | solution.py:246
  19.9 2.0 %shard_map.87 = (f32[3,2,32,256]{3,2,1,0:T(8,128)S(1)}, bf16[3,2,32,256]{3,2,1,0:T(8,128)(2,1)S(1)}, bf16[1,2,32,256]{3,2,1,0:T(8,128)(2,1)S(1)}, bf16[1,2,32,256]{3,2,1,0:T(8,128)(2,1)S(1)}) custom-call(bf16[8,256,256]{2,1,0:T(8,128)(2,1)S(1)} %copy-done, bf16[8,256,256]{2,1,0:T(8,128)(2,1)S(1)} %copy-done.2, ...), custom_call_target="tpu_custom_call" | custom-call | flops 3000000000 | bytes 4000000 | tf_op jit(solution)/shard_map/pallas_call | solution.py:202
  21.9 1.2 %collective-permute-start.9 = (bf16[3,2,32,256]{3,2,1,0:T(8,128)(2,1)S(1)}, bf16[3,2,32,256]{3,2,1,0:T(8,128)(2,1)S(1)}, u32[]{:S(2)}, u32[]{:S(2)}) collective-permute-start(bf16[3,2,32,256]{3,2,1,0:T(8,128)(2,1)S(1)} %get-tuple-element.22), channel_id=1, source_target_pairs={{0,1},{1,0},{2,3},{3,2},{4,5},{5,4},{6,7},{7,6},{8,9},{9,8},{10,11... | collective-permute-start | bytes 294920 | tf_op jit(solution)/shard_map/ppermute | solution.py:246
  23.0 1.8 %collective-permute-start.8 = (bf16[2,32,256]{2,1,0:T(8,128)(2,1)S(1)}, bf16[2,32,256]{2,1,0:T(8,128)(2,1)S(1)}, u32[]{:S(2)}, u32[]{:S(2)}) collective-permute-start(bf16[2,32,256]{2,1,0:T(8,128)(2,1)S(1)} %bitcast.19), channel_id=1, source_target_pairs={{0,6},{1,7},{2,4},{3,5},{4,2},{5,3},{6,0},{7,1},{8,15},{9,14},{10,... | collective-permute-start | bytes 98312 | tf_op jit(solution)/shard_map/ppermute | solution.py:262
  24.8 2.4 %collective-permute-start.7 = (bf16[2,32,256]{2,1,0:T(8,128)(2,1)S(1)}, bf16[2,32,256]{2,1,0:T(8,128)(2,1)S(1)}, u32[]{:S(2)}, u32[]{:S(2)}) collective-permute-start(bf16[2,32,256]{2,1,0:T(8,128)(2,1)S(1)} %bitcast.18), channel_id=1, source_target_pairs={{0,7},{1,6},{2,5},{3,4},{4,3},{5,2},{6,1},{7,0},{8,14},{9,15},{10,... | collective-permute-start | bytes 98312 | tf_op jit(solution)/shard_map/ppermute | solution.py:262
  27.2 0.1 collective-permute-start.10
  27.3 2.0 %collective-permute-start.11 = (bf16[2,32,256]{2,1,0:T(8,128)(2,1)S(1)}, bf16[2,32,256]{2,1,0:T(8,128)(2,1)S(1)}, u32[]{:S(2)}, u32[]{:S(2)}) collective-permute-start(bf16[2,32,256]{2,1,0:T(8,128)(2,1)S(1)} %get-tuple-element.24), channel_id=1, source_target_pairs={{0,4},{1,5},{2,6},{3,7},{4,0},{5,1},{6,2},{7,3},{8,12},{9,13},{10,... | collective-permute-start | bytes 98312 | tf_op jit(solution)/shard_map/ppermute | solution.py:246
  29.3 2.2 %collective-permute-done.7 = bf16[2,32,256]{2,1,0:T(8,128)(2,1)S(1)} collective-permute-done((bf16[2,32,256]{2,1,0:T(8,128)(2,1)S(1)}, bf16[2,32,256]{2,1,0:T(8,128)(2,1)S(1)}, u32[]{:S(2)}, u32[]{:S(2)}) %collective-permute-start.7) | collective-permute-done | bytes 32800 | tf_op jit(solution)/shard_map/ppermute | solution.py:262
  31.5 0.7 %collective-permute-done.11 = bf16[2,32,256]{2,1,0:T(8,128)(2,1)S(1)} collective-permute-done((bf16[2,32,256]{2,1,0:T(8,128)(2,1)S(1)}, bf16[2,32,256]{2,1,0:T(8,128)(2,1)S(1)}, u32[]{:S(2)}, u32[]{:S(2)}) %collective-permute-start.11) | collective-permute-done | bytes 32800 | tf_op jit(solution)/shard_map/ppermute | solution.py:246
  32.2 0.7 %convert_add_fusion = f32[2,32,256]{2,1,0:T(8,128)} fusion(f32[3,2,32,256]{3,2,1,0:T(8,128)S(1)} %get-tuple-element.21.own_ref, bf16[2,32,256]{2,1,0:T(8,128)(2,1)S(1)} %collective-permute-done.11, bf16[2,32,256]{2,1,0:T(8,128)(2,1)S(1)} %collective-permute-done.10, bf16[2,32,256]{2,1,0:T(8,128)(2,1)S(1)} %collective-permute-done.8, ...), kind=kLoop, calls=%fused_computation | loop fusion | flops 163840 | bytes 294912 | tf_op jit(solution)/shard_map/add | solution.py:272
  (17 shorter events, 0.2 us)
Async XLA Ops:
  0.0 7.2 %collective-permute-start = (bf16[2,32,256]{2,1,0:T(8,128)(2,1)}, bf16[2,32,256]{2,1,0:T(8,128)(2,1)S(1)}, u32[]{:S(2)}, u32[]{:S(2)}) collective-permute-start(bf16[2,32,256]{2,1,0:T(8,128)(2,1)} %from_ref.1), channel_id=1, source_target_pairs={{0,6},{1,7},{2,4},{3,5},{4,2},{5,3},{6,0},{7,1},{8,14},{9,15},{10,... | collective-permute-start | bytes 98312 | tf_op jit(solution)/shard_map/ppermute | solution.py:246
  5.0 5.0 %collective-permute-start.2 = (bf16[2,32,256]{2,1,0:T(8,128)(2,1)}, bf16[2,32,256]{2,1,0:T(8,128)(2,1)S(1)}, u32[]{:S(2)}, u32[]{:S(2)}) collective-permute-start(bf16[2,32,256]{2,1,0:T(8,128)(2,1)} %from_ref.1), channel_id=1, source_target_pairs={{0,4},{1,5},{2,6},{3,7},{4,0},{5,1},{6,2},{7,3},{8,12},{9,13},{10,... | collective-permute-start | bytes 98312 | tf_op jit(solution)/shard_map/ppermute | solution.py:246
  5.1 5.0 %collective-permute-start.1 = (bf16[2,32,256]{2,1,0:T(8,128)(2,1)}, bf16[2,32,256]{2,1,0:T(8,128)(2,1)S(1)}, u32[]{:S(2)}, u32[]{:S(2)}) collective-permute-start(bf16[2,32,256]{2,1,0:T(8,128)(2,1)} %from_ref.1), channel_id=1, source_target_pairs={{0,2},{1,3},{2,0},{3,1},{4,6},{5,7},{6,4},{7,5},{8,10},{9,11},{10,... | collective-permute-start | bytes 98312 | tf_op jit(solution)/shard_map/ppermute | solution.py:246
  5.6 0.8 %copy-start.1 = (bf16[2,32,256]{2,1,0:T(8,128)(2,1)S(1)}, bf16[2,32,256]{2,1,0:T(8,128)(2,1)}, u32[]{:S(2)}) copy-start(bf16[2,32,256]{2,1,0:T(8,128)(2,1)} %from_ref.1) | copy-start | bytes 98308
  10.1 7.3 %collective-permute-start.5 = (bf16[4,2,32,256]{3,2,1,0:T(8,128)(2,1)S(1)}, bf16[4,2,32,256]{3,2,1,0:T(8,128)(2,1)S(1)}, u32[]{:S(2)}, u32[]{:S(2)}) collective-permute-start(bf16[4,2,32,256]{3,2,1,0:T(8,128)(2,1)S(1)} %shard_map.84.refs_0_), channel_id=1, source_target_pairs={{0,17},{1,16},{2,19},{3,18},{4,21},{5,20},{6,23},{7,22},{8,25},{9,... | collective-permute-start | bytes 393224 | tf_op jit(solution)/shard_map/ppermute | solution.py:246
  12.6 5.6 %collective-permute-start.4 = (bf16[4,2,32,256]{3,2,1,0:T(8,128)(2,1)S(1)}, bf16[4,2,32,256]{3,2,1,0:T(8,128)(2,1)S(1)}, u32[]{:S(2)}, u32[]{:S(2)}) collective-permute-start(bf16[4,2,32,256]{3,2,1,0:T(8,128)(2,1)S(1)} %shard_map.84.refs_0_), channel_id=1, source_target_pairs={{0,16},{1,17},{2,18},{3,19},{4,20},{5,21},{6,22},{7,23},{8,24},{9,... | collective-permute-start | bytes 393224 | tf_op jit(solution)/shard_map/ppermute | solution.py:246
  13.1 5.1 %collective-permute-start.3 = (bf16[4,2,32,256]{3,2,1,0:T(8,128)(2,1)S(1)}, bf16[4,2,32,256]{3,2,1,0:T(8,128)(2,1)S(1)}, u32[]{:S(2)}, u32[]{:S(2)}) collective-permute-start(bf16[4,2,32,256]{3,2,1,0:T(8,128)(2,1)S(1)} %shard_map.84.refs_0_), channel_id=1, source_target_pairs={{0,1},{1,0},{2,3},{3,2},{4,5},{5,4},{6,7},{7,6},{8,9},{9,8},{10,11... | collective-permute-start | bytes 393224 | tf_op jit(solution)/shard_map/ppermute | solution.py:246
  14.4 0.7 %copy-start.3 = (s32[4,8,4,1]{1,3,2,0:T(1,128)S(1)}, s32[4,8,4,1]{1,3,2,0:T(1,128)}, u32[]{:S(2)}) copy-start(s32[4,8,4,1]{1,3,2,0:T(1,128)} %param.11) | copy-start | bytes 1540
  15.1 3.3 %copy-start = (bf16[8,256,256]{2,1,0:T(8,128)(2,1)S(1)}, bf16[8,256,256]{2,1,0:T(8,128)(2,1)}, u32[]{:S(2)}) copy-start(bf16[8,256,256]{2,1,0:T(8,128)(2,1)} %left_ref.3) | copy-start | bytes 3145732
  15.9 4.0 %copy-start.2 = (bf16[8,256,256]{2,1,0:T(8,128)(2,1)S(1)}, bf16[8,256,256]{2,1,0:T(8,128)(2,1)}, u32[]{:S(2)}) copy-start(bf16[8,256,256]{2,1,0:T(8,128)(2,1)} %right_ref.1) | copy-start | bytes 3145732
  18.3 1.6 %collective-permute-start.6 = (bf16[2,256,256]{2,1,0:T(8,128)(2,1)S(1)}, bf16[2,256,256]{2,1,0:T(8,128)(2,1)S(1)}, u32[]{:S(2)}, u32[]{:S(2)}) collective-permute-start(bf16[2,256,256]{2,1,0:T(8,128)(2,1)S(1)} %bitcast.17), channel_id=1, source_target_pairs={{0,8},{1,9},{2,10},{3,11},{4,12},{5,13},{6,14},{7,15},{8,0},{9,1},... | collective-permute-start | bytes 786440 | tf_op jit(solution)/shard_map/ppermute | solution.py:246
  21.9 5.4 %collective-permute-start.9 = (bf16[3,2,32,256]{3,2,1,0:T(8,128)(2,1)S(1)}, bf16[3,2,32,256]{3,2,1,0:T(8,128)(2,1)S(1)}, u32[]{:S(2)}, u32[]{:S(2)}) collective-permute-start(bf16[3,2,32,256]{3,2,1,0:T(8,128)(2,1)S(1)} %get-tuple-element.22), channel_id=1, source_target_pairs={{0,1},{1,0},{2,3},{3,2},{4,5},{5,4},{6,7},{7,6},{8,9},{9,8},{10,11... | collective-permute-start | bytes 294920 | tf_op jit(solution)/shard_map/ppermute | solution.py:246
  23.0 6.3 %collective-permute-start.8 = (bf16[2,32,256]{2,1,0:T(8,128)(2,1)S(1)}, bf16[2,32,256]{2,1,0:T(8,128)(2,1)S(1)}, u32[]{:S(2)}, u32[]{:S(2)}) collective-permute-start(bf16[2,32,256]{2,1,0:T(8,128)(2,1)S(1)} %bitcast.19), channel_id=1, source_target_pairs={{0,6},{1,7},{2,4},{3,5},{4,2},{5,3},{6,0},{7,1},{8,15},{9,14},{10,... | collective-permute-start | bytes 98312 | tf_op jit(solution)/shard_map/ppermute | solution.py:262
  24.8 6.6 %collective-permute-start.7 = (bf16[2,32,256]{2,1,0:T(8,128)(2,1)S(1)}, bf16[2,32,256]{2,1,0:T(8,128)(2,1)S(1)}, u32[]{:S(2)}, u32[]{:S(2)}) collective-permute-start(bf16[2,32,256]{2,1,0:T(8,128)(2,1)S(1)} %bitcast.18), channel_id=1, source_target_pairs={{0,7},{1,6},{2,5},{3,4},{4,3},{5,2},{6,1},{7,0},{8,14},{9,15},{10,... | collective-permute-start | bytes 98312 | tf_op jit(solution)/shard_map/ppermute | solution.py:262
  27.2 4.2 %collective-permute-start.10 = (bf16[2,32,256]{2,1,0:T(8,128)(2,1)S(1)}, bf16[2,32,256]{2,1,0:T(8,128)(2,1)S(1)}, u32[]{:S(2)}, u32[]{:S(2)}) collective-permute-start(bf16[2,32,256]{2,1,0:T(8,128)(2,1)S(1)} %get-tuple-element.23), channel_id=1, source_target_pairs={{0,2},{1,3},{2,0},{3,1},{4,6},{5,7},{6,4},{7,5},{8,10},{9,11},{10,... | collective-permute-start | bytes 98312 | tf_op jit(solution)/shard_map/ppermute | solution.py:246
  27.3 4.9 %collective-permute-start.11 = (bf16[2,32,256]{2,1,0:T(8,128)(2,1)S(1)}, bf16[2,32,256]{2,1,0:T(8,128)(2,1)S(1)}, u32[]{:S(2)}, u32[]{:S(2)}) collective-permute-start(bf16[2,32,256]{2,1,0:T(8,128)(2,1)S(1)} %get-tuple-element.24), channel_id=1, source_target_pairs={{0,4},{1,5},{2,6},{3,7},{4,0},{5,1},{6,2},{7,3},{8,12},{9,13},{10,... | collective-permute-start | bytes 98312 | tf_op jit(solution)/shard_map/ppermute | solution.py:246
